TPU v7x, 32 devices: a whole 2x2x4 slice. The times are simulated.
32 devices in a mesh: groups: 2 (over y), replica: 4 (over z), tensor: 4 (over x, core).
Axes of the slice: x: 2, y: 2, z: 4, core: 2. Of those that a mesh axis runs over, the one named last changes fastest.
Arguments:
- queries: bfloat16 [144, 8192], P(('groups', 'replica'), 'tensor'), parts along dimension 0, may hold values from -64 to 64
- past_cache: bfloat16 [2, 144, 128, 1024], P(None, ('groups', 'replica'), None, 'tensor'), parts along dimension 1, may hold values from -6 to 6
- lengths: int32 [144], P(('groups', 'replica')), parts along dimension 0, may hold values from 2 to 128, as said below
- live_counts: int32 [8], P(('groups', 'replica')), parts along dimension 0, may hold values from 1 to 16, as said below
- adapter_index: int32 [144], P(('groups', 'replica')), parts along dimension 0, may hold values from 0 to 15, as said below
- adapter_down: bfloat16 [16, 16, 8192], P('replica', None, 'tensor'), may hold values from -0.0625 to 0.0625
- adapter_up: bfloat16 [16, 16, 8192], P('replica', None, 'tensor'), may hold values from -6 to 6
Outputs:
- attention: bfloat16 [144, 8192], P(('groups', 'replica'), 'tensor'), parts along dimension 0
- adapted: bfloat16 [144, 8192], P(('groups', 'replica'), 'tensor'), parts along dimension 0
There are 2 independent parts, one for each index of `groups`. A program takes and returns all parts, laid end to end along the dimension named above; an argument that names none is the same for every part. Nothing has to cross between parts.
Inputs may be any that keep to these rules, and one draw needn't show every extreme that they name: `adapter_index`: over the first 16 slots of all replicas, exactly 4 distinct adapters appear, homed on 4 distinct replicas. Each of the last 2 slots of a replica names an adapter outside that set; the homes (adapter a lives on replica a // 4) of one replica's last 2 slots are distinct, and some replica is the home of one such slot of every replica. `lengths`: some request has exactly 128. `live_counts`: some replica has exactly 16.
All inputs are finite; a program needn't handle non-finite values.
Results may differ from a plain program's by a relative error of at most 0.008.
Values may be sent and summed in bfloat16 or wider, within the bound.
No kernel may reach another device: no remote copies, remote signals or barrier semaphores. Data moves between devices by JAX's collectives and lax.ppermute only.
A program may use at most 64 MiB of HBM per device.

v0:
```python
import math

import jax
import jax.numpy as jnp
from jax import lax
from jax.sharding import PartitionSpec as P

HEAD_DIM = 128
STAY = 16


SCALING = 2.0


def broadcast(block, axis, owner):
    block = jnp.where(lax.axis_index(axis) == owner, block, jnp.zeros_like(block))
    return lax.psum(block, axis)


def attend(queries, keys, values, visible):
    count = queries.shape[0]
    key_width = keys.shape[-1]
    key_heads = key_width // HEAD_DIM
    group_size = queries.shape[1] // key_width
    context = keys.shape[1]
    query_rows = queries.reshape(count, key_heads, group_size, HEAD_DIM)
    key_rows = keys.reshape(count, context, key_heads, HEAD_DIM)
    value_rows = values.reshape(count, context, key_heads, HEAD_DIM)
    scores = jnp.einsum(
        "nhgd,nlhd->nhgl", query_rows, key_rows, preferred_element_type=jnp.float32
    ) / math.sqrt(HEAD_DIM)
    scores = jnp.where(visible[:, None, None, :], scores, -jnp.inf)
    peak = jnp.max(scores, axis=-1, keepdims=True)
    raised = jnp.exp(scores - peak)
    weights = (raised / jnp.sum(raised, axis=-1, keepdims=True)).astype(jnp.bfloat16)
    mixed = jnp.einsum("nhgl,nlhd->nhgd", weights, value_rows, preferred_element_type=jnp.float32)
    return mixed.reshape(count, key_heads * group_size * HEAD_DIM)


def widen_rows(rank_rows, up_rows):
    widened = jnp.einsum("nr,nrc->nc", rank_rows, up_rows.astype(jnp.float32))
    return (SCALING * widened).astype(jnp.bfloat16)


def on_device(queries, past_cache, lengths, live_counts, adapter_index, adapter_down, adapter_up):
    slots = queries.shape[0]
    moving = slots - STAY
    replicas = lax.axis_size("replica")
    hot_total = min(8, replicas)
    local_count = adapter_down.shape[0]
    total_adapters = local_count * replicas
    context = past_cache.shape[2]
    position = jnp.arange(context, dtype=jnp.int32)
    slot_index = jnp.arange(slots, dtype=jnp.int32)
    alive = (slot_index >= STAY) | (slot_index < live_counts[0])
    visible = position[None, :] < lengths[:, None]
    stay_index = adapter_index[:STAY]
    catalog = jnp.arange(total_adapters, dtype=jnp.int32)
    usage = jnp.sum((stay_index[:, None] == catalog[None, :]).astype(jnp.int32), axis=0)
    usage = lax.psum(usage, "replica")
    ranking = jnp.where(usage > 0, total_adapters - catalog, 0)
    hot_index = total_adapters - lax.top_k(ranking, hot_total)[0]
    down_list = []
    up_list = []
    for hot_slot in range(hot_total):
        holder = hot_index[hot_slot] // local_count
        within = hot_index[hot_slot] % local_count
        local_pair = (
            lax.dynamic_index_in_dim(adapter_down, within, 0, False),
            lax.dynamic_index_in_dim(adapter_up, within, 0, False),
        )
        fetched = (
            broadcast(local_pair[0], "replica", holder),
            broadcast(local_pair[1], "replica", holder),
        )
        down_list.append(fetched[0])
        up_list.append(fetched[1])
    hot_down = jnp.stack(down_list)
    hot_up = jnp.stack(up_list)
    hot_pick = (stay_index[:, None] == hot_index[None, :]).astype(jnp.bfloat16)
    stay_down = jnp.einsum("nh,hrc->nrc", hot_pick, hot_down)
    stay_up = jnp.einsum("nh,hrc->nrc", hot_pick, hot_up)
    stay_attention = attend(
        queries[:STAY], past_cache[0, :STAY], past_cache[1, :STAY], visible[:STAY]
    )
    stay_attention = jnp.where(alive[:STAY, None], stay_attention, 0.0).astype(jnp.bfloat16)
    stay_partial = jnp.einsum(
        "nc,nrc->nr", stay_attention, stay_down, preferred_element_type=jnp.float32
    )
    moved_index = adapter_index[STAY:]
    homes = moved_index // local_count
    replica_ids = jnp.arange(replicas, dtype=jnp.int32)
    matched = homes[None, :] == replica_ids[:, None]
    occupied = jnp.any(matched, axis=1)
    source_slot = jnp.sum(
        jnp.where(matched, jnp.arange(moving, dtype=jnp.int32)[None, :], 0), axis=1
    )
    wanted = jnp.where(occupied, jnp.take(moved_index, source_slot) % local_count, -1)
    local_catalog = jnp.arange(local_count, dtype=jnp.int32)
    chooser = (
        lax.all_to_all(wanted[:, None], "replica", split_axis=0, concat_axis=0, tiled=True)[
            :, :, None
        ]
        == local_catalog[None, None, :]
    ).astype(jnp.bfloat16)
    send_down = jnp.einsum("sna,arc->snrc", chooser, adapter_down)
    send_up = jnp.einsum("sna,arc->snrc", chooser, adapter_up)
    got_down = lax.all_to_all(send_down, "replica", split_axis=0, concat_axis=0, tiled=True)
    got_up = lax.all_to_all(send_up, "replica", split_axis=0, concat_axis=0, tiled=True)
    moved_down = jnp.take(got_down[:, 0], homes, axis=0)
    moved_up = jnp.take(got_up[:, 0], homes, axis=0)
    moved_attention = attend(
        queries[STAY:], past_cache[0, STAY:], past_cache[1, STAY:], visible[STAY:]
    ).astype(jnp.bfloat16)
    moved_partial = jnp.einsum(
        "nc,nrc->nr", moved_attention, moved_down, preferred_element_type=jnp.float32
    )
    rank_rows = lax.psum(jnp.concatenate([stay_partial, moved_partial], axis=0), "tensor")
    stay_adapted = widen_rows(rank_rows[:STAY], stay_up)
    moved_adapted = widen_rows(rank_rows[STAY:], moved_up)
    attention = jnp.concatenate([stay_attention, moved_attention], axis=0)
    adapted = jnp.concatenate([stay_adapted, moved_adapted], axis=0)
    return (attention, adapted)


def solution(mesh):
    in_specs = (
        P(("groups", "replica"), "tensor"),
        P(None, ("groups", "replica"), None, "tensor"),
        P(("groups", "replica")),
        P(("groups", "replica")),
        P(("groups", "replica")),
        P("replica", None, "tensor"),
        P("replica", None, "tensor"),
    )
    out_specs = (P(("groups", "replica"), "tensor"), P(("groups", "replica"), "tensor"))
    return jax.shard_map(
        on_device, mesh=mesh, in_specs=in_specs, out_specs=out_specs, check_vma=False
    )
```

profile of v0, /device:TPU:0, one launch (start us, length us, event | category | flops | bytes accessed | tf_op | source)
XLA Modules:
  0.0 127.5 jit_solution(2885234638877340328)
XLA Ops:
  7.2 0.7 compare_and_fusion
  7.9 0.7 slice.70
  8.8 0.6 gather_fusion
  9.5 0.7 copy.78
  10.1 6.3 %all-to-all-start = ((s32[4,1,1]{2,1,0:T(1,128)}), s32[4,1,1]{2,1,0:T(1,128)S(1)}, u32[]{:S(2)}, u32[]{:S(2)}) async-start(s32[4,1,1]{2,1,0:T(1,128)} %copy.78), calls=%async_computation | async-start | bytes 4096 | tf_op jit(solution)/shard_map/all_to_all | solution.py:101
  16.5 0.7 convert_reduce_fusion
  17.2 8.8 %psum.70 = s32[16]{0:T(128)S(1)} all-reduce(s32[16]{0:T(128)S(1)} %convert_reduce_fusion), channel_id=1, replica_groups=mesh['groups'=2,'replica'=4,'tensor'=4] {'replica'}, use_global_device_ids=true, to_apply=%region_5.6 | all-reduce | flops 16 | bytes 128 | tf_op jit(solution)/shard_map/psum | solution.py:60
  26.0 1.2 top_k.9
  27.3 0.7 fusion.67
  38.1 1.2 copy.73
  39.4 1.2 copy.81
  40.6 1.4 %broadcast_select_fusion.7 = (bf16[1,16,2048]{2,0,1:T(2,128)(2,1)}, bf16[1,16,2048]{2,0,1:T(2,128)(2,1)}, bf16[1,16,2048]{2,0,1:T(2,128)(2,1)}, bf16[1,16,2048]{2,0,1:T(2,128)(2,1)}) fusion(pred[]{:T(512)S(6)} %eq.87, bf16[4,16,2048]{2,0,1:T(4,128)(2,1)S(1)} %copy.73, s32[]{:T(128)S(6)} %select_n.215, s32[]{:T(128)S(6)} %select_n.233, pred[]{:T(512)S(6)} %eq.90, ...), kind=kLoop, calls=%fused_computation.43 | loop fusion | flops 131072 | bytes 524308 | tf_op jit(solution)/shard_map/jit(_where)/select_n | solution.py:16
  42.0 1.5 %broadcast_select_fusion.6 = (bf16[1,16,2048]{2,0,1:T(2,128)(2,1)}, bf16[1,16,2048]{2,0,1:T(2,128)(2,1)}, bf16[1,16,2048]{2,0,1:T(2,128)(2,1)}, bf16[1,16,2048]{2,0,1:T(2,128)(2,1)}) fusion(pred[]{:T(512)S(6)} %eq.87, bf16[4,16,2048]{2,0,1:T(4,128)(2,1)S(1)} %copy.81, s32[]{:T(128)S(6)} %select_n.215, s32[]{:T(128)S(6)} %select_n.233, pred[]{:T(512)S(6)} %eq.90, ...), kind=kLoop, calls=%fused_computation.42 | loop fusion | flops 131072 | bytes 524308 | tf_op jit(solution)/shard_map/jit(_where)/select_n | solution.py:16
  43.5 1.0 fusion.66
  44.5 1.7 %fusion.65 = (bf16[1,16,128,256]{3,2,1,0:T(8,128)(2,1)S(1)}, bf16[1,16,128,256]{3,2,1,0:T(8,128)(2,1)S(1)}) fusion(bf16[2,18,128,256]{3,2,1,0:T(8,128)(2,1)} %param.10), kind=kLoop, calls=%fused_computation.114 | loop fusion | bytes 4194304 | tf_op jit(solution)/shard_map/slice | solution.py:84
  47.2 1.3 %copy.103 = bf16[1,16,128,256]{2,3,1,0:T(8,128)(2,1)} copy(bf16[1,16,128,256]{3,2,1,0:T(8,128)(2,1)S(1)} %get-tuple-element.17) | data formatting | bytes 2097152
  48.5 0.7 copy.102
  50.5 1.9 %fusion.37 = bf16[16,2,8,128]{3,2,1,0:T(8,128)(2,1)S(1)} fusion(bf16[16,128,2,128]{1,3,2,0:T(8,128)(2,1)} %bitcast.99, f32[16,2,8]{2,1,0:T(2,128)S(1)} %fusion.69, f32[16,2,8,128]{3,2,1,0:T(8,128)S(1)} %fusion.4), kind=kOutput, calls=%fused_computation.58 | convolution fusion | flops 8487295 | bytes 1246208 | tf_op jit(solution)/shard_map/nhgl,nlhd->nhgd/dot_general | solution.py:36
  53.0 0.8 copy.80
  53.9 3.4 %all-to-all-start.1 = ((bf16[4,1,16,2048]{3,2,1,0:T(8,128)(2,1)}), bf16[4,1,16,2048]{3,2,1,0:T(8,128)(2,1)S(1)}, u32[]{:S(2)}, u32[]{:S(2)}) async-start(bf16[4,1,16,2048]{3,2,1,0:T(8,128)(2,1)} %copy.80), calls=%async_computation.1 | async-start | bytes 524288 | tf_op jit(solution)/shard_map/all_to_all | solution.py:108
  57.7 0.8 copy.86
  58.5 14.9 %all-to-all-done.1 = bf16[4,1,16,2048]{3,2,1,0:T(8,128)(2,1)S(1)} async-done(((bf16[4,1,16,2048]{3,2,1,0:T(8,128)(2,1)}), bf16[4,1,16,2048]{3,2,1,0:T(8,128)(2,1)S(1)}, u32[]{:S(2)}, u32[]{:S(2)}) %all-to-all-start.1) | async-done | bytes 262176 | tf_op jit(solution)/shard_map/all_to_all | solution.py:108
  73.4 3.4 %all-to-all-start.2 = ((bf16[4,1,16,2048]{3,2,1,0:T(8,128)(2,1)}), bf16[4,1,16,2048]{3,2,1,0:T(8,128)(2,1)S(1)}, u32[]{:S(2)}, u32[]{:S(2)}) async-start(bf16[4,1,16,2048]{3,2,1,0:T(8,128)(2,1)} %copy.86), calls=%async_computation.2 | async-start | bytes 524288 | tf_op jit(solution)/shard_map/all_to_all | solution.py:109
  76.9 0.6 gather_fusion.1
  77.5 6.2 %all-to-all-done.2 = bf16[4,1,16,2048]{3,2,1,0:T(8,128)(2,1)S(1)} async-done(((bf16[4,1,16,2048]{3,2,1,0:T(8,128)(2,1)}), bf16[4,1,16,2048]{3,2,1,0:T(8,128)(2,1)S(1)}, u32[]{:S(2)}, u32[]{:S(2)}) %all-to-all-start.2) | async-done | bytes 262176 | tf_op jit(solution)/shard_map/all_to_all | solution.py:109
  84.4 19.1 %all-reduce.3.cloned.1.call-done = (bf16[1,16,2048]{2,0,1:T(2,128)(2,1)}, bf16[1,16,2048]{2,0,1:T(2,128)(2,1)}, bf16[1,16,2048]{2,0,1:T(2,128)(2,1)}, bf16[1,16,...) async-done(((bf16[1,16,2048]{2,0,1:T(2,128)(2,1)}, ...) | async-done | bytes 524304 | tf_op jit(solution)/shard_map/psum | solution.py:17
  103.6 2.1 %fusion.12 = bf16[16,16,2048]{2,0,1:T(8,128)(2,1)S(1)} fusion(bf16[1,16,2048]{2,0,1:T(2,128)(2,1)} %get-tuple-element.6, bf16[1,16,2048]{2,0,1:T(2,128)(2,1)} %get-tuple-element.7, bf16[1,16,2048]{2,0,1:T(2,128)(2,1)} %get-tuple-element.8, bf16[1,16,2048]{2,0,1:T(2,128)(2,1)} %get-tuple-element.9, s32[16]{0:T(128)S(1)} %bitcast.116, ...), kind=kOutput, calls=%fused_computation.20 | convolution fusion | flops 5242944 | bytes 1310800 | tf_op jit(solution)/shard_map/nh,hrc->nrc/dot_general | solution.py:81
  105.7 0.7 fusion.10
  106.4 11.1 %psum.75 = f32[18,16]{1,0:T(8,128)S(1)} all-reduce(f32[18,16]{1,0:T(8,128)S(1)} %pad_maximum_fusion.2), channel_id=1, replica_groups=mesh['groups'=2,'replica'=4,'tensor'=4] {'tensor'}, use_global_device_ids=true, to_apply=%region_13.15 | all-reduce | flops 288 | bytes 2304 | tf_op jit(solution)/shard_map/psum | solution.py:118
  117.8 0.9 fusion.20
  118.7 1.2 fusion.8
  120.0 0.7 pad_maximum_fusion
  (56 shorter events, 3.9 us)
Async XLA Ops:
  10.1 42.4 %all-to-all-start = ((s32[4,1,1]{2,1,0:T(1,128)}), s32[4,1,1]{2,1,0:T(1,128)S(1)}, u32[]{:S(2)}, u32[]{:S(2)}) async-start(s32[4,1,1]{2,1,0:T(1,128)} %copy.78), calls=%async_computation | async-start | bytes 4096 | tf_op jit(solution)/shard_map/all_to_all | solution.py:101
  16.5 87.1 %all-reduce.3.cloned.1.call-start = ((), (), s32[]{:S(2)}) async-start(), calls=%async_computation.3 | async-start | bytes 2097152 | tf_op jit(solution)/shard_map/psum | solution.py:17
  43.5 2.7 %copy-start = (bf16[18,2048]{1,0:T(8,128)(2,1)S(1)}, bf16[18,2048]{1,0:T(8,128)(2,1)}, u32[]{:S(2)}) copy-start(bf16[18,2048]{1,0:T(8,128)(2,1)} %param.9) | copy-start | bytes 221188
  43.5 2.8 %copy-start.1 = (s32[18]{0:T(128)S(1)}, s32[18]{0:T(128)}, u32[]{:S(2)}) copy-start(s32[18]{0:T(128)} %param.11) | copy-start | bytes 220
  52.4 51.2 %copy-start.6 = (s32[18]{0:T(128)S(1)}, s32[18]{0:T(128)}, u32[]{:S(2)}) copy-start(s32[18]{0:T(128)} %param.13) | copy-start | bytes 220
  53.9 19.6 %all-to-all-start.1 = ((bf16[4,1,16,2048]{3,2,1,0:T(8,128)(2,1)}), bf16[4,1,16,2048]{3,2,1,0:T(8,128)(2,1)S(1)}, u32[]{:S(2)}, u32[]{:S(2)}) async-start(bf16[4,1,16,2048]{3,2,1,0:T(8,128)(2,1)} %copy.80), calls=%async_computation.1 | async-start | bytes 524288 | tf_op jit(solution)/shard_map/all_to_all | solution.py:108
  73.4 10.2 %all-to-all-start.2 = ((bf16[4,1,16,2048]{3,2,1,0:T(8,128)(2,1)}), bf16[4,1,16,2048]{3,2,1,0:T(8,128)(2,1)S(1)}, u32[]{:S(2)}, u32[]{:S(2)}) async-start(bf16[4,1,16,2048]{3,2,1,0:T(8,128)(2,1)} %copy.86), calls=%async_computation.2 | async-start | bytes 524288 | tf_op jit(solution)/shard_map/all_to_all | solution.py:109
  103.6 14.2 %copy-start.2 = (bf16[1,16,2048]{2,0,1:T(2,128)(2,1)S(1)}, bf16[1,16,2048]{2,0,1:T(2,128)(2,1)}, u32[]{:S(2)}) copy-start(bf16[1,16,2048]{2,0,1:T(2,128)(2,1)} %get-tuple-element.10) | copy-start | bytes 196612
  103.6 14.2 %copy-start.3 = (bf16[1,16,2048]{2,0,1:T(2,128)(2,1)S(1)}, bf16[1,16,2048]{2,0,1:T(2,128)(2,1)}, u32[]{:S(2)}) copy-start(bf16[1,16,2048]{2,0,1:T(2,128)(2,1)} %get-tuple-element.11) | copy-start | bytes 196612
  103.6 14.2 %copy-start.4 = (bf16[1,16,2048]{2,0,1:T(2,128)(2,1)S(1)}, bf16[1,16,2048]{2,0,1:T(2,128)(2,1)}, u32[]{:S(2)}) copy-start(bf16[1,16,2048]{2,0,1:T(2,128)(2,1)} %get-tuple-element.12) | copy-start | bytes 196612
  103.6 14.2 %copy-start.5 = (bf16[1,16,2048]{2,0,1:T(2,128)(2,1)S(1)}, bf16[1,16,2048]{2,0,1:T(2,128)(2,1)}, u32[]{:S(2)}) copy-start(bf16[1,16,2048]{2,0,1:T(2,128)(2,1)} %get-tuple-element.13) | copy-start | bytes 196612
Sparse Core Ops, SparseCore 0:
  43.6 59.8 all-reduce.2
where the time goes:
time: 128 us
  waiting for transfers between devices  40.2 us (31%)
  between operations  25.2 us (20%)
  blocking collectives  19.9 us (16%)
  starting transfers between devices  13.1 us (10%)
  local copies, waits for them, and re-layouts  12.9 us (10%)
  matrix products  8.78 us (7%)
  other arithmetic  7.4 us (6%)
    psum x1, waiting for transfers between devices, broadcast(): return lax.psum(block, axis)  19.1 us
    all_to_all x1, waiting for transfers between devices, on_device(): lax.all_to_all(send_down, 'replica', split_axis=0, concat_axis=0, tiled=T...  14.9 us
    psum x1, blocking collectives, on_device(): lax.psum(jnp.concatenate([stay_partial, moved_partial], axis=0), 'tensor')  11.1 us
    psum x1, blocking collectives, on_device(): usage = lax.psum(usage, 'replica')  8.8 us
    all_to_all x1, starting transfers between devices, on_device(): lax.all_to_all(wanted[:, None], 'replica', split_axis=0, concat_axis=0, t...  6.32 us
    all_to_all x1, waiting for transfers between devices, on_device(): lax.all_to_all(send_up, 'replica', split_axis=0, concat_axis=0, tiled=True)  6.17 us
    unnamed x24, local copies, waits for them, and re-layouts  4.62 us
    all_to_all x1, starting transfers between devices, on_device(): lax.all_to_all(send_up, 'replica', split_axis=0, concat_axis=0, tiled=True)  3.4 us
  transfers between devices with their start and end apart: 4, of which 3 were waited for; matrix products, arithmetic and copies ran while one was open for 16% of the time, Pallas kernels for 0%

commit v1 on v0

v1 whole, which is shorter than its diff:
```python
import functools
import math

import jax
import jax.numpy as jnp
from jax import lax
from jax.experimental import pallas as pl
from jax.experimental.pallas import tpu as pltpu
from jax.sharding import PartitionSpec as P

HEAD_DIM = 128
STAY = 16
SCALING = 2.0
LANES = 128
DIGIT = 7

VMEM = pl.BlockSpec(memory_space=pltpu.VMEM)
SMEM = pl.BlockSpec(memory_space=pltpu.SMEM)
ANY = pl.BlockSpec(memory_space=pl.ANY)


def chunks_of(slots):
    for parts in (3, 4, 2):
        if slots % parts == 0:
            return parts
    return 1


def attend_kernel(q_ref, cache_ref, lengths_ref, live_ref, index_ref, rows_ref, keys, values, q_rows, o_rows, sems):
    slots, cols = q_ref.shape
    heads = cols // HEAD_DIM
    context, width = keys.shape[1:]
    key_heads = width // HEAD_DIM
    group = heads // key_heads
    parts = chunks_of(slots)
    step = slots // parts
    copies = []
    for side, buffer in enumerate((keys, values)):
        for part in range(parts):
            span = pl.ds(part * step, step)
            copy = pltpu.make_async_copy(cache_ref.at[side, span], buffer.at[span], sems.at[side, part])
            copy.start()
            copies.append(copy)
    for head in range(heads):
        block = q_ref[:, head * HEAD_DIM : (head + 1) * HEAD_DIM]
        q_rows[pl.ds(head, slots, stride=heads), :] = block.astype(jnp.float32)
    owner = lax.broadcasted_iota(jnp.int32, (heads, HEAD_DIM), 0) // group
    position = lax.broadcasted_iota(jnp.int32, (heads, context), 1)
    weights = []
    for slot in range(slots):
        if slot % step == 0:
            copies[slot // step].wait()
        rows = q_rows[slot * heads : (slot + 1) * heads, :]
        wide = [jnp.where(owner == k, rows, 0.0) for k in range(key_heads)]
        wide = jnp.concatenate(wide, axis=1).astype(jnp.bfloat16)
        scores = lax.dot_general(
            wide, keys[slot], (((1,), (1,)), ((), ())), preferred_element_type=jnp.float32
        ) / math.sqrt(HEAD_DIM)
        scores = jnp.where(position < lengths_ref[slot], scores, -jnp.inf)
        raised = jnp.exp(scores - jnp.max(scores, axis=-1, keepdims=True))
        weights.append((raised / jnp.sum(raised, axis=-1, keepdims=True)).astype(jnp.bfloat16))
    live = live_ref[0]
    for slot in range(slots):
        if slot % step == 0:
            copies[parts + slot // step].wait()
        mixed = jnp.dot(weights[slot], values[slot], preferred_element_type=jnp.float32)
        rows = mixed[:, :HEAD_DIM]
        for k in range(1, key_heads):
            rows = jnp.where(owner == k, mixed[:, k * HEAD_DIM : (k + 1) * HEAD_DIM], rows)
        if slot < STAY:
            rows = jnp.where(slot < live, rows, 0.0)
        o_rows[slot * heads : (slot + 1) * heads, :] = rows
    rows_ref[: slots * heads, :] = o_rows[...].astype(jnp.bfloat16)
    lane = lax.broadcasted_iota(jnp.int32, (16, LANES), 1)
    line = lax.broadcasted_iota(jnp.int32, (16, LANES), 0)
    index = jnp.zeros((16, LANES), jnp.int32)
    for slot in range(slots):
        index = jnp.where(lane == slot, index_ref[slot], index)
    digits = jnp.where(line == 0, index >> DIGIT, index & ((1 << DIGIT) - 1))
    rows_ref[slots * heads :, :] = digits.astype(jnp.float32).astype(jnp.bfloat16)


def attend(queries, past_cache, lengths, live_counts, adapter_index):
    slots, cols = queries.shape
    heads = cols // HEAD_DIM
    buffer = pltpu.VMEM(past_cache.shape[1:], past_cache.dtype)
    return pl.pallas_call(
        attend_kernel,
        out_shape=jax.ShapeDtypeStruct((slots * heads + 16, HEAD_DIM), jnp.bfloat16),
        in_specs=[VMEM, ANY, SMEM, SMEM, SMEM],
        out_specs=VMEM,
        scratch_shapes=[
            buffer,
            buffer,
            pltpu.VMEM((slots * heads, HEAD_DIM), jnp.float32),
            pltpu.VMEM((slots * heads, HEAD_DIM), jnp.float32),
            pltpu.SemaphoreType.DMA((2, chunks_of(slots))),
        ],
        cost_estimate=pl.CostEstimate(
            flops=4 * past_cache.size * heads, bytes_accessed=2 * past_cache.size, transcendentals=0
        ),
        name="attend",
    )(queries, past_cache, lengths, live_counts, adapter_index)


def unfold_kernel(slots, heads, rows_ref, out_ref, flat):
    flat[...] = rows_ref[: slots * heads, :].astype(jnp.float32)
    for head in range(heads):
        out_ref[:, head * HEAD_DIM : (head + 1) * HEAD_DIM] = flat[
            pl.ds(head, slots, stride=heads), :
        ].astype(out_ref.dtype)


def unfold(rows, slots, heads):
    return pl.pallas_call(
        functools.partial(unfold_kernel, slots, heads),
        out_shape=jax.ShapeDtypeStruct((slots, heads * HEAD_DIM), jnp.bfloat16),
        in_specs=[VMEM],
        out_specs=VMEM,
        scratch_shapes=[pltpu.VMEM((slots * heads, HEAD_DIM), jnp.float32)],
        name="unfold",
    )(rows)


def lower_kernel(slots, heads, pad, sources, base_ref, down_ref, *refs):
    rows_refs = refs[:sources]
    partial_ref, index_ref, flat, wide = refs[sources:]
    local_count, rank, cols = down_ref.shape
    for source in range(sources):
        flat[source, : slots * heads, :] = rows_refs[source][: slots * heads, :].astype(jnp.float32)
        if pad > slots:
            flat[source, slots * heads :, :] = jnp.zeros(((pad - slots) * heads, HEAD_DIM), jnp.float32)
        digits = rows_refs[source][slots * heads :, :].astype(jnp.float32).astype(jnp.int32)
        index = (digits[0:1, :] << DIGIT) + digits[1:2, :]
        index_ref[:, source * pad : (source + 1) * pad] = index[:, :pad]
    for source in range(sources):
        for head in range(heads):
            wide[source * pad : (source + 1) * pad, head * HEAD_DIM : (head + 1) * HEAD_DIM] = flat[
                source, pl.ds(head, pad, stride=heads), :
            ].astype(jnp.bfloat16)
    down = down_ref[...].reshape(local_count * rank, cols)
    every = lax.dot_general(down, wide[...], (((1,), (1,)), ((), ())), preferred_element_type=jnp.float32)
    total = jnp.zeros((rank, sources * pad), jnp.float32)
    for local in range(local_count):
        mine = index_ref[...] == base_ref[0] + local
        total += jnp.where(mine, every[local * rank : (local + 1) * rank, :], 0.0)
    partial_ref[...] = total


def lower(base, down, rows, slots, heads, pad):
    sources = len(rows)
    lanes = sources * pad
    cols = heads * HEAD_DIM
    return pl.pallas_call(
        functools.partial(lower_kernel, slots, heads, pad, sources),
        out_shape=(
            jax.ShapeDtypeStruct((down.shape[1], lanes), jnp.float32),
            jax.ShapeDtypeStruct((1, lanes), jnp.int32),
        ),
        in_specs=[SMEM] + [VMEM] * (1 + sources),
        out_specs=(VMEM, VMEM),
        scratch_shapes=[
            pltpu.VMEM((sources, pad * heads, HEAD_DIM), jnp.float32),
            pltpu.VMEM((lanes, cols), jnp.bfloat16),
        ],
        compiler_params=pltpu.CompilerParams(vmem_limit_bytes=32 * 2**20),
        name="lower",
    )(base, down, *rows)


def raise_kernel(slots, heads, pad, sources, base_ref, index_ref, up_ref, *refs):
    tensor = len(refs) - sources - 1
    partials = refs[:tensor]
    outs = refs[tensor : tensor + sources]
    flat = refs[-1]
    local_count, rank, cols = up_ref.shape
    total = partials[0][...]
    for other in partials[1:]:
        total += other[...]
    total = SCALING * total
    high = total.astype(jnp.bfloat16).astype(jnp.float32)
    spread = []
    for part in (high, total - high):
        for local in range(local_count):
            mine = index_ref[...] == base_ref[0] + local
            spread.append(jnp.where(mine, part, 0.0))
    spread = jnp.concatenate(spread, axis=0).astype(jnp.bfloat16)
    up = up_ref[...].reshape(local_count * rank, cols)
    up = jnp.concatenate([up, up], axis=0)
    block = min(sources, max(1, LANES // pad))
    for first in range(0, sources, block):
        count = min(block, sources - first)
        part = spread[:, first * pad : (first + count) * pad]
        wide = lax.dot_general(part, up, (((0,), (0,)), ((), ())), preferred_element_type=jnp.float32)
        for source in range(count):
            for head in range(heads):
                flat[source, pl.ds(head, slots, stride=heads), :] = wide[
                    source * pad : source * pad + slots, head * HEAD_DIM : (head + 1) * HEAD_DIM
                ]
        for source in range(count):
            outs[first + source][...] = flat[source].astype(jnp.bfloat16)


def raise_rows(base, index, up, partials, slots, heads, pad, sources):
    block = min(sources, max(1, LANES // pad))
    return pl.pallas_call(
        functools.partial(raise_kernel, slots, heads, pad, sources),
        out_shape=[jax.ShapeDtypeStruct((slots * heads, HEAD_DIM), jnp.bfloat16)] * sources,
        in_specs=[SMEM] + [VMEM] * (2 + len(partials)),
        out_specs=[VMEM] * sources,
        scratch_shapes=[pltpu.VMEM((block, slots * heads, HEAD_DIM), jnp.float32)],
        compiler_params=pltpu.CompilerParams(vmem_limit_bytes=32 * 2**20),
        name="raise_rows",
    )(base, index, up, *partials)


def merge_kernel(slots, heads, *refs):
    rows_refs, out_ref, flat = refs[:-2], refs[-2], refs[-1]
    total = rows_refs[0][...].astype(jnp.float32)
    for other in rows_refs[1:]:
        total += other[...].astype(jnp.float32)
    flat[...] = total
    for head in range(heads):
        out_ref[:, head * HEAD_DIM : (head + 1) * HEAD_DIM] = flat[
            pl.ds(head, slots, stride=heads), :
        ].astype(out_ref.dtype)


def merge(rows, slots, heads):
    return pl.pallas_call(
        functools.partial(merge_kernel, slots, heads),
        out_shape=jax.ShapeDtypeStruct((slots, heads * HEAD_DIM), jnp.bfloat16),
        in_specs=[VMEM] * len(rows),
        out_specs=VMEM,
        scratch_shapes=[pltpu.VMEM((slots * heads, HEAD_DIM), jnp.float32)],
        name="merge",
    )(*rows)


def shift(block, axis, offset):
    size = lax.axis_size(axis)
    return lax.ppermute(block, axis, [(i, (i + offset) % size) for i in range(size)])


def on_device(queries, past_cache, lengths, live_counts, adapter_index, adapter_down, adapter_up):
    slots, cols = queries.shape
    heads = cols // HEAD_DIM
    replicas = lax.axis_size("replica")
    tensor = lax.axis_size("tensor")
    pad = 16
    while pad < slots or pad * replicas % LANES:
        pad *= 2
    base = (lax.axis_index("replica") * adapter_down.shape[0]).astype(jnp.int32).reshape(1)
    rows = attend(queries, past_cache, lengths, live_counts, adapter_index)
    gathered = [rows] + [shift(rows, "replica", k) for k in range(1, replicas)]
    attention = unfold(rows, slots, heads)
    partial, index = lower(base, adapter_down, gathered, slots, heads, pad)
    partials = [partial] + [shift(partial, "tensor", k) for k in range(1, tensor)]
    widened = raise_rows(base, index, adapter_up, partials, slots, heads, pad, replicas)
    returned = [widened[0]] + [shift(widened[k], "replica", -k) for k in range(1, replicas)]
    adapted = merge(returned, slots, heads)
    return (attention, adapted)


def solution(mesh):
    in_specs = (
        P(("groups", "replica"), "tensor"),
        P(None, ("groups", "replica"), None, "tensor"),
        P(("groups", "replica")),
        P(("groups", "replica")),
        P(("groups", "replica")),
        P("replica", None, "tensor"),
        P("replica", None, "tensor"),
    )
    out_specs = (P(("groups", "replica"), "tensor"), P(("groups", "replica"), "tensor"))
    return jax.shard_map(
        on_device, mesh=mesh, in_specs=in_specs, out_specs=out_specs, check_vma=False
    )
```

time: 128 us -> 37.7 us (0.29)
  waiting for transfers between devices: 40.2 us -> 11.3 us
  between operations: 25.2 us -> 1.4 us
  blocking collectives: 19.9 us -> 0 us
  local copies, waits for them, and re-layouts: 12.9 us -> 2.18 us
  matrix products: 8.78 us -> 0 us
  Pallas kernels: 0 us -> 8.66 us
  other arithmetic: 7.4 us -> 0 us
    all_to_all x3 -> x0, waiting for transfers between devices: 21.1 us -> none  [the longest x1 14.9 us: on_device(): lax.all_to_all(send_down, 'replica', split_axis=0, concat_axis=0, tiled=T...]
    psum x2 -> x0, blocking collectives: 19.9 us -> none  [the longest x1 11.1 us: on_device(): lax.psum(jnp.concatenate([stay_partial, moved_partial], axis=0), 'tensor')]
    psum x1 -> x0, waiting for transfers between devices: 19.1 us -> none  [broadcast(): return lax.psum(block, axis)]
    ppermute x0 -> x9, starting transfers between devices: none -> 13.8 us  [shift(): lax.ppermute(block, axis, [(i, (i + offset) % size) for i in range(size)])]
    all_to_all x3 -> x0, starting transfers between devices: 13.1 us -> none  [the longest x1 6.32 us: on_device(): lax.all_to_all(wanted[:, None], 'replica', split_axis=0, concat_axis=0, t...]
    ppermute x0 -> x9, waiting for transfers between devices: none -> 11.3 us  [shift(): lax.ppermute(block, axis, [(i, (i + offset) % size) for i in range(size)])]
    dot_general x12 -> x0, matrix products: 8.78 us -> none  [the longest x2 2.15 us: attend(): jnp.einsum('nhgl,nlhd->nhgd', weights, value_rows, preferred_element_type...]
    pallas_call x0 -> x5, Pallas kernels: none -> 8.66 us  [the longest x1 4.24 us: attend(): pl.pallas_call(attend_kernel, out_shape=jax.ShapeDtypeStruct((slots * hea...]
  transfers between devices with their start and end apart: 4 -> 9, of which waited for: 3 -> 8; matrix products, arithmetic and copies ran while one was open for 16% -> 0% of each run, Pallas kernels for 0% -> 4%
where the time goes in v1:
time: 37.7 us; the launch traced here: 37.4 us
  starting transfers between devices  13.8 us (37%)
  waiting for transfers between devices  11.3 us (30%)
  Pallas kernels  8.66 us (23%)
  local copies, waits for them, and re-layouts  2.18 us (6%)
  between operations  1.4 us (4%)
    ppermute x9, starting transfers between devices, shift(): lax.ppermute(block, axis, [(i, (i + offset) % size) for i in range(size)])  13.8 us
    ppermute x9, waiting for transfers between devices, shift(): lax.ppermute(block, axis, [(i, (i + offset) % size) for i in range(size)])  11.3 us
    pallas_call x1, Pallas kernels, attend(): pl.pallas_call(attend_kernel, out_shape=jax.ShapeDtypeStruct((slots * hea...  4.24 us
    unnamed x14, local copies, waits for them, and re-layouts  2.18 us
    pallas_call x1, Pallas kernels, merge(): pl.pallas_call(functools.partial(merge_kernel, slots, heads), out_shape=j...  1.73 us
    pallas_call x1, Pallas kernels, unfold(): pl.pallas_call(functools.partial(unfold_kernel, slots, heads), out_shape=...  1.59 us
  transfers between devices with their start and end apart: 9, of which 8 were waited for; matrix products, arithmetic and copies ran while one was open for 0% of the time, Pallas kernels for 4%

profile of v1, /device:TPU:0, one launch (start us, length us, event | category | flops | bytes accessed | tf_op | source)
XLA Modules:
  0.0 37.4 jit_solution(902300638454916003)
XLA Ops:
  0.6 0.0 copy-start.2
  0.6 0.0 copy-start.1
  1.4 4.2 %attend.1.rows_ref.refs_0_ = bf16[304,128]{1,0:T(8,128)(2,1)} custom-call(bf16[18,2048]{1,0:T(8,128)(2,1)} %q_ref.1, bf16[2,18,128,256]{3,2,1,0:T(8,128)(2,1)} %cache_ref.1, s32[18]{0:T(128)} %lengths_ref.1, s32[1]{0:T(128)S(6)} %copy.9.live_ref, s32[18]{0:T(128)} %index_ref.1), custom_call_target="tpu_custom_call" | custom-call | flops 75497472 | bytes 2359296 | tf_op jit(solution)/shard_map/attend/pallas_call | solution.py:87
  5.6 3.1 %collective-permute-start = (bf16[304,128]{1,0:T(8,128)(2,1)}, bf16[304,128]{1,0:T(8,128)(2,1)S(1)}, u32[]{:S(2)}, u32[]{:S(2)}) collective-permute-start(bf16[304,128]{1,0:T(8,128)(2,1)} %attend.1.rows_ref.refs_0_), channel_id=1, source_target_pairs={{0,4},{4,8},{8,12},{12,0},{1,5},{5,9},{9,13},{13,1},{2,6},{6,10},{... | collective-permute-start | bytes 233480 | tf_op jit(solution)/shard_map/ppermute | solution.py:242
  8.7 2.6 %collective-permute-start.1 = (bf16[304,128]{1,0:T(8,128)(2,1)}, bf16[304,128]{1,0:T(8,128)(2,1)S(1)}, u32[]{:S(2)}, u32[]{:S(2)}) collective-permute-start(bf16[304,128]{1,0:T(8,128)(2,1)} %attend.1.rows_ref.refs_0_), channel_id=1, source_target_pairs={{0,8},{4,12},{8,0},{12,4},{1,9},{5,13},{9,1},{13,5},{2,10},{6,14},... | collective-permute-start | bytes 233480 | tf_op jit(solution)/shard_map/ppermute | solution.py:242
  11.3 1.3 %collective-permute-start.2 = (bf16[304,128]{1,0:T(8,128)(2,1)}, bf16[304,128]{1,0:T(8,128)(2,1)S(1)}, u32[]{:S(2)}, u32[]{:S(2)}) collective-permute-start(bf16[304,128]{1,0:T(8,128)(2,1)} %attend.1.rows_ref.refs_0_), channel_id=1, source_target_pairs={{0,12},{4,0},{8,4},{12,8},{1,13},{5,1},{9,5},{13,9},{2,14},{6,2},{... | collective-permute-start | bytes 233480 | tf_op jit(solution)/shard_map/ppermute | solution.py:242
  12.6 1.2 %collective-permute-done.refs_1_ = bf16[304,128]{1,0:T(8,128)(2,1)S(1)} collective-permute-done((bf16[304,128]{1,0:T(8,128)(2,1)}, bf16[304,128]{1,0:T(8,128)(2,1)S(1)}, u32[]{:S(2)}, u32[]{:S(2)}) %collective-permute-start) | collective-permute-done | bytes 77856 | tf_op jit(solution)/shard_map/ppermute | solution.py:242
  13.8 2.9 %collective-permute-done.1.refs_2_ = bf16[304,128]{1,0:T(8,128)(2,1)S(1)} collective-permute-done((bf16[304,128]{1,0:T(8,128)(2,1)}, bf16[304,128]{1,0:T(8,128)(2,1)S(1)}, u32[]{:S(2)}, u32[]{:S(2)}) %collective-permute-start.1) | collective-permute-done | bytes 77856 | tf_op jit(solution)/shard_map/ppermute | solution.py:242
  16.7 0.2 collective-permute-done.2.refs_3_
  16.9 0.0 copy-done.2
  16.9 0.9 %copy-done = bf16[304,128]{1,0:T(8,128)(2,1)S(1)} copy-done((bf16[304,128]{1,0:T(8,128)(2,1)S(1)}, bf16[304,128]{1,0:T(8,128)(2,1)}, u32[]{:S(2)}) %copy-start) | copy-done | bytes 77848
  17.8 0.7 %lower.1 = (f32[16,128]{1,0:T(8,128)S(1)}, s32[1,128]{1,0:T(1,128)S(1)}) custom-call(s32[1]{0:T(128)} %bitcast.base_ref, bf16[4,16,2048]{2,1,0:T(8,128)(2,1)S(1)} %copy-done.2, bf16[304,128]{1,0:T(8,128)(2,1)S(1)} %copy-done, bf16[304,128]{1,0:T(8,128)(2,1)S(1)} %collective-permute-done.refs_1_, bf16[304,128]{1,0:T(8,128)(2,1)S(1)} %collective-permute-done.1.refs_2_, ...), custom_call_target="tpu_custom_call" | custom-call | tf_op jit(solution)/shard_map/lower/pallas_call | solution.py:154
  18.5 0.1 collective-permute-start.3
  18.5 1.6 %collective-permute-start.4 = (f32[16,128]{1,0:T(8,128)S(1)}, f32[16,128]{1,0:T(8,128)S(1)}, u32[]{:S(2)}, u32[]{:S(2)}) collective-permute-start(f32[16,128]{1,0:T(8,128)S(1)} %get-tuple-element.9.refs_0_), channel_id=1, source_target_pairs={{0,2},{1,3},{2,0},{3,1},{4,6},{5,7},{6,4},{7,5},{8,10},{9,11},{10,... | collective-permute-start | bytes 24584 | tf_op jit(solution)/shard_map/ppermute | solution.py:242
  20.1 1.4 %collective-permute-start.5 = (f32[16,128]{1,0:T(8,128)S(1)}, f32[16,128]{1,0:T(8,128)S(1)}, u32[]{:S(2)}, u32[]{:S(2)}) collective-permute-start(f32[16,128]{1,0:T(8,128)S(1)} %get-tuple-element.9.refs_0_), channel_id=1, source_target_pairs={{0,3},{1,0},{2,1},{3,2},{4,7},{5,4},{6,5},{7,6},{8,11},{9,8},{10,9... | collective-permute-start | bytes 24584 | tf_op jit(solution)/shard_map/ppermute | solution.py:242
  21.5 0.1 collective-permute-done.3.refs_1_
  21.6 0.7 %collective-permute-done.4.refs_2_ = f32[16,128]{1,0:T(8,128)S(1)} collective-permute-done((f32[16,128]{1,0:T(8,128)S(1)}, f32[16,128]{1,0:T(8,128)S(1)}, u32[]{:S(2)}, u32[]{:S(2)}) %collective-permute-start.4) | collective-permute-done | bytes 8224 | tf_op jit(solution)/shard_map/ppermute | solution.py:242
  22.3 0.6 %collective-permute-done.5.refs_3_ = f32[16,128]{1,0:T(8,128)S(1)} collective-permute-done((f32[16,128]{1,0:T(8,128)S(1)}, f32[16,128]{1,0:T(8,128)S(1)}, u32[]{:S(2)}, u32[]{:S(2)}) %collective-permute-start.5) | collective-permute-done | bytes 8224 | tf_op jit(solution)/shard_map/ppermute | solution.py:242
  22.9 0.0 copy-done.1
  22.9 0.4 %raise_rows.1 = (bf16[288,128]{1,0:T(8,128)(2,1)S(1)}, bf16[288,128]{1,0:T(8,128)(2,1)S(1)}, bf16[288,128]{1,0:T(8,128)(2,1)S(1)}, bf16[288,128]{1,0:T(8,128)(2,1)S(1)}) custom-call(s32[1]{0:T(128)} %bitcast.base_ref, s32[1,128]{1,0:T(1,128)S(1)} %get-tuple-element.8.index_ref, bf16[4,16,2048]{2,1,0:T(8,128)(2,1)S(1)} %copy-done.1, ...), custom_call_target="tpu_custom_call" | custom-call | tf_op jit(solution)/shard_map/raise_rows/pallas_call | solution.py:206
  23.3 0.6 %copy-done.3 = bf16[288,128]{1,0:T(8,128)(2,1)} copy-done((bf16[288,128]{1,0:T(8,128)(2,1)}, bf16[288,128]{1,0:T(8,128)(2,1)S(1)}, u32[]{:S(2)}) %copy-start.3) | copy-done | bytes 73752
  23.9 3.2 %collective-permute-start.6 = (bf16[288,128]{1,0:T(8,128)(2,1)S(1)}, bf16[288,128]{1,0:T(8,128)(2,1)S(1)}, u32[]{:S(2)}, u32[]{:S(2)}) collective-permute-start(bf16[288,128]{1,0:T(8,128)(2,1)S(1)} %get-tuple-element.11), channel_id=1, source_target_pairs={{0,12},{4,0},{8,4},{12,8},{1,13},{5,1},{9,5},{13,9},{2,14},{6,2},{... | collective-permute-start | bytes 221192 | tf_op jit(solution)/shard_map/ppermute | solution.py:242
  27.2 0.1 collective-permute-start.7
  27.3 0.4 %collective-permute-start.8 = (bf16[288,128]{1,0:T(8,128)(2,1)S(1)}, bf16[288,128]{1,0:T(8,128)(2,1)S(1)}, u32[]{:S(2)}, u32[]{:S(2)}) collective-permute-start(bf16[288,128]{1,0:T(8,128)(2,1)S(1)} %get-tuple-element.13), channel_id=1, source_target_pairs={{0,4},{4,8},{8,12},{12,0},{1,5},{5,9},{9,13},{13,1},{2,6},{6,10},{... | collective-permute-start | bytes 221192 | tf_op jit(solution)/shard_map/ppermute | solution.py:242
  27.7 1.6 %unfold.1 = bf16[18,2048]{1,0:T(8,128)(2,1)} custom-call(bf16[304,128]{1,0:T(8,128)(2,1)} %attend.1.rows_ref.refs_0_), custom_call_target="tpu_custom_call" | custom-call | tf_op jit(solution)/shard_map/unfold/pallas_call | solution.py:115
  29.3 0.5 %collective-permute-done.6.refs_1_ = bf16[288,128]{1,0:T(8,128)(2,1)S(1)} collective-permute-done((bf16[288,128]{1,0:T(8,128)(2,1)S(1)}, bf16[288,128]{1,0:T(8,128)(2,1)S(1)}, u32[]{:S(2)}, u32[]{:S(2)}) %collective-permute-start.6) | collective-permute-done | bytes 73760 | tf_op jit(solution)/shard_map/ppermute | solution.py:242
  29.8 5.2 %collective-permute-done.7.refs_2_ = bf16[288,128]{1,0:T(8,128)(2,1)S(1)} collective-permute-done((bf16[288,128]{1,0:T(8,128)(2,1)S(1)}, bf16[288,128]{1,0:T(8,128)(2,1)S(1)}, u32[]{:S(2)}, u32[]{:S(2)}) %collective-permute-start.7) | collective-permute-done | bytes 73760 | tf_op jit(solution)/shard_map/ppermute | solution.py:242
  35.0 0.0 collective-permute-done.8.refs_3_
  35.0 0.0 copy-done.4
  35.0 0.6 %copy-done.5 = bf16[288,128]{1,0:T(8,128)(2,1)} copy-done((bf16[288,128]{1,0:T(8,128)(2,1)}, bf16[288,128]{1,0:T(8,128)(2,1)S(1)}, u32[]{:S(2)}) %copy-start.5) | copy-done | bytes 73752
  35.6 0.0 copy-done.6
  35.6 1.7 %merge.1 = bf16[18,2048]{1,0:T(8,128)(2,1)} custom-call(bf16[288,128]{1,0:T(8,128)(2,1)} %copy-done.3, bf16[288,128]{1,0:T(8,128)(2,1)} %copy-done.4, bf16[288,128]{1,0:T(8,128)(2,1)} %copy-done.5, bf16[288,128]{1,0:T(8,128)(2,1)} %copy-done.6), custom_call_target="tpu_custom_call" | custom-call | tf_op jit(solution)/shard_map/merge/pallas_call | solution.py:230
  (5 shorter events, 0.0 us)
Async XLA Ops:
  0.6 16.3 %copy-start.2 = (bf16[4,16,2048]{2,1,0:T(8,128)(2,1)S(1)}, bf16[4,16,2048]{2,1,0:T(8,128)(2,1)}, u32[]{:S(2)}) copy-start(bf16[4,16,2048]{2,1,0:T(8,128)(2,1)} %down_ref.1) | copy-start | bytes 786436
  0.6 22.2 %copy-start.1 = (bf16[4,16,2048]{2,1,0:T(8,128)(2,1)S(1)}, bf16[4,16,2048]{2,1,0:T(8,128)(2,1)}, u32[]{:S(2)}) copy-start(bf16[4,16,2048]{2,1,0:T(8,128)(2,1)} %up_ref.1) | copy-start | bytes 786436
  5.6 8.2 %collective-permute-start = (bf16[304,128]{1,0:T(8,128)(2,1)}, bf16[304,128]{1,0:T(8,128)(2,1)S(1)}, u32[]{:S(2)}, u32[]{:S(2)}) collective-permute-start(bf16[304,128]{1,0:T(8,128)(2,1)} %attend.1.rows_ref.refs_0_), channel_id=1, source_target_pairs={{0,4},{4,8},{8,12},{12,0},{1,5},{5,9},{9,13},{13,1},{2,6},{6,10},{... | collective-permute-start | bytes 233480 | tf_op jit(solution)/shard_map/ppermute | solution.py:242
  8.7 8.0 %collective-permute-start.1 = (bf16[304,128]{1,0:T(8,128)(2,1)}, bf16[304,128]{1,0:T(8,128)(2,1)S(1)}, u32[]{:S(2)}, u32[]{:S(2)}) collective-permute-start(bf16[304,128]{1,0:T(8,128)(2,1)} %attend.1.rows_ref.refs_0_), channel_id=1, source_target_pairs={{0,8},{4,12},{8,0},{12,4},{1,9},{5,13},{9,1},{13,5},{2,10},{6,14},... | collective-permute-start | bytes 233480 | tf_op jit(solution)/shard_map/ppermute | solution.py:242
  11.3 5.6 %collective-permute-start.2 = (bf16[304,128]{1,0:T(8,128)(2,1)}, bf16[304,128]{1,0:T(8,128)(2,1)S(1)}, u32[]{:S(2)}, u32[]{:S(2)}) collective-permute-start(bf16[304,128]{1,0:T(8,128)(2,1)} %attend.1.rows_ref.refs_0_), channel_id=1, source_target_pairs={{0,12},{4,0},{8,4},{12,8},{1,13},{5,1},{9,5},{13,9},{2,14},{6,2},{... | collective-permute-start | bytes 233480 | tf_op jit(solution)/shard_map/ppermute | solution.py:242
  16.9 0.9 %copy-start = (bf16[304,128]{1,0:T(8,128)(2,1)S(1)}, bf16[304,128]{1,0:T(8,128)(2,1)}, u32[]{:S(2)}) copy-start(bf16[304,128]{1,0:T(8,128)(2,1)} %attend.1.rows_ref.refs_0_) | copy-start | bytes 233476
  18.5 3.1 %collective-permute-start.3 = (f32[16,128]{1,0:T(8,128)S(1)}, f32[16,128]{1,0:T(8,128)S(1)}, u32[]{:S(2)}, u32[]{:S(2)}) collective-permute-start(f32[16,128]{1,0:T(8,128)S(1)} %get-tuple-element.9.refs_0_), channel_id=1, source_target_pairs={{0,1},{1,2},{2,3},{3,0},{4,5},{5,6},{6,7},{7,4},{8,9},{9,10},{10,1... | collective-permute-start | bytes 24584 | tf_op jit(solution)/shard_map/ppermute | solution.py:242
  18.5 3.7 %collective-permute-start.4 = (f32[16,128]{1,0:T(8,128)S(1)}, f32[16,128]{1,0:T(8,128)S(1)}, u32[]{:S(2)}, u32[]{:S(2)}) collective-permute-start(f32[16,128]{1,0:T(8,128)S(1)} %get-tuple-element.9.refs_0_), channel_id=1, source_target_pairs={{0,2},{1,3},{2,0},{3,1},{4,6},{5,7},{6,4},{7,5},{8,10},{9,11},{10,... | collective-permute-start | bytes 24584 | tf_op jit(solution)/shard_map/ppermute | solution.py:242
  20.1 2.8 %collective-permute-start.5 = (f32[16,128]{1,0:T(8,128)S(1)}, f32[16,128]{1,0:T(8,128)S(1)}, u32[]{:S(2)}, u32[]{:S(2)}) collective-permute-start(f32[16,128]{1,0:T(8,128)S(1)} %get-tuple-element.9.refs_0_), channel_id=1, source_target_pairs={{0,3},{1,0},{2,1},{3,2},{4,7},{5,4},{6,5},{7,6},{8,11},{9,8},{10,9... | collective-permute-start | bytes 24584 | tf_op jit(solution)/shard_map/ppermute | solution.py:242
  23.3 0.6 %copy-start.3 = (bf16[288,128]{1,0:T(8,128)(2,1)}, bf16[288,128]{1,0:T(8,128)(2,1)S(1)}, u32[]{:S(2)}) copy-start(bf16[288,128]{1,0:T(8,128)(2,1)S(1)} %get-tuple-element.10.refs_0_) | copy-start | bytes 221188
  23.9 5.9 %collective-permute-start.6 = (bf16[288,128]{1,0:T(8,128)(2,1)S(1)}, bf16[288,128]{1,0:T(8,128)(2,1)S(1)}, u32[]{:S(2)}, u32[]{:S(2)}) collective-permute-start(bf16[288,128]{1,0:T(8,128)(2,1)S(1)} %get-tuple-element.11), channel_id=1, source_target_pairs={{0,12},{4,0},{8,4},{12,8},{1,13},{5,1},{9,5},{13,9},{2,14},{6,2},{... | collective-permute-start | bytes 221192 | tf_op jit(solution)/shard_map/ppermute | solution.py:242
  27.2 7.8 %collective-permute-start.7 = (bf16[288,128]{1,0:T(8,128)(2,1)S(1)}, bf16[288,128]{1,0:T(8,128)(2,1)S(1)}, u32[]{:S(2)}, u32[]{:S(2)}) collective-permute-start(bf16[288,128]{1,0:T(8,128)(2,1)S(1)} %get-tuple-element.12), channel_id=1, source_target_pairs={{0,8},{4,12},{8,0},{12,4},{1,9},{5,13},{9,1},{13,5},{2,10},{6,14},... | collective-permute-start | bytes 221192 | tf_op jit(solution)/shard_map/ppermute | solution.py:242
  27.3 7.7 %collective-permute-start.8 = (bf16[288,128]{1,0:T(8,128)(2,1)S(1)}, bf16[288,128]{1,0:T(8,128)(2,1)S(1)}, u32[]{:S(2)}, u32[]{:S(2)}) collective-permute-start(bf16[288,128]{1,0:T(8,128)(2,1)S(1)} %get-tuple-element.13), channel_id=1, source_target_pairs={{0,4},{4,8},{8,12},{12,0},{1,5},{5,9},{9,13},{13,1},{2,6},{6,10},{... | collective-permute-start | bytes 221192 | tf_op jit(solution)/shard_map/ppermute | solution.py:242
  29.8 5.2 %copy-start.4 = (bf16[288,128]{1,0:T(8,128)(2,1)}, bf16[288,128]{1,0:T(8,128)(2,1)S(1)}, u32[]{:S(2)}) copy-start(bf16[288,128]{1,0:T(8,128)(2,1)S(1)} %collective-permute-done.6.refs_1_) | copy-start | bytes 221188
  35.0 0.6 %copy-start.5 = (bf16[288,128]{1,0:T(8,128)(2,1)}, bf16[288,128]{1,0:T(8,128)(2,1)S(1)}, u32[]{:S(2)}) copy-start(bf16[288,128]{1,0:T(8,128)(2,1)S(1)} %collective-permute-done.7.refs_2_) | copy-start | bytes 221188
  35.0 0.7 %copy-start.6 = (bf16[288,128]{1,0:T(8,128)(2,1)}, bf16[288,128]{1,0:T(8,128)(2,1)S(1)}, u32[]{:S(2)}) copy-start(bf16[288,128]{1,0:T(8,128)(2,1)S(1)} %collective-permute-done.8.refs_3_) | copy-start | bytes 221188

commit v2 on v1

v2 whole, which is shorter than its diff:
```python
import functools
import math

import jax
import jax.numpy as jnp
from jax import lax
from jax.experimental import pallas as pl
from jax.experimental.pallas import tpu as pltpu
from jax.sharding import PartitionSpec as P

HEAD_DIM = 128
STAY = 16
SCALING = 2.0
LANES = 128
DIGIT = 7

VMEM = pl.BlockSpec(memory_space=pltpu.VMEM)
SMEM = pl.BlockSpec(memory_space=pltpu.SMEM)
HBM = pl.BlockSpec(memory_space=pltpu.HBM)
PARAMS = pltpu.CompilerParams(vmem_limit_bytes=16 * 2**20)


def chunks_of(slots):
    for parts in (3, 4, 2):
        if slots % parts == 0:
            return parts
    return 1


def attend_kernel(
    q_ref, cache_ref, lengths_ref, index_ref, rows_ref,
    q_flat, lengths, index, keys, values, q_rows, o_rows, small, large,
):
    slots, cols = q_ref.shape
    heads = cols // HEAD_DIM
    context, width = keys.shape[1:]
    key_heads = width // HEAD_DIM
    group = heads // key_heads
    parts = chunks_of(slots)
    step = slots // parts
    fetches = []
    for number, (source, target) in enumerate(((q_ref, q_flat), (lengths_ref, lengths), (index_ref, index))):
        fetches.append(pltpu.make_async_copy(source, target, small.at[number]))
        fetches[-1].start()
    copies = []
    for side, buffer in enumerate((keys, values)):
        for part in range(parts):
            span = pl.ds(part * step, step)
            copies.append(pltpu.make_async_copy(cache_ref.at[side, span], buffer.at[span], large.at[side, part]))
            copies[-1].start()
    for fetch in fetches:
        fetch.wait()
    for head in range(heads):
        block = q_flat[:, head * HEAD_DIM : (head + 1) * HEAD_DIM]
        q_rows[pl.ds(head, slots, stride=heads), :] = block.astype(jnp.float32)
    owner = lax.broadcasted_iota(jnp.int32, (heads, HEAD_DIM), 0) // group
    position = lax.broadcasted_iota(jnp.int32, (heads, context), 1)
    weights = []
    for slot in range(slots):
        if slot % step == 0:
            copies[slot // step].wait()
        rows = q_rows[slot * heads : (slot + 1) * heads, :]
        wide = [jnp.where(owner == k, rows, 0.0) for k in range(key_heads)]
        wide = jnp.concatenate(wide, axis=1).astype(jnp.bfloat16)
        scores = lax.dot_general(
            wide, keys[slot], (((1,), (1,)), ((), ())), preferred_element_type=jnp.float32
        ) / math.sqrt(HEAD_DIM)
        scores = jnp.where(position < lengths[slot], scores, -jnp.inf)
        raised = jnp.exp(scores - jnp.max(scores, axis=-1, keepdims=True))
        weights.append((raised / jnp.sum(raised, axis=-1, keepdims=True)).astype(jnp.bfloat16))
    for slot in range(slots):
        if slot % step == 0:
            copies[parts + slot // step].wait()
        mixed = jnp.dot(weights[slot], values[slot], preferred_element_type=jnp.float32)
        rows = mixed[:, :HEAD_DIM]
        for k in range(1, key_heads):
            rows = jnp.where(owner == k, mixed[:, k * HEAD_DIM : (k + 1) * HEAD_DIM], rows)
        o_rows[slot * heads : (slot + 1) * heads, :] = rows
    rows_ref[: slots * heads, :] = o_rows[...].astype(jnp.bfloat16)
    lane = lax.broadcasted_iota(jnp.int32, (16, LANES), 1)
    line = lax.broadcasted_iota(jnp.int32, (16, LANES), 0)
    named = jnp.zeros((16, LANES), jnp.int32)
    for slot in range(slots):
        named = jnp.where(lane == slot, index[slot], named)
    digits = jnp.where(line == 0, named >> DIGIT, named & ((1 << DIGIT) - 1))
    rows_ref[slots * heads :, :] = digits.astype(jnp.float32).astype(jnp.bfloat16)


def attend(queries, past_cache, lengths, adapter_index):
    slots, cols = queries.shape
    heads = cols // HEAD_DIM
    buffer = pltpu.VMEM(past_cache.shape[1:], past_cache.dtype)
    return pl.pallas_call(
        attend_kernel,
        out_shape=jax.ShapeDtypeStruct((slots * heads + 16, HEAD_DIM), jnp.bfloat16),
        in_specs=[HBM] * 4,
        out_specs=VMEM,
        scratch_shapes=[
            pltpu.VMEM(queries.shape, queries.dtype),
            pltpu.SMEM(lengths.shape, jnp.int32),
            pltpu.SMEM(adapter_index.shape, jnp.int32),
            buffer,
            buffer,
            pltpu.VMEM((slots * heads, HEAD_DIM), jnp.float32),
            pltpu.VMEM((slots * heads, HEAD_DIM), jnp.float32),
            pltpu.SemaphoreType.DMA((3,)),
            pltpu.SemaphoreType.DMA((2, chunks_of(slots))),
        ],
        cost_estimate=pl.CostEstimate(
            flops=4 * past_cache.size * heads, bytes_accessed=2 * past_cache.size, transcendentals=0
        ),
        compiler_params=PARAMS,
        name="attend",
    )(*[pltpu.with_memory_space_constraint(x, pltpu.HBM) for x in (queries, past_cache, lengths, adapter_index)])


def alive_lines(live_ref, slots):
    slot = lax.broadcasted_iota(jnp.int32, (slots, HEAD_DIM), 0)
    return (slot >= STAY) | (slot < live_ref[0])


def attention_kernel(slots, heads, live_ref, rows_ref, out_ref, alive_ref, flat):
    alive = alive_lines(live_ref, slots)
    alive_ref[...] = alive.astype(jnp.float32)
    flat[...] = rows_ref[: slots * heads, :].astype(jnp.float32)
    for head in range(heads):
        block = flat[pl.ds(head, slots, stride=heads), :]
        out_ref[:, head * HEAD_DIM : (head + 1) * HEAD_DIM] = jnp.where(alive, block, 0.0).astype(out_ref.dtype)


def attention_out(live, rows, slots, heads):
    return pl.pallas_call(
        functools.partial(attention_kernel, slots, heads),
        out_shape=(
            jax.ShapeDtypeStruct((slots, heads * HEAD_DIM), jnp.bfloat16),
            jax.ShapeDtypeStruct((slots, HEAD_DIM), jnp.float32),
        ),
        in_specs=[SMEM, VMEM],
        out_specs=(VMEM, VMEM),
        scratch_shapes=[pltpu.VMEM((slots * heads, HEAD_DIM), jnp.float32)],
        compiler_params=PARAMS,
        name="attention_out",
    )(live, rows)


def adapted_kernel(slots, heads, alive_ref, own_ref, *refs):
    rows_refs, out_ref, flat = refs[:-2], refs[-2], refs[-1]
    alive = alive_ref[...] > 0
    if rows_refs:
        total = rows_refs[0][...].astype(jnp.float32)
        for other in rows_refs[1:]:
            total += other[...].astype(jnp.float32)
        flat[...] = total
    for head in range(heads):
        block = own_ref[:, head * HEAD_DIM : (head + 1) * HEAD_DIM]
        if rows_refs:
            block += flat[pl.ds(head, slots, stride=heads), :]
        out_ref[:, head * HEAD_DIM : (head + 1) * HEAD_DIM] = jnp.where(alive, block, 0.0).astype(out_ref.dtype)


def adapted_out(alive, own, rows, slots, heads):
    return pl.pallas_call(
        functools.partial(adapted_kernel, slots, heads),
        out_shape=jax.ShapeDtypeStruct((slots, heads * HEAD_DIM), jnp.bfloat16),
        in_specs=[VMEM] * (2 + len(rows)),
        out_specs=VMEM,
        scratch_shapes=[pltpu.VMEM((slots * heads, HEAD_DIM), jnp.float32)],
        compiler_params=PARAMS,
        name="adapted_out",
    )(alive, own, *rows)


def first_adapter(holder, local_count):
    return (lax.axis_index("replica") ^ holder) * local_count


def lower_kernel(slots, heads, pad, sources, holders, before, *refs):
    down_refs, rows_refs = refs[:holders], refs[holders : holders + sources]
    partial_ref, index_ref, flat, wide = refs[-4:]
    local_count, rank, cols = down_refs[0].shape
    for source in range(sources):
        flat[source, : slots * heads, :] = rows_refs[source][: slots * heads, :].astype(jnp.float32)
        if pad > slots:
            flat[source, slots * heads :, :] = jnp.zeros(((pad - slots) * heads, HEAD_DIM), jnp.float32)
        digits = rows_refs[source][slots * heads :, :].astype(jnp.float32).astype(jnp.int32)
        index = (digits[0:1, :] << DIGIT) + digits[1:2, :]
        index_ref[:, source * pad : (source + 1) * pad] = index[:, :pad]
    for source in range(sources):
        for head in range(heads):
            wide[source * pad : (source + 1) * pad, head * HEAD_DIM : (head + 1) * HEAD_DIM] = flat[
                source, pl.ds(head, pad, stride=heads), :
            ].astype(jnp.bfloat16)
    total = jnp.zeros((rank, sources * pad), jnp.float32)
    for holder in range(holders):
        down = down_refs[holder][...].reshape(local_count * rank, cols)
        every = lax.dot_general(down, wide[...], (((1,), (1,)), ((), ())), preferred_element_type=jnp.float32)
        base = first_adapter(holder, local_count)
        for local in range(local_count):
            mine = index_ref[...] == base + local
            total += jnp.where(mine, every[local * rank : (local + 1) * rank, :], 0.0)
    if before:
        partial_ref[: before * rank, :] = refs[holders + sources][...]
    for source in range(sources):
        partial_ref[(before + source) * rank : (before + source + 1) * rank, :] = total[:, source * pad : (source + 1) * pad]


def lower(downs, rows, slots, heads, pad, name, cost, earlier=()):
    sources = len(rows)
    rank = downs[0].shape[1]
    before = sum(part.shape[0] // rank for part in earlier)
    return pl.pallas_call(
        functools.partial(lower_kernel, slots, heads, pad, sources, len(downs), before),
        out_shape=(
            jax.ShapeDtypeStruct(((before + sources) * rank, pad), jnp.float32),
            jax.ShapeDtypeStruct((1, sources * pad), jnp.int32),
        ),
        in_specs=[VMEM] * (len(downs) + sources + len(earlier)),
        out_specs=(VMEM, VMEM),
        scratch_shapes=[
            pltpu.VMEM((sources, pad * heads, HEAD_DIM), jnp.float32),
            pltpu.VMEM((sources * pad, heads * HEAD_DIM), jnp.bfloat16),
        ],
        cost_estimate=pl.CostEstimate(flops=cost, bytes_accessed=0, transcendentals=0),
        compiler_params=PARAMS,
        name=name,
    )(*downs, *rows, *earlier)


def spread_ranks(index, total, holders, local_count):
    total = SCALING * total
    high = total.astype(jnp.bfloat16).astype(jnp.float32)
    spread = []
    for part in (high, total - high):
        for holder in range(holders):
            for local in range(local_count):
                mine = index == first_adapter(holder, local_count) + local
                spread.append(jnp.where(mine, part, 0.0))
    return jnp.concatenate(spread, axis=0).astype(jnp.bfloat16)


def stack_ups(up_refs):
    local_count, rank, cols = up_refs[0].shape
    up = [up_ref[...].reshape(local_count * rank, cols) for up_ref in up_refs]
    return jnp.concatenate(up + up, axis=0)


def raise_kernel(slots, heads, pad, sources, holders, index_ref, *refs):
    up_refs, partials, outs, flat = refs[:holders], refs[holders : -sources - 1], refs[-sources - 1 : -1], refs[-1]
    local_count, rank, cols = up_refs[0].shape
    up = stack_ups(up_refs)
    for source in range(sources):
        lines = slice((1 + source) * rank, (2 + source) * rank)
        total = partials[0][lines, :]
        for other in partials[1:]:
            total += other[lines, :]
        spread = spread_ranks(index_ref[:, source * pad : (source + 1) * pad], total, holders, local_count)
        wide = lax.dot_general(spread, up, (((0,), (0,)), ((), ())), preferred_element_type=jnp.float32)
        for head in range(heads):
            flat[pl.ds(head, slots, stride=heads), :] = wide[:slots, head * HEAD_DIM : (head + 1) * HEAD_DIM]
        outs[source][...] = flat[...].astype(jnp.bfloat16)


def raise_rows(index, ups, partials, slots, heads, pad, sources):
    return pl.pallas_call(
        functools.partial(raise_kernel, slots, heads, pad, sources, len(ups)),
        out_shape=[jax.ShapeDtypeStruct((slots * heads, HEAD_DIM), jnp.bfloat16)] * sources,
        in_specs=[VMEM] * (1 + len(ups) + len(partials)),
        out_specs=[VMEM] * sources,
        scratch_shapes=[pltpu.VMEM((slots * heads, HEAD_DIM), jnp.float32)],
        compiler_params=PARAMS,
        name="raise_rows",
    )(index, *ups, *partials)


def raise_own_kernel(slots, holders, index_ref, *refs):
    up_refs, partials, out_ref = refs[:holders], refs[holders:-1], refs[-1]
    local_count, rank, cols = up_refs[0].shape
    total = partials[0][:rank, :]
    for other in partials[1:]:
        total += other[:rank, :]
    spread = spread_ranks(index_ref[...], total, holders, local_count)
    wide = lax.dot_general(spread, stack_ups(up_refs), (((0,), (0,)), ((), ())), preferred_element_type=jnp.float32)
    out_ref[...] = wide[:slots, :]


def raise_own(index, ups, partials, slots):
    return pl.pallas_call(
        functools.partial(raise_own_kernel, slots, len(ups)),
        out_shape=jax.ShapeDtypeStruct((slots, ups[0].shape[2]), jnp.float32),
        in_specs=[VMEM] * (1 + len(ups) + len(partials)),
        out_specs=VMEM,
        compiler_params=PARAMS,
        name="raise_own",
    )(index, *ups, *partials)


def shift(block, axis, offset):
    size = lax.axis_size(axis)
    return lax.ppermute(block, axis, [(i, (i + offset) % size) for i in range(size)])


def swap(block, axis):
    size = lax.axis_size(axis)
    return lax.ppermute(block, axis, [(i, i ^ 1) for i in range(size)])


def on_device(queries, past_cache, lengths, live_counts, adapter_index, adapter_down, adapter_up):
    slots, cols = queries.shape
    heads = cols // HEAD_DIM
    replicas = lax.axis_size("replica")
    tensor = lax.axis_size("tensor")
    holders = 2 if replicas % 2 == 0 else 1
    sources = replicas // holders
    pad = 16
    while pad < slots:
        pad *= 2
    downs = [adapter_down] + [swap(adapter_down, "replica") for _ in range(1, holders)]
    rows = attend(queries, past_cache, lengths, adapter_index)
    gathered = [shift(rows, "replica", holders * k) for k in range(1, sources)]
    attention, alive = attention_out(live_counts, rows, slots, heads)
    own_partial, own_index = lower(downs, [rows], slots, heads, pad, "lower_own", 10**6)
    later_up = lax.optimization_barrier((adapter_up, alive))[0]
    ups = [adapter_up] + [swap(later_up, "replica") for _ in range(1, holders)]
    partial, index = lower(downs, gathered, slots, heads, pad, "lower", 2 * 10**10, [own_partial])
    partials = [partial] + [shift(partial, "tensor", k) for k in range(1, tensor)]
    widened = raise_rows(index, ups, partials, slots, heads, pad, sources - 1)
    returned = [shift(widened[k - 1], "replica", -holders * k) for k in range(1, sources)]
    own = raise_own(own_index, ups, partials, slots)
    adapted = adapted_out(alive, own, returned, slots, heads)
    return (attention, adapted)


def solution(mesh):
    in_specs = (
        P(("groups", "replica"), "tensor"),
        P(None, ("groups", "replica"), None, "tensor"),
        P(("groups", "replica")),
        P(("groups", "replica")),
        P(("groups", "replica")),
        P("replica", None, "tensor"),
        P("replica", None, "tensor"),
    )
    out_specs = (P(("groups", "replica"), "tensor"), P(("groups", "replica"), "tensor"))
    return jax.shard_map(
        on_device, mesh=mesh, in_specs=in_specs, out_specs=out_specs, check_vma=False
    )
```

time: 37.7 us -> 25 us (0.66)
  waiting for transfers between devices: 11.3 us -> 6.59 us
  Pallas kernels: 8.66 us -> 5.82 us
  starting transfers between devices: 13.8 us -> 11.1 us
  local copies, waits for them, and re-layouts: 2.18 us -> 0.01 us
    ppermute x9 -> x5, waiting for transfers between devices: 11.3 us -> 4.57 us  [shift(): lax.ppermute(block, axis, [(i, (i + offset) % size) for i in range(size)])]
    ppermute x9 -> x5, starting transfers between devices: 13.8 us -> 7.55 us  [shift(): lax.ppermute(block, axis, [(i, (i + offset) % size) for i in range(size)])]
    ppermute x0 -> x2, starting transfers between devices: none -> 3.54 us  [swap(): return lax.ppermute(block, axis, [(i, i ^ 1) for i in range(size)])]
    unnamed x14 -> x4, local copies, waits for them, and re-layouts: 2.18 us -> 0.01 us
    ppermute x0 -> x2, waiting for transfers between devices: none -> 2.02 us  [swap(): return lax.ppermute(block, axis, [(i, i ^ 1) for i in range(size)])]
    pallas_call x2 -> x3, Pallas kernels: 3.32 us -> 1.74 us  [the longest x1 0.72 us: adapted_out(): pl.pallas_call(functools.partial(adapted_kernel, slots, heads), out_shape...]
    pallas_call x1, Pallas kernels: 4.24 us -> 3.05 us  [attend(): pl.pallas_call(attend_kernel, out_shape=jax.ShapeDtypeStruct((slots * hea...]
  transfers between devices with their start and end apart: 9 -> 7, of which waited for: 8 -> 3; matrix products, arithmetic and copies ran while one was open for 0% -> 0% of each run, Pallas kernels for 4% -> 19%
where the time goes in v2:
time: 25 us; the launch traced here: 24.9 us
  starting transfers between devices  11.1 us (44%)
  waiting for transfers between devices  6.59 us (26%)
  Pallas kernels  5.82 us (23%)
  between operations  1.34 us (5%)
    ppermute x5, starting transfers between devices, shift(): lax.ppermute(block, axis, [(i, (i + offset) % size) for i in range(size)])  7.55 us
    ppermute x5, waiting for transfers between devices, shift(): lax.ppermute(block, axis, [(i, (i + offset) % size) for i in range(size)])  4.57 us
    ppermute x2, starting transfers between devices, swap(): return lax.ppermute(block, axis, [(i, i ^ 1) for i in range(size)])  3.54 us
    pallas_call x1, Pallas kernels, attend(): pl.pallas_call(attend_kernel, out_shape=jax.ShapeDtypeStruct((slots * hea...  3.05 us
    ppermute x2, waiting for transfers between devices, swap(): return lax.ppermute(block, axis, [(i, i ^ 1) for i in range(size)])  2.02 us
    pallas_call x1, Pallas kernels, adapted_out(): pl.pallas_call(functools.partial(adapted_kernel, slots, heads), out_shape...  0.72 us
    pallas_call x1, Pallas kernels, attention_out(): pl.pallas_call(functools.partial(attention_kernel, slots, heads), out_sha...  0.71 us
    pallas_call x2, Pallas kernels, lower(): pl.pallas_call(functools.partial(lower_kernel, slots, heads, pad, sources...  0.69 us
  transfers between devices with their start and end apart: 7, of which 3 were waited for; matrix products, arithmetic and copies ran while one was open for 0% of the time, Pallas kernels for 19%

profile of v2, /device:TPU:0, one launch (start us, length us, event | category | flops | bytes accessed | tf_op | source)
XLA Modules:
  0.0 24.9 jit_solution(13207943693381364601)
XLA Ops:
  0.6 0.0 copy-start.1
  0.6 0.0 copy-start
  0.7 3.1 %collective-permute-start = (bf16[4,16,2048]{2,1,0:T(8,128)(2,1)}, bf16[4,16,2048]{2,1,0:T(8,128)(2,1)S(1)}, u32[]{:S(2)}, u32[]{:S(2)}) collective-permute-start(bf16[4,16,2048]{2,1,0:T(8,128)(2,1)} %refs_0_.5), channel_id=1, source_target_pairs={{0,4},{4,0},{8,12},{12,8},{1,5},{5,1},{9,13},{13,9},{2,6},{6,2},{1... | collective-permute-start | bytes 786440 | tf_op jit(solution)/shard_map/ppermute | solution.py:304
  3.7 3.1 %attend.1.rows_ref.refs_2_ = bf16[304,128]{1,0:T(8,128)(2,1)S(1)} custom-call(bf16[18,2048]{1,0:T(8,128)(2,1)} %q_ref.1, bf16[2,18,128,256]{3,2,1,0:T(8,128)(2,1)} %cache_ref.1, s32[18]{0:T(128)} %lengths_ref.1, s32[18]{0:T(128)} %index_ref.1), custom_call_target="tpu_custom_call" | custom-call | flops 75497472 | bytes 2359296 | tf_op jit(solution)/shard_map/attend/pallas_call | solution.py:93
  6.8 2.7 %collective-permute-start.2 = (bf16[304,128]{1,0:T(8,128)(2,1)S(1)}, bf16[304,128]{1,0:T(8,128)(2,1)S(1)}, u32[]{:S(2)}, u32[]{:S(2)}) collective-permute-start(bf16[304,128]{1,0:T(8,128)(2,1)S(1)} %attend.1.rows_ref.refs_2_), channel_id=1, source_target_pairs={{0,8},{4,12},{8,0},{12,4},{1,9},{5,13},{9,1},{13,5},{2,10},{6,14},... | collective-permute-start | bytes 233480 | tf_op jit(solution)/shard_map/ppermute | solution.py:299
  10.1 0.7 %attention_out.1 = (bf16[18,2048]{1,0:T(8,128)(2,1)}, f32[18,128]{1,0:T(8,128)S(1)}) custom-call(s32[1]{0:T(128)S(6)} %copy.9.live_ref, bf16[304,128]{1,0:T(8,128)(2,1)S(1)} %attend.1.rows_ref.refs_2_), custom_call_target="tpu_custom_call" | custom-call | tf_op jit(solution)/shard_map/attention_out/pallas_call | solution.py:132
  10.8 0.0 copy-done
  10.8 0.4 %collective-permute-start.1 = (bf16[4,16,2048]{2,1,0:T(8,128)(2,1)S(1)}, bf16[4,16,2048]{2,1,0:T(8,128)(2,1)S(1)}, u32[]{:S(2)}, u32[]{:S(2)}) collective-permute-start(bf16[4,16,2048]{2,1,0:T(8,128)(2,1)S(1)} %copy-done), channel_id=1, source_target_pairs={{0,4},{4,0},{8,12},{12,8},{1,5},{5,1},{9,13},{13,9},{2,6},{6,2},{1... | collective-permute-start | bytes 786440 | tf_op jit(solution)/shard_map/ppermute | solution.py:304
  11.3 0.0 collective-permute-done.refs_1_
  11.3 0.0 copy-done.1
  11.3 0.3 %lower_own.1 = (f32[16,32]{1,0:T(8,128)S(1)}, s32[1,32]{1,0:T(1,128)S(1)}) custom-call(bf16[4,16,2048]{2,1,0:T(8,128)(2,1)S(1)} %copy-done.1, bf16[4,16,2048]{2,1,0:T(8,128)(2,1)S(1)} %collective-permute-done.refs_1_, bf16[304,128]{1,0:T(8,128)(2,1)S(1)} %attend.1.rows_ref.refs_2_), custom_call_target="tpu_custom_call" | custom-call | flops 1000000 | tf_op jit(solution)/shard_map/lower_own/pallas_call | solution.py:211
  11.6 1.5 %collective-permute-done.2.refs_2_ = bf16[304,128]{1,0:T(8,128)(2,1)S(1)} collective-permute-done((bf16[304,128]{1,0:T(8,128)(2,1)S(1)}, bf16[304,128]{1,0:T(8,128)(2,1)S(1)}, u32[]{:S(2)}, u32[]{:S(2)}) %collective-permute-start.2) | collective-permute-done | bytes 77856 | tf_op jit(solution)/shard_map/ppermute | solution.py:299
  13.1 0.3 %lower.1 = (f32[32,32]{1,0:T(8,128)S(1)}, s32[1,32]{1,0:T(1,128)S(1)}) custom-call(bf16[4,16,2048]{2,1,0:T(8,128)(2,1)S(1)} %copy-done.1, bf16[4,16,2048]{2,1,0:T(8,128)(2,1)S(1)} %collective-permute-done.refs_1_, bf16[304,128]{1,0:T(8,128)(2,1)S(1)} %collective-permute-done.2.refs_2_, f32[16,32]{1,0:T(8,128)S(1)} %get-tuple-element.13.refs_3_), custom_call_target="tpu_custom_call" | custom-call | flops 20000000000 | tf_op jit(solution)/shard_map/lower/pallas_call | solution.py:211
  13.4 0.1 collective-permute-start.3
  13.5 1.6 %collective-permute-start.4 = (f32[32,32]{1,0:T(8,128)S(1)}, f32[32,32]{1,0:T(8,128)S(1)}, u32[]{:S(2)}, u32[]{:S(2)}) collective-permute-start(f32[32,32]{1,0:T(8,128)S(1)} %get-tuple-element.14.refs_2_), channel_id=1, source_target_pairs={{0,2},{1,3},{2,0},{3,1},{4,6},{5,7},{6,4},{7,5},{8,10},{9,11},{10,... | collective-permute-start | bytes 12296 | tf_op jit(solution)/shard_map/ppermute | solution.py:299
  15.1 1.4 %collective-permute-start.5 = (f32[32,32]{1,0:T(8,128)S(1)}, f32[32,32]{1,0:T(8,128)S(1)}, u32[]{:S(2)}, u32[]{:S(2)}) collective-permute-start(f32[32,32]{1,0:T(8,128)S(1)} %get-tuple-element.14.refs_2_), channel_id=1, source_target_pairs={{0,3},{1,0},{2,1},{3,2},{4,7},{5,4},{6,5},{7,6},{8,11},{9,8},{10,9... | collective-permute-start | bytes 12296 | tf_op jit(solution)/shard_map/ppermute | solution.py:299
  16.4 2.0 %collective-permute-done.1.refs_1_ = bf16[4,16,2048]{2,1,0:T(8,128)(2,1)S(1)} collective-permute-done((bf16[4,16,2048]{2,1,0:T(8,128)(2,1)S(1)}, bf16[4,16,2048]{2,1,0:T(8,128)(2,1)S(1)}, u32[]{:S(2)}, u32[]{:S(2)}) %collective-permute-start.1) | collective-permute-done | bytes 262176 | tf_op jit(solution)/shard_map/ppermute | solution.py:304
  18.5 0.0 collective-permute-done.3.refs_3_
  18.5 0.0 collective-permute-done.4.refs_4_
  18.5 0.0 collective-permute-done.5.refs_5_
  18.5 0.3 %raise_rows.1 = bf16[288,128]{1,0:T(8,128)(2,1)S(1)} custom-call(s32[1,32]{1,0:T(1,128)S(1)} %get-tuple-element.15.index_ref, bf16[4,16,2048]{2,1,0:T(8,128)(2,1)S(1)} %copy-done, bf16[4,16,2048]{2,1,0:T(8,128)(2,1)S(1)} %collective-permute-done.1.refs_1_, f32[32,32]{1,0:T(8,128)S(1)} %get-tuple-element.14.refs_2_, ...), custom_call_target="tpu_custom_call" | custom-call | tf_op jit(solution)/shard_map/raise_rows/pallas_call | solution.py:264
  18.8 1.9 %collective-permute-start.6 = (bf16[288,128]{1,0:T(8,128)(2,1)S(1)}, bf16[288,128]{1,0:T(8,128)(2,1)S(1)}, u32[]{:S(2)}, u32[]{:S(2)}) collective-permute-start(bf16[288,128]{1,0:T(8,128)(2,1)S(1)} %raise_rows.1), channel_id=1, source_target_pairs={{0,8},{4,12},{8,0},{12,4},{1,9},{5,13},{9,1},{13,5},{2,10},{6,14},... | collective-permute-start | bytes 221192 | tf_op jit(solution)/shard_map/ppermute | solution.py:299
  20.7 0.3 %raise_own.1.own_ref = f32[18,2048]{1,0:T(8,128)S(1)} custom-call(s32[1,32]{1,0:T(1,128)S(1)} %get-tuple-element.11.index_ref, bf16[4,16,2048]{2,1,0:T(8,128)(2,1)S(1)} %copy-done, bf16[4,16,2048]{2,1,0:T(8,128)(2,1)S(1)} %collective-permute-done.1.refs_1_, f32[32,32]{1,0:T(8,128)S(1)} %get-tuple-element.14.refs_2_, ...), custom_call_target="tpu_custom_call" | custom-call | tf_op jit(solution)/shard_map/raise_own/pallas_call | solution.py:287
  21.0 3.1 %collective-permute-done.6.refs_0_ = bf16[288,128]{1,0:T(8,128)(2,1)S(1)} collective-permute-done((bf16[288,128]{1,0:T(8,128)(2,1)S(1)}, bf16[288,128]{1,0:T(8,128)(2,1)S(1)}, u32[]{:S(2)}, u32[]{:S(2)}) %collective-permute-start.6) | collective-permute-done | bytes 73760 | tf_op jit(solution)/shard_map/ppermute | solution.py:299
  24.1 0.7 %adapted_out.1 = bf16[18,2048]{1,0:T(8,128)(2,1)} custom-call(f32[18,128]{1,0:T(8,128)S(1)} %get-tuple-element.10.alive_ref, f32[18,2048]{1,0:T(8,128)S(1)} %raise_own.1.own_ref, bf16[288,128]{1,0:T(8,128)(2,1)S(1)} %collective-permute-done.6.refs_0_), custom_call_target="tpu_custom_call" | custom-call | tf_op jit(solution)/shard_map/adapted_out/pallas_call | solution.py:162
Async XLA Ops:
  0.6 10.6 %copy-start.1 = (bf16[4,16,2048]{2,1,0:T(8,128)(2,1)S(1)}, bf16[4,16,2048]{2,1,0:T(8,128)(2,1)}, u32[]{:S(2)}) copy-start(bf16[4,16,2048]{2,1,0:T(8,128)(2,1)} %refs_0_.5) | copy-start | bytes 786436
  0.6 10.2 %copy-start = (bf16[4,16,2048]{2,1,0:T(8,128)(2,1)S(1)}, bf16[4,16,2048]{2,1,0:T(8,128)(2,1)}, u32[]{:S(2)}) copy-start(bf16[4,16,2048]{2,1,0:T(8,128)(2,1)} %refs_0_.7) | copy-start | bytes 786436
  0.7 10.6 %collective-permute-start = (bf16[4,16,2048]{2,1,0:T(8,128)(2,1)}, bf16[4,16,2048]{2,1,0:T(8,128)(2,1)S(1)}, u32[]{:S(2)}, u32[]{:S(2)}) collective-permute-start(bf16[4,16,2048]{2,1,0:T(8,128)(2,1)} %refs_0_.5), channel_id=1, source_target_pairs={{0,4},{4,0},{8,12},{12,8},{1,5},{5,1},{9,13},{13,9},{2,6},{6,2},{1... | collective-permute-start | bytes 786440 | tf_op jit(solution)/shard_map/ppermute | solution.py:304
  6.8 6.3 %collective-permute-start.2 = (bf16[304,128]{1,0:T(8,128)(2,1)S(1)}, bf16[304,128]{1,0:T(8,128)(2,1)S(1)}, u32[]{:S(2)}, u32[]{:S(2)}) collective-permute-start(bf16[304,128]{1,0:T(8,128)(2,1)S(1)} %attend.1.rows_ref.refs_2_), channel_id=1, source_target_pairs={{0,8},{4,12},{8,0},{12,4},{1,9},{5,13},{9,1},{13,5},{2,10},{6,14},... | collective-permute-start | bytes 233480 | tf_op jit(solution)/shard_map/ppermute | solution.py:299
  10.8 7.6 %collective-permute-start.1 = (bf16[4,16,2048]{2,1,0:T(8,128)(2,1)S(1)}, bf16[4,16,2048]{2,1,0:T(8,128)(2,1)S(1)}, u32[]{:S(2)}, u32[]{:S(2)}) collective-permute-start(bf16[4,16,2048]{2,1,0:T(8,128)(2,1)S(1)} %copy-done), channel_id=1, source_target_pairs={{0,4},{4,0},{8,12},{12,8},{1,5},{5,1},{9,13},{13,9},{2,6},{6,2},{1... | collective-permute-start | bytes 786440 | tf_op jit(solution)/shard_map/ppermute | solution.py:304
  13.4 5.0 %collective-permute-start.3 = (f32[32,32]{1,0:T(8,128)S(1)}, f32[32,32]{1,0:T(8,128)S(1)}, u32[]{:S(2)}, u32[]{:S(2)}) collective-permute-start(f32[32,32]{1,0:T(8,128)S(1)} %get-tuple-element.14.refs_2_), channel_id=1, source_target_pairs={{0,1},{1,2},{2,3},{3,0},{4,5},{5,6},{6,7},{7,4},{8,9},{9,10},{10,1... | collective-permute-start | bytes 12296 | tf_op jit(solution)/shard_map/ppermute | solution.py:299
  13.5 5.0 %collective-permute-start.4 = (f32[32,32]{1,0:T(8,128)S(1)}, f32[32,32]{1,0:T(8,128)S(1)}, u32[]{:S(2)}, u32[]{:S(2)}) collective-permute-start(f32[32,32]{1,0:T(8,128)S(1)} %get-tuple-element.14.refs_2_), channel_id=1, source_target_pairs={{0,2},{1,3},{2,0},{3,1},{4,6},{5,7},{6,4},{7,5},{8,10},{9,11},{10,... | collective-permute-start | bytes 12296 | tf_op jit(solution)/shard_map/ppermute | solution.py:299
  15.1 3.4 %collective-permute-start.5 = (f32[32,32]{1,0:T(8,128)S(1)}, f32[32,32]{1,0:T(8,128)S(1)}, u32[]{:S(2)}, u32[]{:S(2)}) collective-permute-start(f32[32,32]{1,0:T(8,128)S(1)} %get-tuple-element.14.refs_2_), channel_id=1, source_target_pairs={{0,3},{1,0},{2,1},{3,2},{4,7},{5,4},{6,5},{7,6},{8,11},{9,8},{10,9... | collective-permute-start | bytes 12296 | tf_op jit(solution)/shard_map/ppermute | solution.py:299
  18.8 5.3 %collective-permute-start.6 = (bf16[288,128]{1,0:T(8,128)(2,1)S(1)}, bf16[288,128]{1,0:T(8,128)(2,1)S(1)}, u32[]{:S(2)}, u32[]{:S(2)}) collective-permute-start(bf16[288,128]{1,0:T(8,128)(2,1)S(1)} %raise_rows.1), channel_id=1, source_target_pairs={{0,8},{4,12},{8,0},{12,4},{1,9},{5,13},{9,1},{13,5},{2,10},{6,14},... | collective-permute-start | bytes 221192 | tf_op jit(solution)/shard_map/ppermute | solution.py:299

commit v3 on v2

--- a/solution.py
+++ b/solution.py
@@ -18,13 +18,6 @@
 SMEM = pl.BlockSpec(memory_space=pltpu.SMEM)
 HBM = pl.BlockSpec(memory_space=pltpu.HBM)
 PARAMS = pltpu.CompilerParams(vmem_limit_bytes=16 * 2**20)
-
-
-def chunks_of(slots):
-    for parts in (3, 4, 2):
-        if slots % parts == 0:
-            return parts
-    return 1
 
 
 def attend_kernel(
@@ -36,18 +29,14 @@
     context, width = keys.shape[1:]
     key_heads = width // HEAD_DIM
     group = heads // key_heads
-    parts = chunks_of(slots)
-    step = slots // parts
     fetches = []
     for number, (source, target) in enumerate(((q_ref, q_flat), (lengths_ref, lengths), (index_ref, index))):
         fetches.append(pltpu.make_async_copy(source, target, small.at[number]))
         fetches[-1].start()
     copies = []
     for side, buffer in enumerate((keys, values)):
-        for part in range(parts):
-            span = pl.ds(part * step, step)
-            copies.append(pltpu.make_async_copy(cache_ref.at[side, span], buffer.at[span], large.at[side, part]))
-            copies[-1].start()
+        copies.append(pltpu.make_async_copy(cache_ref.at[side], buffer, large.at[side]))
+        copies[-1].start()
     for fetch in fetches:
         fetch.wait()
     for head in range(heads):
@@ -56,9 +45,8 @@
     owner = lax.broadcasted_iota(jnp.int32, (heads, HEAD_DIM), 0) // group
     position = lax.broadcasted_iota(jnp.int32, (heads, context), 1)
     weights = []
+    copies[0].wait()
     for slot in range(slots):
-        if slot % step == 0:
-            copies[slot // step].wait()
         rows = q_rows[slot * heads : (slot + 1) * heads, :]
         wide = [jnp.where(owner == k, rows, 0.0) for k in range(key_heads)]
         wide = jnp.concatenate(wide, axis=1).astype(jnp.bfloat16)
@@ -68,9 +56,8 @@
         scores = jnp.where(position < lengths[slot], scores, -jnp.inf)
         raised = jnp.exp(scores - jnp.max(scores, axis=-1, keepdims=True))
         weights.append((raised / jnp.sum(raised, axis=-1, keepdims=True)).astype(jnp.bfloat16))
+    copies[1].wait()
     for slot in range(slots):
-        if slot % step == 0:
-            copies[parts + slot // step].wait()
         mixed = jnp.dot(weights[slot], values[slot], preferred_element_type=jnp.float32)
         rows = mixed[:, :HEAD_DIM]
         for k in range(1, key_heads):
@@ -104,7 +91,7 @@
             pltpu.VMEM((slots * heads, HEAD_DIM), jnp.float32),
             pltpu.VMEM((slots * heads, HEAD_DIM), jnp.float32),
             pltpu.SemaphoreType.DMA((3,)),
-            pltpu.SemaphoreType.DMA((2, chunks_of(slots))),
+            pltpu.SemaphoreType.DMA((2,)),
         ],
         cost_estimate=pl.CostEstimate(
             flops=4 * past_cache.size * heads, bytes_accessed=2 * past_cache.size, transcendentals=0
@@ -174,95 +161,130 @@
     return (lax.axis_index("replica") ^ holder) * local_count
 
 
-def lower_kernel(slots, heads, pad, sources, holders, before, *refs):
-    down_refs, rows_refs = refs[:holders], refs[holders : holders + sources]
+def unfold_rows(rows_ref, slots, heads, pad, flat, wide_ref, first):
+    flat[: slots * heads, :] = rows_ref[: slots * heads, :].astype(jnp.float32)
+    if pad > slots:
+        flat[slots * heads :, :] = jnp.zeros(((pad - slots) * heads, HEAD_DIM), jnp.float32)
+    for head in range(heads):
+        wide_ref[first : first + pad, head * HEAD_DIM : (head + 1) * HEAD_DIM] = flat[
+            pl.ds(head, pad, stride=heads), :
+        ].astype(jnp.bfloat16)
+    digits = rows_ref[slots * heads :, :].astype(jnp.float32).astype(jnp.int32)
+    return ((digits[0:1, :] << DIGIT) + digits[1:2, :])[:, :pad]
+
+
+def rank_rows(down_ref, holder, wide, named):
+    local_count, rank, cols = down_ref.shape
+    down = down_ref[...].reshape(local_count * rank, cols)
+    every = lax.dot_general(down, wide, (((1,), (1,)), ((), ())), preferred_element_type=jnp.float32)
+    base = first_adapter(holder, local_count)
+    total = jnp.zeros((rank, named.shape[1]), jnp.float32)
+    for local in range(local_count):
+        total += jnp.where(named == base + local, every[local * rank : (local + 1) * rank, :], 0.0)
+    return total
+
+
+def lower_own_kernel(slots, heads, pad, down_ref, rows_ref, partial_ref, index_ref, wide_ref, flat):
+    named = unfold_rows(rows_ref, slots, heads, pad, flat, wide_ref, 0)
+    index_ref[...] = named
+    partial_ref[...] = rank_rows(down_ref, 0, wide_ref[...], named)
+
+
+def lower_own(down, rows, slots, heads, pad):
+    rank = down.shape[1]
+    return pl.pallas_call(
+        functools.partial(lower_own_kernel, slots, heads, pad),
+        out_shape=(
+            jax.ShapeDtypeStruct((rank, pad), jnp.float32),
+            jax.ShapeDtypeStruct((1, pad), jnp.int32),
+            jax.ShapeDtypeStruct((pad, heads * HEAD_DIM), jnp.bfloat16),
+        ),
+        in_specs=[VMEM] * 2,
+        out_specs=[VMEM] * 3,
+        scratch_shapes=[pltpu.VMEM((pad * heads, HEAD_DIM), jnp.float32)],
+        compiler_params=PARAMS,
+        name="lower_own",
+    )(down, rows)
+
+
+def lower_kernel(slots, heads, pad, sources, holders, *refs):
+    own_partial, own_index, own_wide = refs[:3]
+    down_refs, rows_refs = refs[3 : 3 + holders], refs[3 + holders : 3 + holders + sources]
     partial_ref, index_ref, flat, wide = refs[-4:]
-    local_count, rank, cols = down_refs[0].shape
+    rank = down_refs[0].shape[1]
+    named = [own_index[...]]
     for source in range(sources):
-        flat[source, : slots * heads, :] = rows_refs[source][: slots * heads, :].astype(jnp.float32)
-        if pad > slots:
-            flat[source, slots * heads :, :] = jnp.zeros(((pad - slots) * heads, HEAD_DIM), jnp.float32)
-        digits = rows_refs[source][slots * heads :, :].astype(jnp.float32).astype(jnp.int32)
-        index = (digits[0:1, :] << DIGIT) + digits[1:2, :]
-        index_ref[:, source * pad : (source + 1) * pad] = index[:, :pad]
+        named.append(unfold_rows(rows_refs[source], slots, heads, pad, flat, wide, source * pad))
+    for block in range(sources + 1):
+        index_ref[block : block + 1, :] = named[block]
+    total = own_partial[...]
+    for holder in range(1, holders):
+        total += rank_rows(down_refs[holder], holder, own_wide[...], named[0])
+    totals = [total]
     for source in range(sources):
-        for head in range(heads):
-            wide[source * pad : (source + 1) * pad, head * HEAD_DIM : (head + 1) * HEAD_DIM] = flat[
-                source, pl.ds(head, pad, stride=heads), :
-            ].astype(jnp.bfloat16)
-    total = jnp.zeros((rank, sources * pad), jnp.float32)
-    for holder in range(holders):
-        down = down_refs[holder][...].reshape(local_count * rank, cols)
-        every = lax.dot_general(down, wide[...], (((1,), (1,)), ((), ())), preferred_element_type=jnp.float32)
-        base = first_adapter(holder, local_count)
-        for local in range(local_count):
-            mine = index_ref[...] == base + local
-            total += jnp.where(mine, every[local * rank : (local + 1) * rank, :], 0.0)
-    if before:
-        partial_ref[: before * rank, :] = refs[holders + sources][...]
-    for source in range(sources):
-        partial_ref[(before + source) * rank : (before + source + 1) * rank, :] = total[:, source * pad : (source + 1) * pad]
-
-
-def lower(downs, rows, slots, heads, pad, name, cost, earlier=()):
+        total = jnp.zeros((rank, pad), jnp.float32)
+        for holder in range(holders):
+            total += rank_rows(down_refs[holder], holder, wide[source * pad : (source + 1) * pad, :], named[1 + source])
+        totals.append(total)
+    partial_ref[...] = jnp.concatenate(totals[1:] + totals[:1], axis=1)
+
+def lower(own, downs, rows, slots, heads, pad):
     sources = len(rows)
     rank = downs[0].shape[1]
-    before = sum(part.shape[0] // rank for part in earlier)
-    return pl.pallas_call(
-        functools.partial(lower_kernel, slots, heads, pad, sources, len(downs), before),
+    return pl.pallas_call(
+        functools.partial(lower_kernel, slots, heads, pad, sources, len(downs)),
         out_shape=(
-            jax.ShapeDtypeStruct(((before + sources) * rank, pad), jnp.float32),
-            jax.ShapeDtypeStruct((1, sources * pad), jnp.int32),
+            jax.ShapeDtypeStruct((rank, (1 + sources) * pad), jnp.float32),
+            jax.ShapeDtypeStruct((1 + sources, pad), jnp.int32),
         ),
-        in_specs=[VMEM] * (len(downs) + sources + len(earlier)),
-        out_specs=(VMEM, VMEM),
+        in_specs=[VMEM] * (3 + len(downs) + sources),
+        out_specs=[VMEM] * 2,
         scratch_shapes=[
-            pltpu.VMEM((sources, pad * heads, HEAD_DIM), jnp.float32),
+            pltpu.VMEM((pad * heads, HEAD_DIM), jnp.float32),
             pltpu.VMEM((sources * pad, heads * HEAD_DIM), jnp.bfloat16),
         ],
-        cost_estimate=pl.CostEstimate(flops=cost, bytes_accessed=0, transcendentals=0),
-        compiler_params=PARAMS,
-        name=name,
-    )(*downs, *rows, *earlier)
+        cost_estimate=pl.CostEstimate(flops=2 * 10**10, bytes_accessed=0, transcendentals=0),
+        compiler_params=PARAMS,
+        name="lower",
+    )(*own, *downs, *rows)
 
 
 def spread_ranks(index, total, holders, local_count):
     total = SCALING * total
-    high = total.astype(jnp.bfloat16).astype(jnp.float32)
     spread = []
-    for part in (high, total - high):
-        for holder in range(holders):
-            for local in range(local_count):
-                mine = index == first_adapter(holder, local_count) + local
-                spread.append(jnp.where(mine, part, 0.0))
+    for holder in range(holders):
+        for local in range(local_count):
+            mine = index == first_adapter(holder, local_count) + local
+            spread.append(jnp.where(mine, total, 0.0))
     return jnp.concatenate(spread, axis=0).astype(jnp.bfloat16)
 
 
 def stack_ups(up_refs):
     local_count, rank, cols = up_refs[0].shape
     up = [up_ref[...].reshape(local_count * rank, cols) for up_ref in up_refs]
-    return jnp.concatenate(up + up, axis=0)
-
-
-def raise_kernel(slots, heads, pad, sources, holders, index_ref, *refs):
+    return jnp.concatenate(up, axis=0)
+
+
+def raise_kernel(slots, heads, sources, holders, index_ref, *refs):
     up_refs, partials, outs, flat = refs[:holders], refs[holders : -sources - 1], refs[-sources - 1 : -1], refs[-1]
     local_count, rank, cols = up_refs[0].shape
     up = stack_ups(up_refs)
+    packed = partials[0][...]
+    for other in partials[1:]:
+        packed += other[...]
+    pad = index_ref.shape[1]
     for source in range(sources):
-        lines = slice((1 + source) * rank, (2 + source) * rank)
-        total = partials[0][lines, :]
-        for other in partials[1:]:
-            total += other[lines, :]
-        spread = spread_ranks(index_ref[:, source * pad : (source + 1) * pad], total, holders, local_count)
+        total = packed[:, source * pad : (source + 1) * pad]
+        spread = spread_ranks(index_ref[1 + source : 2 + source, :], total, holders, local_count)
         wide = lax.dot_general(spread, up, (((0,), (0,)), ((), ())), preferred_element_type=jnp.float32)
         for head in range(heads):
             flat[pl.ds(head, slots, stride=heads), :] = wide[:slots, head * HEAD_DIM : (head + 1) * HEAD_DIM]
         outs[source][...] = flat[...].astype(jnp.bfloat16)
 
 
-def raise_rows(index, ups, partials, slots, heads, pad, sources):
-    return pl.pallas_call(
-        functools.partial(raise_kernel, slots, heads, pad, sources, len(ups)),
+def raise_rows(index, ups, partials, slots, heads, sources):
+    return pl.pallas_call(
+        functools.partial(raise_kernel, slots, heads, sources, len(ups)),
         out_shape=[jax.ShapeDtypeStruct((slots * heads, HEAD_DIM), jnp.bfloat16)] * sources,
         in_specs=[VMEM] * (1 + len(ups) + len(partials)),
         out_specs=[VMEM] * sources,
@@ -275,10 +297,11 @@
 def raise_own_kernel(slots, holders, index_ref, *refs):
     up_refs, partials, out_ref = refs[:holders], refs[holders:-1], refs[-1]
     local_count, rank, cols = up_refs[0].shape
-    total = partials[0][:rank, :]
+    packed = partials[0][...]
     for other in partials[1:]:
-        total += other[:rank, :]
-    spread = spread_ranks(index_ref[...], total, holders, local_count)
+        packed += other[...]
+    total = packed[:, packed.shape[1] - index_ref.shape[1] :]
+    spread = spread_ranks(index_ref[0:1, :], total, holders, local_count)
     wide = lax.dot_general(spread, stack_ups(up_refs), (((0,), (0,)), ((), ())), preferred_element_type=jnp.float32)
     out_ref[...] = wide[:slots, :]
 
@@ -299,16 +322,22 @@
     return lax.ppermute(block, axis, [(i, (i + offset) % size) for i in range(size)])
 
 
-def swap(block, axis):
+def swap(block, axis, bits=1):
     size = lax.axis_size(axis)
-    return lax.ppermute(block, axis, [(i, i ^ 1) for i in range(size)])
+    return lax.ppermute(block, axis, [(i, i ^ bits) for i in range(size)])
+
+
+def exchange(block, axis):
+    size = lax.axis_size(axis)
+    if size & (size - 1):
+        return [shift(block, axis, k) for k in range(1, size)]
+    return [swap(block, axis, k) for k in [*range(2, size), 1]]
 
 
 def on_device(queries, past_cache, lengths, live_counts, adapter_index, adapter_down, adapter_up):
     slots, cols = queries.shape
     heads = cols // HEAD_DIM
     replicas = lax.axis_size("replica")
-    tensor = lax.axis_size("tensor")
     holders = 2 if replicas % 2 == 0 else 1
     sources = replicas // holders
     pad = 16
@@ -318,14 +347,14 @@
     rows = attend(queries, past_cache, lengths, adapter_index)
     gathered = [shift(rows, "replica", holders * k) for k in range(1, sources)]
     attention, alive = attention_out(live_counts, rows, slots, heads)
-    own_partial, own_index = lower(downs, [rows], slots, heads, pad, "lower_own", 10**6)
-    later_up = lax.optimization_barrier((adapter_up, alive))[0]
+    own = lower_own(adapter_down, rows, slots, heads, pad)
+    later_up = lax.optimization_barrier((adapter_up, alive, own[0]))[0]
     ups = [adapter_up] + [swap(later_up, "replica") for _ in range(1, holders)]
-    partial, index = lower(downs, gathered, slots, heads, pad, "lower", 2 * 10**10, [own_partial])
-    partials = [partial] + [shift(partial, "tensor", k) for k in range(1, tensor)]
-    widened = raise_rows(index, ups, partials, slots, heads, pad, sources - 1)
+    partial, index = lower(own, downs, gathered, slots, heads, pad)
+    partials = [partial] + exchange(partial, "tensor")
+    widened = raise_rows(index, ups, partials, slots, heads, sources - 1)
     returned = [shift(widened[k - 1], "replica", -holders * k) for k in range(1, sources)]
-    own = raise_own(own_index, ups, partials, slots)
+    own = raise_own(index, ups, partials, slots)
     adapted = adapted_out(alive, own, returned, slots, heads)
     return (attention, adapted)
 

time: 25 us -> 24.3 us (0.972)
  Pallas kernels: 5.82 us -> 4.9 us
    ppermute x2 -> x5, starting transfers between devices: 3.54 us -> 5.74 us  [swap(): return lax.ppermute(block, axis, [(i, i ^ bits) for i in range(size)])]
    ppermute x5 -> x2, starting transfers between devices: 7.55 us -> 5.47 us  [shift(): lax.ppermute(block, axis, [(i, (i + offset) % size) for i in range(size)])]
    ppermute x2 -> x5, waiting for transfers between devices: 2.02 us -> 3.05 us  [swap(): return lax.ppermute(block, axis, [(i, i ^ bits) for i in range(size)])]
    ppermute x5 -> x2, waiting for transfers between devices: 4.57 us -> 3.62 us  [shift(): lax.ppermute(block, axis, [(i, (i + offset) % size) for i in range(size)])]
    pallas_call x1, Pallas kernels: 3.05 us -> 2.23 us  [attend(): pl.pallas_call(attend_kernel, out_shape=jax.ShapeDtypeStruct((slots * hea...]
    pallas_call x2 -> x1, Pallas kernels: 0.69 us -> 0.37 us  [lower(): pl.pallas_call(functools.partial(lower_kernel, slots, heads, pad, sources...]
    pallas_call x1 -> x2, Pallas kernels: 0.33 us -> 0.56 us  [the longest x1 0.29 us: lower_own(): pl.pallas_call(functools.partial(lower_own_kernel, slots, heads, pad), ou...]
  transfers between devices with their start and end apart: 7 -> 7, of which waited for: 3 -> 3; matrix products, arithmetic and copies ran while one was open for 0% -> 0% of each run, Pallas kernels for 19% -> 16%
where the time goes in v3:
time: 24.3 us; the launch traced here: 24.1 us
  starting transfers between devices  11.2 us (46%)
  waiting for transfers between devices  6.67 us (27%)
  Pallas kernels  4.9 us (20%)
  between operations  1.34 us (6%)
    ppermute x5, starting transfers between devices, swap(): return lax.ppermute(block, axis, [(i, i ^ bits) for i in range(size)])  5.74 us
    ppermute x2, starting transfers between devices, shift(): lax.ppermute(block, axis, [(i, (i + offset) % size) for i in range(size)])  5.47 us
    ppermute x2, waiting for transfers between devices, shift(): lax.ppermute(block, axis, [(i, (i + offset) % size) for i in range(size)])  3.62 us
    ppermute x5, waiting for transfers between devices, swap(): return lax.ppermute(block, axis, [(i, i ^ bits) for i in range(size)])  3.05 us
    pallas_call x1, Pallas kernels, attend(): pl.pallas_call(attend_kernel, out_shape=jax.ShapeDtypeStruct((slots * hea...  2.23 us
    pallas_call x1, Pallas kernels, adapted_out(): pl.pallas_call(functools.partial(adapted_kernel, slots, heads), out_shape...  0.72 us
    pallas_call x1, Pallas kernels, attention_out(): pl.pallas_call(functools.partial(attention_kernel, slots, heads), out_sha...  0.71 us
  transfers between devices with their start and end apart: 7, of which 3 were waited for; matrix products, arithmetic and copies ran while one was open for 0% of the time, Pallas kernels for 16%

profile of v3, /device:TPU:0, one launch (start us, length us, event | category | flops | bytes accessed | tf_op | source)
XLA Modules:
  0.0 24.1 jit_solution(1587085159325798431)
XLA Ops:
  0.6 0.0 copy-start.1
  0.6 0.0 copy-start
  0.7 3.1 %collective-permute-start = (bf16[4,16,2048]{2,1,0:T(8,128)(2,1)}, bf16[4,16,2048]{2,1,0:T(8,128)(2,1)S(1)}, u32[]{:S(2)}, u32[]{:S(2)}) collective-permute-start(bf16[4,16,2048]{2,1,0:T(8,128)(2,1)} %refs_3_.1), channel_id=1, source_target_pairs={{0,4},{4,0},{8,12},{12,8},{1,5},{5,1},{9,13},{13,9},{2,6},{6,2},{1... | collective-permute-start | bytes 786440 | tf_op jit(solution)/shard_map/ppermute | solution.py:327
  3.7 2.2 %attend.1.rows_ref = bf16[304,128]{1,0:T(8,128)(2,1)S(1)} custom-call(bf16[18,2048]{1,0:T(8,128)(2,1)} %q_ref.1, bf16[2,18,128,256]{3,2,1,0:T(8,128)(2,1)} %cache_ref.1, s32[18]{0:T(128)} %lengths_ref.1, s32[18]{0:T(128)} %index_ref.1), custom_call_target="tpu_custom_call" | custom-call | flops 75497472 | bytes 2359296 | tf_op jit(solution)/shard_map/attend/pallas_call | solution.py:80
  6.0 2.7 %collective-permute-start.1 = (bf16[304,128]{1,0:T(8,128)(2,1)S(1)}, bf16[304,128]{1,0:T(8,128)(2,1)S(1)}, u32[]{:S(2)}, u32[]{:S(2)}) collective-permute-start(bf16[304,128]{1,0:T(8,128)(2,1)S(1)} %attend.1.rows_ref), channel_id=1, source_target_pairs={{0,8},{4,12},{8,0},{12,4},{1,9},{5,13},{9,1},{13,5},{2,10},{6,14},... | collective-permute-start | bytes 233480 | tf_op jit(solution)/shard_map/ppermute | solution.py:322
  8.6 0.0 copy-done.1
  8.6 0.3 %lower_own.1 = (f32[16,32]{1,0:T(8,128)S(1)}, s32[1,32]{1,0:T(1,128)S(1)}, bf16[32,2048]{1,0:T(8,128)(2,1)S(1)}) custom-call(bf16[4,16,2048]{2,1,0:T(8,128)(2,1)S(1)} %copy-done.1, bf16[304,128]{1,0:T(8,128)(2,1)S(1)} %attend.1.rows_ref), custom_call_target="tpu_custom_call" | custom-call | tf_op jit(solution)/shard_map/lower_own/pallas_call | solution.py:195
  9.6 0.7 %attention_out.1 = (bf16[18,2048]{1,0:T(8,128)(2,1)}, f32[18,128]{1,0:T(8,128)S(1)}) custom-call(s32[1]{0:T(128)S(6)} %copy.9.live_ref, bf16[304,128]{1,0:T(8,128)(2,1)S(1)} %attend.1.rows_ref), custom_call_target="tpu_custom_call" | custom-call | tf_op jit(solution)/shard_map/attention_out/pallas_call | solution.py:119
  10.3 0.0 copy-done
  10.3 0.4 %collective-permute-start.2 = (bf16[4,16,2048]{2,1,0:T(8,128)(2,1)S(1)}, bf16[4,16,2048]{2,1,0:T(8,128)(2,1)S(1)}, u32[]{:S(2)}, u32[]{:S(2)}) collective-permute-start(bf16[4,16,2048]{2,1,0:T(8,128)(2,1)S(1)} %copy-done), channel_id=1, source_target_pairs={{0,4},{4,0},{8,12},{12,8},{1,5},{5,1},{9,13},{13,9},{2,6},{6,2},{1... | collective-permute-start | bytes 786440 | tf_op jit(solution)/shard_map/ppermute | solution.py:327
  10.8 1.4 %collective-permute-done.1.refs_5_ = bf16[304,128]{1,0:T(8,128)(2,1)S(1)} collective-permute-done((bf16[304,128]{1,0:T(8,128)(2,1)S(1)}, bf16[304,128]{1,0:T(8,128)(2,1)S(1)}, u32[]{:S(2)}, u32[]{:S(2)}) %collective-permute-start.1) | collective-permute-done | bytes 77856 | tf_op jit(solution)/shard_map/ppermute | solution.py:322
  12.2 0.0 collective-permute-done.refs_4_
  12.2 0.4 %lower.1 = (f32[16,64]{1,0:T(8,128)S(1)}, s32[2,32]{1,0:T(2,128)S(1)}) custom-call(f32[16,32]{1,0:T(8,128)S(1)} %get-tuple-element.12.refs_0_, s32[1,32]{1,0:T(1,128)S(1)} %get-tuple-element.13.refs_1_, bf16[32,2048]{1,0:T(8,128)(2,1)S(1)} %get-tuple-element.14.refs_2_, bf16[4,16,2048]{2,1,0:T(8,128)(2,1)S(1)} %copy-done.1, ...), custom_call_target="tpu_custom_call" | custom-call | flops 20000000000 | tf_op jit(solution)/shard_map/lower/pallas_call | solution.py:234
  12.5 1.6 %collective-permute-start.3 = (f32[16,64]{1,0:T(8,128)S(1)}, f32[16,64]{1,0:T(8,128)S(1)}, u32[]{:S(2)}, u32[]{:S(2)}) collective-permute-start(f32[16,64]{1,0:T(8,128)S(1)} %get-tuple-element.17.refs_2_), channel_id=1, source_target_pairs={{0,2},{1,3},{2,0},{3,1},{4,6},{5,7},{6,4},{7,5},{8,10},{9,11},{10,... | collective-permute-start | bytes 12296 | tf_op jit(solution)/shard_map/ppermute | solution.py:327
  14.1 0.0 collective-permute-start.4
  14.1 0.6 %collective-permute-start.5 = (f32[16,64]{1,0:T(8,128)S(1)}, f32[16,64]{1,0:T(8,128)S(1)}, u32[]{:S(2)}, u32[]{:S(2)}) collective-permute-start(f32[16,64]{1,0:T(8,128)S(1)} %get-tuple-element.17.refs_2_), channel_id=1, source_target_pairs={{0,1},{1,0},{2,3},{3,2},{4,5},{5,4},{6,7},{7,6},{8,9},{9,8},{10,11... | collective-permute-start | bytes 12296 | tf_op jit(solution)/shard_map/ppermute | solution.py:327
  14.7 3.0 %collective-permute-done.2.refs_1_ = bf16[4,16,2048]{2,1,0:T(8,128)(2,1)S(1)} collective-permute-done((bf16[4,16,2048]{2,1,0:T(8,128)(2,1)S(1)}, bf16[4,16,2048]{2,1,0:T(8,128)(2,1)S(1)}, u32[]{:S(2)}, u32[]{:S(2)}) %collective-permute-start.2) | collective-permute-done | bytes 262176 | tf_op jit(solution)/shard_map/ppermute | solution.py:327
  17.8 0.0 collective-permute-done.3.refs_3_
  17.8 0.0 collective-permute-done.4.refs_4_
  17.8 0.0 collective-permute-done.5.refs_5_
  17.8 0.3 %raise_rows.1 = bf16[288,128]{1,0:T(8,128)(2,1)S(1)} custom-call(s32[2,32]{1,0:T(2,128)S(1)} %get-tuple-element.15.index_ref, bf16[4,16,2048]{2,1,0:T(8,128)(2,1)S(1)} %copy-done, bf16[4,16,2048]{2,1,0:T(8,128)(2,1)S(1)} %collective-permute-done.2.refs_1_, f32[16,64]{1,0:T(8,128)S(1)} %get-tuple-element.17.refs_2_, ...), custom_call_target="tpu_custom_call" | custom-call | tf_op jit(solution)/shard_map/raise_rows/pallas_call | solution.py:286
  18.1 2.8 %collective-permute-start.6 = (bf16[288,128]{1,0:T(8,128)(2,1)S(1)}, bf16[288,128]{1,0:T(8,128)(2,1)S(1)}, u32[]{:S(2)}, u32[]{:S(2)}) collective-permute-start(bf16[288,128]{1,0:T(8,128)(2,1)S(1)} %raise_rows.1), channel_id=1, source_target_pairs={{0,8},{4,12},{8,0},{12,4},{1,9},{5,13},{9,1},{13,5},{2,10},{6,14},... | collective-permute-start | bytes 221192 | tf_op jit(solution)/shard_map/ppermute | solution.py:322
  20.9 0.3 %raise_own.1.own_ref = f32[18,2048]{1,0:T(8,128)S(1)} custom-call(s32[2,32]{1,0:T(2,128)S(1)} %get-tuple-element.15.index_ref, bf16[4,16,2048]{2,1,0:T(8,128)(2,1)S(1)} %copy-done, bf16[4,16,2048]{2,1,0:T(8,128)(2,1)S(1)} %collective-permute-done.2.refs_1_, f32[16,64]{1,0:T(8,128)S(1)} %get-tuple-element.17.refs_2_, ...), custom_call_target="tpu_custom_call" | custom-call | tf_op jit(solution)/shard_map/raise_own/pallas_call | solution.py:310
  21.2 2.2 %collective-permute-done.6.refs_0_ = bf16[288,128]{1,0:T(8,128)(2,1)S(1)} collective-permute-done((bf16[288,128]{1,0:T(8,128)(2,1)S(1)}, bf16[288,128]{1,0:T(8,128)(2,1)S(1)}, u32[]{:S(2)}, u32[]{:S(2)}) %collective-permute-start.6) | collective-permute-done | bytes 73760 | tf_op jit(solution)/shard_map/ppermute | solution.py:322
  23.4 0.7 %adapted_out.1 = bf16[18,2048]{1,0:T(8,128)(2,1)} custom-call(f32[18,128]{1,0:T(8,128)S(1)} %get-tuple-element.11.alive_ref, f32[18,2048]{1,0:T(8,128)S(1)} %raise_own.1.own_ref, bf16[288,128]{1,0:T(8,128)(2,1)S(1)} %collective-permute-done.6.refs_0_), custom_call_target="tpu_custom_call" | custom-call | tf_op jit(solution)/shard_map/adapted_out/pallas_call | solution.py:149
Async XLA Ops:
  0.6 8.0 %copy-start.1 = (bf16[4,16,2048]{2,1,0:T(8,128)(2,1)S(1)}, bf16[4,16,2048]{2,1,0:T(8,128)(2,1)}, u32[]{:S(2)}) copy-start(bf16[4,16,2048]{2,1,0:T(8,128)(2,1)} %refs_3_.1) | copy-start | bytes 786436
  0.6 9.7 %copy-start = (bf16[4,16,2048]{2,1,0:T(8,128)(2,1)S(1)}, bf16[4,16,2048]{2,1,0:T(8,128)(2,1)}, u32[]{:S(2)}) copy-start(bf16[4,16,2048]{2,1,0:T(8,128)(2,1)} %refs_0_.3) | copy-start | bytes 786436
  0.7 11.5 %collective-permute-start = (bf16[4,16,2048]{2,1,0:T(8,128)(2,1)}, bf16[4,16,2048]{2,1,0:T(8,128)(2,1)S(1)}, u32[]{:S(2)}, u32[]{:S(2)}) collective-permute-start(bf16[4,16,2048]{2,1,0:T(8,128)(2,1)} %refs_3_.1), channel_id=1, source_target_pairs={{0,4},{4,0},{8,12},{12,8},{1,5},{5,1},{9,13},{13,9},{2,6},{6,2},{1... | collective-permute-start | bytes 786440 | tf_op jit(solution)/shard_map/ppermute | solution.py:327
  6.0 6.2 %collective-permute-start.1 = (bf16[304,128]{1,0:T(8,128)(2,1)S(1)}, bf16[304,128]{1,0:T(8,128)(2,1)S(1)}, u32[]{:S(2)}, u32[]{:S(2)}) collective-permute-start(bf16[304,128]{1,0:T(8,128)(2,1)S(1)} %attend.1.rows_ref), channel_id=1, source_target_pairs={{0,8},{4,12},{8,0},{12,4},{1,9},{5,13},{9,1},{13,5},{2,10},{6,14},... | collective-permute-start | bytes 233480 | tf_op jit(solution)/shard_map/ppermute | solution.py:322
  10.3 7.5 %collective-permute-start.2 = (bf16[4,16,2048]{2,1,0:T(8,128)(2,1)S(1)}, bf16[4,16,2048]{2,1,0:T(8,128)(2,1)S(1)}, u32[]{:S(2)}, u32[]{:S(2)}) collective-permute-start(bf16[4,16,2048]{2,1,0:T(8,128)(2,1)S(1)} %copy-done), channel_id=1, source_target_pairs={{0,4},{4,0},{8,12},{12,8},{1,5},{5,1},{9,13},{13,9},{2,6},{6,2},{1... | collective-permute-start | bytes 786440 | tf_op jit(solution)/shard_map/ppermute | solution.py:327
  12.5 5.3 %collective-permute-start.3 = (f32[16,64]{1,0:T(8,128)S(1)}, f32[16,64]{1,0:T(8,128)S(1)}, u32[]{:S(2)}, u32[]{:S(2)}) collective-permute-start(f32[16,64]{1,0:T(8,128)S(1)} %get-tuple-element.17.refs_2_), channel_id=1, source_target_pairs={{0,2},{1,3},{2,0},{3,1},{4,6},{5,7},{6,4},{7,5},{8,10},{9,11},{10,... | collective-permute-start | bytes 12296 | tf_op jit(solution)/shard_map/ppermute | solution.py:327
  14.1 3.7 %collective-permute-start.4 = (f32[16,64]{1,0:T(8,128)S(1)}, f32[16,64]{1,0:T(8,128)S(1)}, u32[]{:S(2)}, u32[]{:S(2)}) collective-permute-start(f32[16,64]{1,0:T(8,128)S(1)} %get-tuple-element.17.refs_2_), channel_id=1, source_target_pairs={{0,3},{1,2},{2,1},{3,0},{4,7},{5,6},{6,5},{7,4},{8,11},{9,10},{10,... | collective-permute-start | bytes 12296 | tf_op jit(solution)/shard_map/ppermute | solution.py:327
  14.1 3.7 %collective-permute-start.5 = (f32[16,64]{1,0:T(8,128)S(1)}, f32[16,64]{1,0:T(8,128)S(1)}, u32[]{:S(2)}, u32[]{:S(2)}) collective-permute-start(f32[16,64]{1,0:T(8,128)S(1)} %get-tuple-element.17.refs_2_), channel_id=1, source_target_pairs={{0,1},{1,0},{2,3},{3,2},{4,5},{5,4},{6,7},{7,6},{8,9},{9,8},{10,11... | collective-permute-start | bytes 12296 | tf_op jit(solution)/shard_map/ppermute | solution.py:327
  18.1 5.3 %collective-permute-start.6 = (bf16[288,128]{1,0:T(8,128)(2,1)S(1)}, bf16[288,128]{1,0:T(8,128)(2,1)S(1)}, u32[]{:S(2)}, u32[]{:S(2)}) collective-permute-start(bf16[288,128]{1,0:T(8,128)(2,1)S(1)} %raise_rows.1), channel_id=1, source_target_pairs={{0,8},{4,12},{8,0},{12,4},{1,9},{5,13},{9,1},{13,5},{2,10},{6,14},... | collective-permute-start | bytes 221192 | tf_op jit(solution)/shard_map/ppermute | solution.py:322

commit v4 on v3

--- a/solution.py
+++ b/solution.py
@@ -331,7 +331,7 @@
     size = lax.axis_size(axis)
     if size & (size - 1):
         return [shift(block, axis, k) for k in range(1, size)]
-    return [swap(block, axis, k) for k in [*range(2, size), 1]]
+    return [swap(block, axis, k) for k in range(size - 1, 0, -1)]
 
 
 def on_device(queries, past_cache, lengths, live_counts, adapter_index, adapter_down, adapter_up):

time: 24.3 us -> 24.3 us (level)
  waiting for transfers between devices: 6.67 us -> 7.19 us
  starting transfers between devices: 11.2 us -> 10.7 us
    ppermute x5, starting transfers between devices: 5.74 us -> 5.46 us  [swap(): return lax.ppermute(block, axis, [(i, i ^ bits) for i in range(size)])]
    ppermute x5, waiting for transfers between devices: 3.05 us -> 3.33 us  [swap(): return lax.ppermute(block, axis, [(i, i ^ bits) for i in range(size)])]
    ppermute x2, starting transfers between devices: 5.47 us -> 5.22 us  [shift(): lax.ppermute(block, axis, [(i, (i + offset) % size) for i in range(size)])]
where the time goes in v4:
time: 24.3 us; the launch traced here: 24.1 us
  starting transfers between devices  10.7 us (44%)
  waiting for transfers between devices  7.19 us (30%)
  Pallas kernels  4.9 us (20%)
  between operations  1.34 us (6%)
    ppermute x5, starting transfers between devices, swap(): return lax.ppermute(block, axis, [(i, i ^ bits) for i in range(size)])  5.46 us
    ppermute x2, starting transfers between devices, shift(): lax.ppermute(block, axis, [(i, (i + offset) % size) for i in range(size)])  5.22 us
    ppermute x2, waiting for transfers between devices, shift(): lax.ppermute(block, axis, [(i, (i + offset) % size) for i in range(size)])  3.85 us
    ppermute x5, waiting for transfers between devices, swap(): return lax.ppermute(block, axis, [(i, i ^ bits) for i in range(size)])  3.33 us
    pallas_call x1, Pallas kernels, attend(): pl.pallas_call(attend_kernel, out_shape=jax.ShapeDtypeStruct((slots * hea...  2.23 us
    pallas_call x1, Pallas kernels, adapted_out(): pl.pallas_call(functools.partial(adapted_kernel, slots, heads), out_shape...  0.72 us
    pallas_call x1, Pallas kernels, attention_out(): pl.pallas_call(functools.partial(attention_kernel, slots, heads), out_sha...  0.71 us
  transfers between devices with their start and end apart: 7, of which 3 were waited for; matrix products, arithmetic and copies ran while one was open for 0% of the time, Pallas kernels for 16%

profile of v4, /device:TPU:0, one launch (start us, length us, event | category | flops | bytes accessed | tf_op | source)
XLA Modules:
  0.0 24.1 jit_solution(12387978880343068836)
XLA Ops:
  0.6 0.0 copy-start.1
  0.6 0.0 copy-start
  0.7 3.1 %collective-permute-start = (bf16[4,16,2048]{2,1,0:T(8,128)(2,1)}, bf16[4,16,2048]{2,1,0:T(8,128)(2,1)S(1)}, u32[]{:S(2)}, u32[]{:S(2)}) collective-permute-start(bf16[4,16,2048]{2,1,0:T(8,128)(2,1)} %refs_3_.1), channel_id=1, source_target_pairs={{0,4},{4,0},{8,12},{12,8},{1,5},{5,1},{9,13},{13,9},{2,6},{6,2},{1... | collective-permute-start | bytes 786440 | tf_op jit(solution)/shard_map/ppermute | solution.py:327
  3.7 2.2 %attend.1.rows_ref = bf16[304,128]{1,0:T(8,128)(2,1)S(1)} custom-call(bf16[18,2048]{1,0:T(8,128)(2,1)} %q_ref.1, bf16[2,18,128,256]{3,2,1,0:T(8,128)(2,1)} %cache_ref.1, s32[18]{0:T(128)} %lengths_ref.1, s32[18]{0:T(128)} %index_ref.1), custom_call_target="tpu_custom_call" | custom-call | flops 75497472 | bytes 2359296 | tf_op jit(solution)/shard_map/attend/pallas_call | solution.py:80
  6.0 2.7 %collective-permute-start.1 = (bf16[304,128]{1,0:T(8,128)(2,1)S(1)}, bf16[304,128]{1,0:T(8,128)(2,1)S(1)}, u32[]{:S(2)}, u32[]{:S(2)}) collective-permute-start(bf16[304,128]{1,0:T(8,128)(2,1)S(1)} %attend.1.rows_ref), channel_id=1, source_target_pairs={{0,8},{4,12},{8,0},{12,4},{1,9},{5,13},{9,1},{13,5},{2,10},{6,14},... | collective-permute-start | bytes 233480 | tf_op jit(solution)/shard_map/ppermute | solution.py:322
  8.6 0.0 copy-done.1
  8.6 0.3 %lower_own.1 = (f32[16,32]{1,0:T(8,128)S(1)}, s32[1,32]{1,0:T(1,128)S(1)}, bf16[32,2048]{1,0:T(8,128)(2,1)S(1)}) custom-call(bf16[4,16,2048]{2,1,0:T(8,128)(2,1)S(1)} %copy-done.1, bf16[304,128]{1,0:T(8,128)(2,1)S(1)} %attend.1.rows_ref), custom_call_target="tpu_custom_call" | custom-call | tf_op jit(solution)/shard_map/lower_own/pallas_call | solution.py:195
  9.6 0.7 %attention_out.1 = (bf16[18,2048]{1,0:T(8,128)(2,1)}, f32[18,128]{1,0:T(8,128)S(1)}) custom-call(s32[1]{0:T(128)S(6)} %copy.9.live_ref, bf16[304,128]{1,0:T(8,128)(2,1)S(1)} %attend.1.rows_ref), custom_call_target="tpu_custom_call" | custom-call | tf_op jit(solution)/shard_map/attention_out/pallas_call | solution.py:119
  10.3 0.0 copy-done
  10.3 0.4 %collective-permute-start.2 = (bf16[4,16,2048]{2,1,0:T(8,128)(2,1)S(1)}, bf16[4,16,2048]{2,1,0:T(8,128)(2,1)S(1)}, u32[]{:S(2)}, u32[]{:S(2)}) collective-permute-start(bf16[4,16,2048]{2,1,0:T(8,128)(2,1)S(1)} %copy-done), channel_id=1, source_target_pairs={{0,4},{4,0},{8,12},{12,8},{1,5},{5,1},{9,13},{13,9},{2,6},{6,2},{1... | collective-permute-start | bytes 786440 | tf_op jit(solution)/shard_map/ppermute | solution.py:327
  10.8 1.4 %collective-permute-done.1.refs_5_ = bf16[304,128]{1,0:T(8,128)(2,1)S(1)} collective-permute-done((bf16[304,128]{1,0:T(8,128)(2,1)S(1)}, bf16[304,128]{1,0:T(8,128)(2,1)S(1)}, u32[]{:S(2)}, u32[]{:S(2)}) %collective-permute-start.1) | collective-permute-done | bytes 77856 | tf_op jit(solution)/shard_map/ppermute | solution.py:322
  12.2 0.0 collective-permute-done.refs_4_
  12.2 0.4 %lower.1 = (f32[16,64]{1,0:T(8,128)S(1)}, s32[2,32]{1,0:T(2,128)S(1)}) custom-call(f32[16,32]{1,0:T(8,128)S(1)} %get-tuple-element.12.refs_0_, s32[1,32]{1,0:T(1,128)S(1)} %get-tuple-element.13.refs_1_, bf16[32,2048]{1,0:T(8,128)(2,1)S(1)} %get-tuple-element.14.refs_2_, bf16[4,16,2048]{2,1,0:T(8,128)(2,1)S(1)} %copy-done.1, ...), custom_call_target="tpu_custom_call" | custom-call | flops 20000000000 | tf_op jit(solution)/shard_map/lower/pallas_call | solution.py:234
  12.5 0.1 collective-permute-start.3
  12.6 1.6 %collective-permute-start.4 = (f32[16,64]{1,0:T(8,128)S(1)}, f32[16,64]{1,0:T(8,128)S(1)}, u32[]{:S(2)}, u32[]{:S(2)}) collective-permute-start(f32[16,64]{1,0:T(8,128)S(1)} %get-tuple-element.17.refs_2_), channel_id=1, source_target_pairs={{0,2},{1,3},{2,0},{3,1},{4,6},{5,7},{6,4},{7,5},{8,10},{9,11},{10,... | collective-permute-start | bytes 12296 | tf_op jit(solution)/shard_map/ppermute | solution.py:327
  14.2 0.3 %collective-permute-start.5 = (f32[16,64]{1,0:T(8,128)S(1)}, f32[16,64]{1,0:T(8,128)S(1)}, u32[]{:S(2)}, u32[]{:S(2)}) collective-permute-start(f32[16,64]{1,0:T(8,128)S(1)} %get-tuple-element.17.refs_2_), channel_id=1, source_target_pairs={{0,1},{1,0},{2,3},{3,2},{4,5},{5,4},{6,7},{7,6},{8,9},{9,8},{10,11... | collective-permute-start | bytes 12296 | tf_op jit(solution)/shard_map/ppermute | solution.py:327
  14.5 3.3 %collective-permute-done.2.refs_1_ = bf16[4,16,2048]{2,1,0:T(8,128)(2,1)S(1)} collective-permute-done((bf16[4,16,2048]{2,1,0:T(8,128)(2,1)S(1)}, bf16[4,16,2048]{2,1,0:T(8,128)(2,1)S(1)}, u32[]{:S(2)}, u32[]{:S(2)}) %collective-permute-start.2) | collective-permute-done | bytes 262176 | tf_op jit(solution)/shard_map/ppermute | solution.py:327
  17.8 0.0 collective-permute-done.3.refs_3_
  17.8 0.0 collective-permute-done.4.refs_4_
  17.8 0.0 collective-permute-done.5.refs_5_
  17.8 0.3 %raise_rows.1 = bf16[288,128]{1,0:T(8,128)(2,1)S(1)} custom-call(s32[2,32]{1,0:T(2,128)S(1)} %get-tuple-element.15.index_ref, bf16[4,16,2048]{2,1,0:T(8,128)(2,1)S(1)} %copy-done, bf16[4,16,2048]{2,1,0:T(8,128)(2,1)S(1)} %collective-permute-done.2.refs_1_, f32[16,64]{1,0:T(8,128)S(1)} %get-tuple-element.17.refs_2_, ...), custom_call_target="tpu_custom_call" | custom-call | tf_op jit(solution)/shard_map/raise_rows/pallas_call | solution.py:286
  18.1 2.6 %collective-permute-start.6 = (bf16[288,128]{1,0:T(8,128)(2,1)S(1)}, bf16[288,128]{1,0:T(8,128)(2,1)S(1)}, u32[]{:S(2)}, u32[]{:S(2)}) collective-permute-start(bf16[288,128]{1,0:T(8,128)(2,1)S(1)} %raise_rows.1), channel_id=1, source_target_pairs={{0,8},{4,12},{8,0},{12,4},{1,9},{5,13},{9,1},{13,5},{2,10},{6,14},... | collective-permute-start | bytes 221192 | tf_op jit(solution)/shard_map/ppermute | solution.py:322
  20.6 0.3 %raise_own.1.own_ref = f32[18,2048]{1,0:T(8,128)S(1)} custom-call(s32[2,32]{1,0:T(2,128)S(1)} %get-tuple-element.15.index_ref, bf16[4,16,2048]{2,1,0:T(8,128)(2,1)S(1)} %copy-done, bf16[4,16,2048]{2,1,0:T(8,128)(2,1)S(1)} %collective-permute-done.2.refs_1_, f32[16,64]{1,0:T(8,128)S(1)} %get-tuple-element.17.refs_2_, ...), custom_call_target="tpu_custom_call" | custom-call | tf_op jit(solution)/shard_map/raise_own/pallas_call | solution.py:310
  20.9 2.4 %collective-permute-done.6.refs_0_ = bf16[288,128]{1,0:T(8,128)(2,1)S(1)} collective-permute-done((bf16[288,128]{1,0:T(8,128)(2,1)S(1)}, bf16[288,128]{1,0:T(8,128)(2,1)S(1)}, u32[]{:S(2)}, u32[]{:S(2)}) %collective-permute-start.6) | collective-permute-done | bytes 73760 | tf_op jit(solution)/shard_map/ppermute | solution.py:322
  23.4 0.7 %adapted_out.1 = bf16[18,2048]{1,0:T(8,128)(2,1)} custom-call(f32[18,128]{1,0:T(8,128)S(1)} %get-tuple-element.11.alive_ref, f32[18,2048]{1,0:T(8,128)S(1)} %raise_own.1.own_ref, bf16[288,128]{1,0:T(8,128)(2,1)S(1)} %collective-permute-done.6.refs_0_), custom_call_target="tpu_custom_call" | custom-call | tf_op jit(solution)/shard_map/adapted_out/pallas_call | solution.py:149
Async XLA Ops:
  0.6 8.0 %copy-start.1 = (bf16[4,16,2048]{2,1,0:T(8,128)(2,1)S(1)}, bf16[4,16,2048]{2,1,0:T(8,128)(2,1)}, u32[]{:S(2)}) copy-start(bf16[4,16,2048]{2,1,0:T(8,128)(2,1)} %refs_3_.1) | copy-start | bytes 786436
  0.6 9.7 %copy-start = (bf16[4,16,2048]{2,1,0:T(8,128)(2,1)S(1)}, bf16[4,16,2048]{2,1,0:T(8,128)(2,1)}, u32[]{:S(2)}) copy-start(bf16[4,16,2048]{2,1,0:T(8,128)(2,1)} %refs_0_.3) | copy-start | bytes 786436
  0.7 11.5 %collective-permute-start = (bf16[4,16,2048]{2,1,0:T(8,128)(2,1)}, bf16[4,16,2048]{2,1,0:T(8,128)(2,1)S(1)}, u32[]{:S(2)}, u32[]{:S(2)}) collective-permute-start(bf16[4,16,2048]{2,1,0:T(8,128)(2,1)} %refs_3_.1), channel_id=1, source_target_pairs={{0,4},{4,0},{8,12},{12,8},{1,5},{5,1},{9,13},{13,9},{2,6},{6,2},{1... | collective-permute-start | bytes 786440 | tf_op jit(solution)/shard_map/ppermute | solution.py:327
  6.0 6.2 %collective-permute-start.1 = (bf16[304,128]{1,0:T(8,128)(2,1)S(1)}, bf16[304,128]{1,0:T(8,128)(2,1)S(1)}, u32[]{:S(2)}, u32[]{:S(2)}) collective-permute-start(bf16[304,128]{1,0:T(8,128)(2,1)S(1)} %attend.1.rows_ref), channel_id=1, source_target_pairs={{0,8},{4,12},{8,0},{12,4},{1,9},{5,13},{9,1},{13,5},{2,10},{6,14},... | collective-permute-start | bytes 233480 | tf_op jit(solution)/shard_map/ppermute | solution.py:322
  10.3 7.5 %collective-permute-start.2 = (bf16[4,16,2048]{2,1,0:T(8,128)(2,1)S(1)}, bf16[4,16,2048]{2,1,0:T(8,128)(2,1)S(1)}, u32[]{:S(2)}, u32[]{:S(2)}) collective-permute-start(bf16[4,16,2048]{2,1,0:T(8,128)(2,1)S(1)} %copy-done), channel_id=1, source_target_pairs={{0,4},{4,0},{8,12},{12,8},{1,5},{5,1},{9,13},{13,9},{2,6},{6,2},{1... | collective-permute-start | bytes 786440 | tf_op jit(solution)/shard_map/ppermute | solution.py:327
  12.5 5.3 %collective-permute-start.3 = (f32[16,64]{1,0:T(8,128)S(1)}, f32[16,64]{1,0:T(8,128)S(1)}, u32[]{:S(2)}, u32[]{:S(2)}) collective-permute-start(f32[16,64]{1,0:T(8,128)S(1)} %get-tuple-element.17.refs_2_), channel_id=1, source_target_pairs={{0,3},{1,2},{2,1},{3,0},{4,7},{5,6},{6,5},{7,4},{8,11},{9,10},{10,... | collective-permute-start | bytes 12296 | tf_op jit(solution)/shard_map/ppermute | solution.py:327
  12.6 5.2 %collective-permute-start.4 = (f32[16,64]{1,0:T(8,128)S(1)}, f32[16,64]{1,0:T(8,128)S(1)}, u32[]{:S(2)}, u32[]{:S(2)}) collective-permute-start(f32[16,64]{1,0:T(8,128)S(1)} %get-tuple-element.17.refs_2_), channel_id=1, source_target_pairs={{0,2},{1,3},{2,0},{3,1},{4,6},{5,7},{6,4},{7,5},{8,10},{9,11},{10,... | collective-permute-start | bytes 12296 | tf_op jit(solution)/shard_map/ppermute | solution.py:327
  14.2 3.6 %collective-permute-start.5 = (f32[16,64]{1,0:T(8,128)S(1)}, f32[16,64]{1,0:T(8,128)S(1)}, u32[]{:S(2)}, u32[]{:S(2)}) collective-permute-start(f32[16,64]{1,0:T(8,128)S(1)} %get-tuple-element.17.refs_2_), channel_id=1, source_target_pairs={{0,1},{1,0},{2,3},{3,2},{4,5},{5,4},{6,7},{7,6},{8,9},{9,8},{10,11... | collective-permute-start | bytes 12296 | tf_op jit(solution)/shard_map/ppermute | solution.py:327
  18.1 5.3 %collective-permute-start.6 = (bf16[288,128]{1,0:T(8,128)(2,1)S(1)}, bf16[288,128]{1,0:T(8,128)(2,1)S(1)}, u32[]{:S(2)}, u32[]{:S(2)}) collective-permute-start(bf16[288,128]{1,0:T(8,128)(2,1)S(1)} %raise_rows.1), channel_id=1, source_target_pairs={{0,8},{4,12},{8,0},{12,4},{1,9},{5,13},{9,1},{13,5},{2,10},{6,14},... | collective-permute-start | bytes 221192 | tf_op jit(solution)/shard_map/ppermute | solution.py:322

commit v5 on v3

--- a/solution.py
+++ b/solution.py
@@ -12,12 +12,49 @@
 STAY = 16
 SCALING = 2.0
 LANES = 128
+GROUP = 16
 DIGIT = 7
 
 VMEM = pl.BlockSpec(memory_space=pltpu.VMEM)
 SMEM = pl.BlockSpec(memory_space=pltpu.SMEM)
 HBM = pl.BlockSpec(memory_space=pltpu.HBM)
 PARAMS = pltpu.CompilerParams(vmem_limit_bytes=16 * 2**20)
+
+
+class Lines:
+    def __init__(self, slots, heads):
+        self.slots, self.heads, self.cols = slots, heads, heads * HEAD_DIM
+        self.groups, self.left = divmod(slots, GROUP)
+        self.main = self.groups * GROUP
+        self.tiles = -(-self.left * heads // GROUP)
+        self.start = self.groups * self.cols
+        self.width = self.start + self.tiles * HEAD_DIM
+        self.small = (max(1, self.tiles) * GROUP, HEAD_DIM)
+
+    def tile(self, number):
+        return slice(self.start + number * HEAD_DIM, self.start + (number + 1) * HEAD_DIM)
+
+    def load_left(self, refs, small):
+        for number in range(self.tiles):
+            total = refs[0][:, self.tile(number)].astype(jnp.float32)
+            for ref in refs[1:]:
+                total += ref[:, self.tile(number)].astype(jnp.float32)
+            small[number * GROUP : (number + 1) * GROUP, :] = total
+
+    def left_rows(self, head, small):
+        return small[pl.ds(head, self.left, stride=self.heads), :]
+
+    def column(self, refs, head, small):
+        pieces = []
+        for group in range(self.groups):
+            lanes = slice(group * self.cols + head * HEAD_DIM, group * self.cols + (head + 1) * HEAD_DIM)
+            total = refs[0][:, lanes].astype(jnp.float32)
+            for ref in refs[1:]:
+                total += ref[:, lanes].astype(jnp.float32)
+            pieces.append(total)
+        if self.left:
+            pieces.append(self.left_rows(head, small))
+        return jnp.concatenate(pieces, axis=0)
 
 
 def attend_kernel(
@@ -63,23 +100,34 @@
         for k in range(1, key_heads):
             rows = jnp.where(owner == k, mixed[:, k * HEAD_DIM : (k + 1) * HEAD_DIM], rows)
         o_rows[slot * heads : (slot + 1) * heads, :] = rows
-    rows_ref[: slots * heads, :] = o_rows[...].astype(jnp.bfloat16)
+    lines = Lines(slots, heads)
+    for group in range(lines.groups):
+        for head in range(heads):
+            lanes = slice(group * cols + head * HEAD_DIM, group * cols + (head + 1) * HEAD_DIM)
+            block = o_rows[pl.ds(group * GROUP * heads + head, GROUP, stride=heads), :]
+            rows_ref[:, lanes] = block.astype(jnp.bfloat16)
+    if lines.tiles * GROUP > lines.left * heads:
+        o_rows[slots * heads :, :] = jnp.zeros((lines.tiles * GROUP - lines.left * heads, HEAD_DIM), jnp.float32)
+    for number in range(lines.tiles):
+        first = lines.main * heads + number * GROUP
+        rows_ref[:, lines.tile(number)] = o_rows[first : first + GROUP, :].astype(jnp.bfloat16)
     lane = lax.broadcasted_iota(jnp.int32, (16, LANES), 1)
     line = lax.broadcasted_iota(jnp.int32, (16, LANES), 0)
     named = jnp.zeros((16, LANES), jnp.int32)
     for slot in range(slots):
         named = jnp.where(lane == slot, index[slot], named)
     digits = jnp.where(line == 0, named >> DIGIT, named & ((1 << DIGIT) - 1))
-    rows_ref[slots * heads :, :] = digits.astype(jnp.float32).astype(jnp.bfloat16)
+    rows_ref[:, lines.width :] = digits.astype(jnp.float32).astype(jnp.bfloat16)
 
 
 def attend(queries, past_cache, lengths, adapter_index):
     slots, cols = queries.shape
     heads = cols // HEAD_DIM
+    lines = Lines(slots, heads)
     buffer = pltpu.VMEM(past_cache.shape[1:], past_cache.dtype)
     return pl.pallas_call(
         attend_kernel,
-        out_shape=jax.ShapeDtypeStruct((slots * heads + 16, HEAD_DIM), jnp.bfloat16),
+        out_shape=jax.ShapeDtypeStruct((GROUP, lines.width + LANES), jnp.bfloat16),
         in_specs=[HBM] * 4,
         out_specs=VMEM,
         scratch_shapes=[
@@ -89,7 +137,7 @@
             buffer,
             buffer,
             pltpu.VMEM((slots * heads, HEAD_DIM), jnp.float32),
-            pltpu.VMEM((slots * heads, HEAD_DIM), jnp.float32),
+            pltpu.VMEM((lines.main * heads + lines.tiles * GROUP, HEAD_DIM), jnp.float32),
             pltpu.SemaphoreType.DMA((3,)),
             pltpu.SemaphoreType.DMA((2,)),
         ],
@@ -106,13 +154,14 @@
     return (slot >= STAY) | (slot < live_ref[0])
 
 
-def attention_kernel(slots, heads, live_ref, rows_ref, out_ref, alive_ref, flat):
+def attention_kernel(slots, heads, live_ref, rows_ref, out_ref, alive_ref, small):
+    lines = Lines(slots, heads)
     alive = alive_lines(live_ref, slots)
     alive_ref[...] = alive.astype(jnp.float32)
-    flat[...] = rows_ref[: slots * heads, :].astype(jnp.float32)
+    lines.load_left([rows_ref], small)
     for head in range(heads):
-        block = flat[pl.ds(head, slots, stride=heads), :]
-        out_ref[:, head * HEAD_DIM : (head + 1) * HEAD_DIM] = jnp.where(alive, block, 0.0).astype(out_ref.dtype)
+        block = jnp.where(alive, lines.column([rows_ref], head, small), 0.0)
+        out_ref[:, head * HEAD_DIM : (head + 1) * HEAD_DIM] = block.astype(out_ref.dtype)
 
 
 def attention_out(live, rows, slots, heads):
@@ -124,24 +173,22 @@
         ),
         in_specs=[SMEM, VMEM],
         out_specs=(VMEM, VMEM),
-        scratch_shapes=[pltpu.VMEM((slots * heads, HEAD_DIM), jnp.float32)],
+        scratch_shapes=[pltpu.VMEM(Lines(slots, heads).small, jnp.float32)],
         compiler_params=PARAMS,
         name="attention_out",
     )(live, rows)
 
 
 def adapted_kernel(slots, heads, alive_ref, own_ref, *refs):
-    rows_refs, out_ref, flat = refs[:-2], refs[-2], refs[-1]
+    rows_refs, out_ref, small = refs[:-2], refs[-2], refs[-1]
+    lines = Lines(slots, heads)
     alive = alive_ref[...] > 0
     if rows_refs:
-        total = rows_refs[0][...].astype(jnp.float32)
-        for other in rows_refs[1:]:
-            total += other[...].astype(jnp.float32)
-        flat[...] = total
+        lines.load_left(rows_refs, small)
     for head in range(heads):
         block = own_ref[:, head * HEAD_DIM : (head + 1) * HEAD_DIM]
         if rows_refs:
-            block += flat[pl.ds(head, slots, stride=heads), :]
+            block += lines.column(rows_refs, head, small)
         out_ref[:, head * HEAD_DIM : (head + 1) * HEAD_DIM] = jnp.where(alive, block, 0.0).astype(out_ref.dtype)
 
 
@@ -151,7 +198,7 @@
         out_shape=jax.ShapeDtypeStruct((slots, heads * HEAD_DIM), jnp.bfloat16),
         in_specs=[VMEM] * (2 + len(rows)),
         out_specs=VMEM,
-        scratch_shapes=[pltpu.VMEM((slots * heads, HEAD_DIM), jnp.float32)],
+        scratch_shapes=[pltpu.VMEM(Lines(slots, heads).small, jnp.float32)],
         compiler_params=PARAMS,
         name="adapted_out",
     )(alive, own, *rows)
@@ -161,72 +208,66 @@
     return (lax.axis_index("replica") ^ holder) * local_count
 
 
-def unfold_rows(rows_ref, slots, heads, pad, flat, wide_ref, first):
-    flat[: slots * heads, :] = rows_ref[: slots * heads, :].astype(jnp.float32)
-    if pad > slots:
-        flat[slots * heads :, :] = jnp.zeros(((pad - slots) * heads, HEAD_DIM), jnp.float32)
-    for head in range(heads):
-        wide_ref[first : first + pad, head * HEAD_DIM : (head + 1) * HEAD_DIM] = flat[
-            pl.ds(head, pad, stride=heads), :
-        ].astype(jnp.bfloat16)
-    digits = rows_ref[slots * heads :, :].astype(jnp.float32).astype(jnp.int32)
+def unfold_rows(rows_ref, slots, heads, pad, small, wide_ref, first):
+    lines = Lines(slots, heads)
+    for group in range(lines.groups):
+        at = first + group * GROUP
+        wide_ref[at : at + GROUP, :] = rows_ref[:, group * lines.cols : (group + 1) * lines.cols]
+    lines.load_left([rows_ref], small)
+    if pad > lines.main:
+        for head in range(heads):
+            block = jnp.zeros((pad - slots, HEAD_DIM), jnp.float32)
+            if lines.left:
+                block = jnp.concatenate([lines.left_rows(head, small), block], axis=0)
+            lanes = slice(head * HEAD_DIM, (head + 1) * HEAD_DIM)
+            wide_ref[first + lines.main : first + pad, lanes] = block.astype(jnp.bfloat16)
+    digits = rows_ref[:, lines.width :].astype(jnp.float32).astype(jnp.int32)
     return ((digits[0:1, :] << DIGIT) + digits[1:2, :])[:, :pad]
 
 
-def rank_rows(down_ref, holder, wide, named):
-    local_count, rank, cols = down_ref.shape
-    down = down_ref[...].reshape(local_count * rank, cols)
-    every = lax.dot_general(down, wide, (((1,), (1,)), ((), ())), preferred_element_type=jnp.float32)
-    base = first_adapter(holder, local_count)
-    total = jnp.zeros((rank, named.shape[1]), jnp.float32)
-    for local in range(local_count):
-        total += jnp.where(named == base + local, every[local * rank : (local + 1) * rank, :], 0.0)
-    return total
-
-
-def lower_own_kernel(slots, heads, pad, down_ref, rows_ref, partial_ref, index_ref, wide_ref, flat):
-    named = unfold_rows(rows_ref, slots, heads, pad, flat, wide_ref, 0)
-    index_ref[...] = named
-    partial_ref[...] = rank_rows(down_ref, 0, wide_ref[...], named)
-
-
-def lower_own(down, rows, slots, heads, pad):
-    rank = down.shape[1]
-    return pl.pallas_call(
-        functools.partial(lower_own_kernel, slots, heads, pad),
+def own_lines_kernel(slots, heads, pad, rows_ref, index_ref, wide_ref, small):
+    index_ref[...] = unfold_rows(rows_ref, slots, heads, pad, small, wide_ref, 0)
+
+
+def own_lines(rows, slots, heads, pad):
+    return pl.pallas_call(
+        functools.partial(own_lines_kernel, slots, heads, pad),
         out_shape=(
-            jax.ShapeDtypeStruct((rank, pad), jnp.float32),
             jax.ShapeDtypeStruct((1, pad), jnp.int32),
             jax.ShapeDtypeStruct((pad, heads * HEAD_DIM), jnp.bfloat16),
         ),
-        in_specs=[VMEM] * 2,
-        out_specs=[VMEM] * 3,
-        scratch_shapes=[pltpu.VMEM((pad * heads, HEAD_DIM), jnp.float32)],
-        compiler_params=PARAMS,
-        name="lower_own",
-    )(down, rows)
-
-
-def lower_kernel(slots, heads, pad, sources, holders, *refs):
-    own_partial, own_index, own_wide = refs[:3]
-    down_refs, rows_refs = refs[3 : 3 + holders], refs[3 + holders : 3 + holders + sources]
-    partial_ref, index_ref, flat, wide = refs[-4:]
-    rank = down_refs[0].shape[1]
-    named = [own_index[...]]
+        in_specs=[VMEM],
+        out_specs=[VMEM] * 2,
+        scratch_shapes=[pltpu.VMEM(Lines(slots, heads).small, jnp.float32)],
+        compiler_params=PARAMS,
+        name="own_lines",
+    )(rows)
+
+
+def lower_kernel(slots, heads, pad, sources, holders, own_index_ref, own_wide_ref, *refs):
+    down_refs, rows_refs = refs[:holders], refs[holders : holders + sources]
+    partial_ref, index_ref, small, wide = refs[-4:]
+    local_count, rank, cols = down_refs[0].shape
+    named = []
     for source in range(sources):
-        named.append(unfold_rows(rows_refs[source], slots, heads, pad, flat, wide, source * pad))
+        named.append(unfold_rows(rows_refs[source], slots, heads, pad, small, wide, source * pad))
+    named.append(own_index_ref[...])
     for block in range(sources + 1):
-        index_ref[block : block + 1, :] = named[block]
-    total = own_partial[...]
-    for holder in range(1, holders):
-        total += rank_rows(down_refs[holder], holder, own_wide[...], named[0])
-    totals = [total]
-    for source in range(sources):
-        total = jnp.zeros((rank, pad), jnp.float32)
-        for holder in range(holders):
-            total += rank_rows(down_refs[holder], holder, wide[source * pad : (source + 1) * pad, :], named[1 + source])
-        totals.append(total)
-    partial_ref[...] = jnp.concatenate(totals[1:] + totals[:1], axis=1)
+        index_ref[block : block + 1, :] = named[block - 1]
+    down = jnp.concatenate([ref[...].reshape(local_count * rank, cols) for ref in down_refs], axis=0)
+    rows = own_wide_ref[...]
+    if sources:
+        rows = jnp.concatenate([wide[...], rows], axis=0)
+    every = lax.dot_general(down, rows, (((1,), (1,)), ((), ())), preferred_element_type=jnp.float32)
+    named = jnp.concatenate(named, axis=1)
+    total = jnp.zeros((rank, named.shape[1]), jnp.float32)
+    for holder in range(holders):
+        for local in range(local_count):
+            line = (holder * local_count + local) * rank
+            mine = named == first_adapter(holder, local_count) + local
+            total += jnp.where(mine, every[line : line + rank, :], 0.0)
+    partial_ref[...] = total
+
 
 def lower(own, downs, rows, slots, heads, pad):
     sources = len(rows)
@@ -237,11 +278,11 @@
             jax.ShapeDtypeStruct((rank, (1 + sources) * pad), jnp.float32),
             jax.ShapeDtypeStruct((1 + sources, pad), jnp.int32),
         ),
-        in_specs=[VMEM] * (3 + len(downs) + sources),
+        in_specs=[VMEM] * (2 + len(downs) + sources),
         out_specs=[VMEM] * 2,
         scratch_shapes=[
-            pltpu.VMEM((pad * heads, HEAD_DIM), jnp.float32),
-            pltpu.VMEM((sources * pad, heads * HEAD_DIM), jnp.bfloat16),
+            pltpu.VMEM(Lines(slots, heads).small, jnp.float32),
+            pltpu.VMEM((max(1, sources) * pad, heads * HEAD_DIM), jnp.bfloat16),
         ],
         cost_estimate=pl.CostEstimate(flops=2 * 10**10, bytes_accessed=0, transcendentals=0),
         compiler_params=PARAMS,
@@ -266,8 +307,9 @@
 
 
 def raise_kernel(slots, heads, sources, holders, index_ref, *refs):
-    up_refs, partials, outs, flat = refs[:holders], refs[holders : -sources - 1], refs[-sources - 1 : -1], refs[-1]
+    up_refs, partials, outs, small = refs[:holders], refs[holders : -sources - 1], refs[-sources - 1 : -1], refs[-1]
     local_count, rank, cols = up_refs[0].shape
+    lines = Lines(slots, heads)
     up = stack_ups(up_refs)
     packed = partials[0][...]
     for other in partials[1:]:
@@ -277,18 +319,28 @@
         total = packed[:, source * pad : (source + 1) * pad]
         spread = spread_ranks(index_ref[1 + source : 2 + source, :], total, holders, local_count)
         wide = lax.dot_general(spread, up, (((0,), (0,)), ((), ())), preferred_element_type=jnp.float32)
-        for head in range(heads):
-            flat[pl.ds(head, slots, stride=heads), :] = wide[:slots, head * HEAD_DIM : (head + 1) * HEAD_DIM]
-        outs[source][...] = flat[...].astype(jnp.bfloat16)
+        out_ref = outs[source]
+        for group in range(lines.groups):
+            block = wide[group * GROUP : (group + 1) * GROUP, :]
+            out_ref[:, group * cols : (group + 1) * cols] = block.astype(jnp.bfloat16)
+        if lines.left:
+            small[...] = jnp.zeros(small.shape, jnp.float32)
+            for head in range(heads):
+                block = wide[lines.main : slots, head * HEAD_DIM : (head + 1) * HEAD_DIM]
+                small[pl.ds(head, lines.left, stride=heads), :] = block
+        for number in range(lines.tiles):
+            block = small[number * GROUP : (number + 1) * GROUP, :]
+            out_ref[:, lines.tile(number)] = block.astype(jnp.bfloat16)
 
 
 def raise_rows(index, ups, partials, slots, heads, sources):
+    lines = Lines(slots, heads)
     return pl.pallas_call(
         functools.partial(raise_kernel, slots, heads, sources, len(ups)),
-        out_shape=[jax.ShapeDtypeStruct((slots * heads, HEAD_DIM), jnp.bfloat16)] * sources,
+        out_shape=[jax.ShapeDtypeStruct((GROUP, lines.width), jnp.bfloat16)] * sources,
         in_specs=[VMEM] * (1 + len(ups) + len(partials)),
         out_specs=[VMEM] * sources,
-        scratch_shapes=[pltpu.VMEM((slots * heads, HEAD_DIM), jnp.float32)],
+        scratch_shapes=[pltpu.VMEM(lines.small, jnp.float32)],
         compiler_params=PARAMS,
         name="raise_rows",
     )(index, *ups, *partials)
@@ -347,8 +399,8 @@
     rows = attend(queries, past_cache, lengths, adapter_index)
     gathered = [shift(rows, "replica", holders * k) for k in range(1, sources)]
     attention, alive = attention_out(live_counts, rows, slots, heads)
-    own = lower_own(adapter_down, rows, slots, heads, pad)
-    later_up = lax.optimization_barrier((adapter_up, alive, own[0]))[0]
+    own = own_lines(rows, slots, heads, pad)
+    later_up = lax.optimization_barrier((adapter_up, alive))[0]
     ups = [adapter_up] + [swap(later_up, "replica") for _ in range(1, holders)]
     partial, index = lower(own, downs, gathered, slots, heads, pad)
     partials = [partial] + exchange(partial, "tensor")

time: 24.3 us -> 24.2 us (level)
  Pallas kernels: 4.9 us -> 4.45 us
  starting transfers between devices: 11.2 us -> 11.6 us
    ppermute x5, waiting for transfers between devices: 3.05 us -> 2.7 us  [swap(): return lax.ppermute(block, axis, [(i, i ^ bits) for i in range(size)])]
    ppermute x2, starting transfers between devices: 5.47 us -> 5.82 us  [shift(): lax.ppermute(block, axis, [(i, (i + offset) % size) for i in range(size)])]
    ppermute x2, waiting for transfers between devices: 3.62 us -> 3.94 us  [shift(): lax.ppermute(block, axis, [(i, (i + offset) % size) for i in range(size)])]
    pallas_call x2, Pallas kernels: 2.53 us -> 2.26 us  [the longest x1 2.24 us: attend(): pl.pallas_call(attend_kernel, out_shape=jax.ShapeDtypeStruct((GROUP, line...]
  transfers between devices with their start and end apart: 7 -> 7, of which waited for: 3 -> 3; matrix products, arithmetic and copies ran while one was open for 0% -> 0% of each run, Pallas kernels for 16% -> 15%
where the time goes in v5:
time: 24.2 us; the launch traced here: 24 us
  starting transfers between devices  11.6 us (48%)
  waiting for transfers between devices  6.64 us (27%)
  Pallas kernels  4.45 us (18%)
  between operations  1.33 us (5%)
    ppermute x2, starting transfers between devices, shift(): lax.ppermute(block, axis, [(i, (i + offset) % size) for i in range(size)])  5.82 us
    ppermute x5, starting transfers between devices, swap(): return lax.ppermute(block, axis, [(i, i ^ bits) for i in range(size)])  5.74 us
    ppermute x2, waiting for transfers between devices, shift(): lax.ppermute(block, axis, [(i, (i + offset) % size) for i in range(size)])  3.94 us
    ppermute x5, waiting for transfers between devices, swap(): return lax.ppermute(block, axis, [(i, i ^ bits) for i in range(size)])  2.7 us
    pallas_call x1, Pallas kernels, attend(): pl.pallas_call(attend_kernel, out_shape=jax.ShapeDtypeStruct((GROUP, line...  2.24 us
    pallas_call x1, Pallas kernels, adapted_out(): pl.pallas_call(functools.partial(adapted_kernel, slots, heads), out_shape...  0.67 us
    pallas_call x1, Pallas kernels, attention_out(): pl.pallas_call(functools.partial(attention_kernel, slots, heads), out_sha...  0.66 us
  transfers between devices with their start and end apart: 7, of which 3 were waited for; matrix products, arithmetic and copies ran while one was open for 0% of the time, Pallas kernels for 15%

profile of v5, /device:TPU:0, one launch (start us, length us, event | category | flops | bytes accessed | tf_op | source)
XLA Modules:
  0.0 24.0 jit_solution(6878469079949313803)
XLA Ops:
  0.6 0.0 copy-start.1
  0.6 0.0 copy-start
  0.7 3.1 %collective-permute-start = (bf16[4,16,2048]{2,1,0:T(8,128)(2,1)}, bf16[4,16,2048]{2,1,0:T(8,128)(2,1)S(1)}, u32[]{:S(2)}, u32[]{:S(2)}) collective-permute-start(bf16[4,16,2048]{2,1,0:T(8,128)(2,1)} %refs_0_.3), channel_id=1, source_target_pairs={{0,4},{4,0},{8,12},{12,8},{1,5},{5,1},{9,13},{13,9},{2,6},{6,2},{1... | collective-permute-start | bytes 786440 | tf_op jit(solution)/shard_map/ppermute | solution.py:379
  3.7 2.2 %attend.1.rows_ref = bf16[16,2432]{1,0:T(8,128)(2,1)S(1)} custom-call(bf16[18,2048]{1,0:T(8,128)(2,1)} %q_ref.1, bf16[2,18,128,256]{3,2,1,0:T(8,128)(2,1)} %cache_ref.1, s32[18]{0:T(128)} %lengths_ref.1, s32[18]{0:T(128)} %index_ref.1), custom_call_target="tpu_custom_call" | custom-call | flops 75497472 | bytes 2359296 | tf_op jit(solution)/shard_map/attend/pallas_call | solution.py:128
  6.0 2.7 %collective-permute-start.1 = (bf16[16,2432]{1,0:T(8,128)(2,1)S(1)}, bf16[16,2432]{1,0:T(8,128)(2,1)S(1)}, u32[]{:S(2)}, u32[]{:S(2)}) collective-permute-start(bf16[16,2432]{1,0:T(8,128)(2,1)S(1)} %attend.1.rows_ref), channel_id=1, source_target_pairs={{0,8},{4,12},{8,0},{12,4},{1,9},{5,13},{9,1},{13,5},{2,10},{6,14},... | collective-permute-start | bytes 233480 | tf_op jit(solution)/shard_map/ppermute | solution.py:374
  9.3 0.7 %attention_out.1 = (bf16[18,2048]{1,0:T(8,128)(2,1)}, f32[18,128]{1,0:T(8,128)S(1)}) custom-call(s32[1]{0:T(128)S(6)} %copy.9.live_ref, bf16[16,2432]{1,0:T(8,128)(2,1)S(1)} %attend.1.rows_ref), custom_call_target="tpu_custom_call" | custom-call | tf_op jit(solution)/shard_map/attention_out/pallas_call | solution.py:168
  10.0 0.0 copy-done
  10.0 0.4 %collective-permute-start.2 = (bf16[4,16,2048]{2,1,0:T(8,128)(2,1)S(1)}, bf16[4,16,2048]{2,1,0:T(8,128)(2,1)S(1)}, u32[]{:S(2)}, u32[]{:S(2)}) collective-permute-start(bf16[4,16,2048]{2,1,0:T(8,128)(2,1)S(1)} %copy-done), channel_id=1, source_target_pairs={{0,4},{4,0},{8,12},{12,8},{1,5},{5,1},{9,13},{13,9},{2,6},{6,2},{1... | collective-permute-start | bytes 786440 | tf_op jit(solution)/shard_map/ppermute | solution.py:379
  10.4 1.9 %collective-permute-done.1.refs_2_ = bf16[16,2432]{1,0:T(8,128)(2,1)S(1)} collective-permute-done((bf16[16,2432]{1,0:T(8,128)(2,1)S(1)}, bf16[16,2432]{1,0:T(8,128)(2,1)S(1)}, u32[]{:S(2)}, u32[]{:S(2)}) %collective-permute-start.1) | collective-permute-done | bytes 77856 | tf_op jit(solution)/shard_map/ppermute | solution.py:374
  12.3 0.0 collective-permute-done.refs_1_
  12.3 0.0 copy-done.1
  12.3 0.3 %lower.1 = (f32[16,64]{1,0:T(8,128)S(1)}, s32[2,32]{1,0:T(2,128)S(1)}) custom-call(s32[1,32]{1,0:T(1,128)S(1)} %get-tuple-element.11.own_index_ref, bf16[32,2048]{1,0:T(8,128)(2,1)S(1)} %get-tuple-element.12.own_wide_ref, bf16[4,16,2048]{2,1,0:T(8,128)(2,1)S(1)} %copy-done.1, bf16[4,16,2048]{2,1,0:T(8,128)(2,1)S(1)} %collective-permute-done.refs_1_, ...), custom_call_target="tpu_custom_call" | custom-call | flops 20000000000 | tf_op jit(solution)/shard_map/lower/pallas_call | solution.py:275
  12.6 1.6 %collective-permute-start.3 = (f32[16,64]{1,0:T(8,128)S(1)}, f32[16,64]{1,0:T(8,128)S(1)}, u32[]{:S(2)}, u32[]{:S(2)}) collective-permute-start(f32[16,64]{1,0:T(8,128)S(1)} %get-tuple-element.15.refs_2_), channel_id=1, source_target_pairs={{0,2},{1,3},{2,0},{3,1},{4,6},{5,7},{6,4},{7,5},{8,10},{9,11},{10,... | collective-permute-start | bytes 12296 | tf_op jit(solution)/shard_map/ppermute | solution.py:379
  14.2 0.0 collective-permute-start.4
  14.2 0.6 %collective-permute-start.5 = (f32[16,64]{1,0:T(8,128)S(1)}, f32[16,64]{1,0:T(8,128)S(1)}, u32[]{:S(2)}, u32[]{:S(2)}) collective-permute-start(f32[16,64]{1,0:T(8,128)S(1)} %get-tuple-element.15.refs_2_), channel_id=1, source_target_pairs={{0,1},{1,0},{2,3},{3,2},{4,5},{5,4},{6,7},{7,6},{8,9},{9,8},{10,11... | collective-permute-start | bytes 12296 | tf_op jit(solution)/shard_map/ppermute | solution.py:379
  14.9 2.7 %collective-permute-done.2.refs_1_ = bf16[4,16,2048]{2,1,0:T(8,128)(2,1)S(1)} collective-permute-done((bf16[4,16,2048]{2,1,0:T(8,128)(2,1)S(1)}, bf16[4,16,2048]{2,1,0:T(8,128)(2,1)S(1)}, u32[]{:S(2)}, u32[]{:S(2)}) %collective-permute-start.2) | collective-permute-done | bytes 262176 | tf_op jit(solution)/shard_map/ppermute | solution.py:379
  17.5 0.0 collective-permute-done.3.refs_3_
  17.5 0.0 collective-permute-done.4.refs_4_
  17.5 0.0 collective-permute-done.5.refs_5_
  17.6 0.3 %raise_rows.1 = bf16[16,2304]{1,0:T(8,128)(2,1)S(1)} custom-call(s32[2,32]{1,0:T(2,128)S(1)} %get-tuple-element.13.index_ref, bf16[4,16,2048]{2,1,0:T(8,128)(2,1)S(1)} %copy-done, bf16[4,16,2048]{2,1,0:T(8,128)(2,1)S(1)} %collective-permute-done.2.refs_1_, f32[16,64]{1,0:T(8,128)S(1)} %get-tuple-element.15.refs_2_, ...), custom_call_target="tpu_custom_call" | custom-call | tf_op jit(solution)/shard_map/raise_rows/pallas_call | solution.py:338
  17.8 3.2 %collective-permute-start.6 = (bf16[16,2304]{1,0:T(8,128)(2,1)S(1)}, bf16[16,2304]{1,0:T(8,128)(2,1)S(1)}, u32[]{:S(2)}, u32[]{:S(2)}) collective-permute-start(bf16[16,2304]{1,0:T(8,128)(2,1)S(1)} %raise_rows.1), channel_id=1, source_target_pairs={{0,8},{4,12},{8,0},{12,4},{1,9},{5,13},{9,1},{13,5},{2,10},{6,14},... | collective-permute-start | bytes 221192 | tf_op jit(solution)/shard_map/ppermute | solution.py:374
  21.0 0.3 %raise_own.1.own_ref = f32[18,2048]{1,0:T(8,128)S(1)} custom-call(s32[2,32]{1,0:T(2,128)S(1)} %get-tuple-element.13.index_ref, bf16[4,16,2048]{2,1,0:T(8,128)(2,1)S(1)} %copy-done, bf16[4,16,2048]{2,1,0:T(8,128)(2,1)S(1)} %collective-permute-done.2.refs_1_, f32[16,64]{1,0:T(8,128)S(1)} %get-tuple-element.15.refs_2_, ...), custom_call_target="tpu_custom_call" | custom-call | tf_op jit(solution)/shard_map/raise_own/pallas_call | solution.py:362
  21.3 2.0 %collective-permute-done.6.refs_0_ = bf16[16,2304]{1,0:T(8,128)(2,1)S(1)} collective-permute-done((bf16[16,2304]{1,0:T(8,128)(2,1)S(1)}, bf16[16,2304]{1,0:T(8,128)(2,1)S(1)}, u32[]{:S(2)}, u32[]{:S(2)}) %collective-permute-start.6) | collective-permute-done | bytes 73760 | tf_op jit(solution)/shard_map/ppermute | solution.py:374
  23.3 0.7 %adapted_out.1 = bf16[18,2048]{1,0:T(8,128)(2,1)} custom-call(f32[18,128]{1,0:T(8,128)S(1)} %get-tuple-element.10.alive_ref, f32[18,2048]{1,0:T(8,128)S(1)} %raise_own.1.own_ref, bf16[16,2304]{1,0:T(8,128)(2,1)S(1)} %collective-permute-done.6.refs_0_), custom_call_target="tpu_custom_call" | custom-call | tf_op jit(solution)/shard_map/adapted_out/pallas_call | solution.py:196
  (1 shorter events, 0.0 us)
Async XLA Ops:
  0.6 11.7 %copy-start.1 = (bf16[4,16,2048]{2,1,0:T(8,128)(2,1)S(1)}, bf16[4,16,2048]{2,1,0:T(8,128)(2,1)}, u32[]{:S(2)}) copy-start(bf16[4,16,2048]{2,1,0:T(8,128)(2,1)} %refs_0_.3) | copy-start | bytes 786436
  0.6 9.3 %copy-start = (bf16[4,16,2048]{2,1,0:T(8,128)(2,1)S(1)}, bf16[4,16,2048]{2,1,0:T(8,128)(2,1)}, u32[]{:S(2)}) copy-start(bf16[4,16,2048]{2,1,0:T(8,128)(2,1)} %refs_0_.5) | copy-start | bytes 786436
  0.7 11.7 %collective-permute-start = (bf16[4,16,2048]{2,1,0:T(8,128)(2,1)}, bf16[4,16,2048]{2,1,0:T(8,128)(2,1)S(1)}, u32[]{:S(2)}, u32[]{:S(2)}) collective-permute-start(bf16[4,16,2048]{2,1,0:T(8,128)(2,1)} %refs_0_.3), channel_id=1, source_target_pairs={{0,4},{4,0},{8,12},{12,8},{1,5},{5,1},{9,13},{13,9},{2,6},{6,2},{1... | collective-permute-start | bytes 786440 | tf_op jit(solution)/shard_map/ppermute | solution.py:379
  6.0 6.3 %collective-permute-start.1 = (bf16[16,2432]{1,0:T(8,128)(2,1)S(1)}, bf16[16,2432]{1,0:T(8,128)(2,1)S(1)}, u32[]{:S(2)}, u32[]{:S(2)}) collective-permute-start(bf16[16,2432]{1,0:T(8,128)(2,1)S(1)} %attend.1.rows_ref), channel_id=1, source_target_pairs={{0,8},{4,12},{8,0},{12,4},{1,9},{5,13},{9,1},{13,5},{2,10},{6,14},... | collective-permute-start | bytes 233480 | tf_op jit(solution)/shard_map/ppermute | solution.py:374
  10.0 7.6 %collective-permute-start.2 = (bf16[4,16,2048]{2,1,0:T(8,128)(2,1)S(1)}, bf16[4,16,2048]{2,1,0:T(8,128)(2,1)S(1)}, u32[]{:S(2)}, u32[]{:S(2)}) collective-permute-start(bf16[4,16,2048]{2,1,0:T(8,128)(2,1)S(1)} %copy-done), channel_id=1, source_target_pairs={{0,4},{4,0},{8,12},{12,8},{1,5},{5,1},{9,13},{13,9},{2,6},{6,2},{1... | collective-permute-start | bytes 786440 | tf_op jit(solution)/shard_map/ppermute | solution.py:379
  12.6 4.9 %collective-permute-start.3 = (f32[16,64]{1,0:T(8,128)S(1)}, f32[16,64]{1,0:T(8,128)S(1)}, u32[]{:S(2)}, u32[]{:S(2)}) collective-permute-start(f32[16,64]{1,0:T(8,128)S(1)} %get-tuple-element.15.refs_2_), channel_id=1, source_target_pairs={{0,2},{1,3},{2,0},{3,1},{4,6},{5,7},{6,4},{7,5},{8,10},{9,11},{10,... | collective-permute-start | bytes 12296 | tf_op jit(solution)/shard_map/ppermute | solution.py:379
  14.2 3.3 %collective-permute-start.4 = (f32[16,64]{1,0:T(8,128)S(1)}, f32[16,64]{1,0:T(8,128)S(1)}, u32[]{:S(2)}, u32[]{:S(2)}) collective-permute-start(f32[16,64]{1,0:T(8,128)S(1)} %get-tuple-element.15.refs_2_), channel_id=1, source_target_pairs={{0,3},{1,2},{2,1},{3,0},{4,7},{5,6},{6,5},{7,4},{8,11},{9,10},{10,... | collective-permute-start | bytes 12296 | tf_op jit(solution)/shard_map/ppermute | solution.py:379
  14.2 3.3 %collective-permute-start.5 = (f32[16,64]{1,0:T(8,128)S(1)}, f32[16,64]{1,0:T(8,128)S(1)}, u32[]{:S(2)}, u32[]{:S(2)}) collective-permute-start(f32[16,64]{1,0:T(8,128)S(1)} %get-tuple-element.15.refs_2_), channel_id=1, source_target_pairs={{0,1},{1,0},{2,3},{3,2},{4,5},{5,4},{6,7},{7,6},{8,9},{9,8},{10,11... | collective-permute-start | bytes 12296 | tf_op jit(solution)/shard_map/ppermute | solution.py:379
  17.8 5.5 %collective-permute-start.6 = (bf16[16,2304]{1,0:T(8,128)(2,1)S(1)}, bf16[16,2304]{1,0:T(8,128)(2,1)S(1)}, u32[]{:S(2)}, u32[]{:S(2)}) collective-permute-start(bf16[16,2304]{1,0:T(8,128)(2,1)S(1)} %raise_rows.1), channel_id=1, source_target_pairs={{0,8},{4,12},{8,0},{12,4},{1,9},{5,13},{9,1},{13,5},{2,10},{6,14},... | collective-permute-start | bytes 221192 | tf_op jit(solution)/shard_map/ppermute | solution.py:374

commit v6 on v5

--- a/solution.py
+++ b/solution.py
@@ -255,9 +255,14 @@
     for block in range(sources + 1):
         index_ref[block : block + 1, :] = named[block - 1]
     down = jnp.concatenate([ref[...].reshape(local_count * rank, cols) for ref in down_refs], axis=0)
-    rows = own_wide_ref[...]
-    if sources:
-        rows = jnp.concatenate([wide[...], rows], axis=0)
+    lines = Lines(slots, heads)
+    blocks = []
+    for source in range(sources):
+        for group in range(lines.groups):
+            blocks.append(rows_refs[source][:, group * cols : (group + 1) * cols])
+        if pad > lines.main:
+            blocks.append(wide[source * pad + lines.main : (source + 1) * pad, :])
+    rows = jnp.concatenate(blocks + [own_wide_ref[...]], axis=0)
     every = lax.dot_general(down, rows, (((1,), (1,)), ((), ())), preferred_element_type=jnp.float32)
     named = jnp.concatenate(named, axis=1)
     total = jnp.zeros((rank, named.shape[1]), jnp.float32)

time: 24.2 us -> 24.2 us (level)
  no operation moved by 1% of the time
where the time goes in v6:
time: 24.2 us; the launch traced here: 24 us
  starting transfers between devices  11.6 us (48%)
  waiting for transfers between devices  6.64 us (27%)
  Pallas kernels  4.45 us (18%)
  between operations  1.33 us (5%)
    ppermute x2, starting transfers between devices, shift(): lax.ppermute(block, axis, [(i, (i + offset) % size) for i in range(size)])  5.82 us
    ppermute x5, starting transfers between devices, swap(): return lax.ppermute(block, axis, [(i, i ^ bits) for i in range(size)])  5.74 us
    ppermute x2, waiting for transfers between devices, shift(): lax.ppermute(block, axis, [(i, (i + offset) % size) for i in range(size)])  3.94 us
    ppermute x5, waiting for transfers between devices, swap(): return lax.ppermute(block, axis, [(i, i ^ bits) for i in range(size)])  2.7 us
    pallas_call x1, Pallas kernels, attend(): pl.pallas_call(attend_kernel, out_shape=jax.ShapeDtypeStruct((GROUP, line...  2.24 us
    pallas_call x1, Pallas kernels, adapted_out(): pl.pallas_call(functools.partial(adapted_kernel, slots, heads), out_shape...  0.67 us
    pallas_call x1, Pallas kernels, attention_out(): pl.pallas_call(functools.partial(attention_kernel, slots, heads), out_sha...  0.66 us
  transfers between devices with their start and end apart: 7, of which 3 were waited for; matrix products, arithmetic and copies ran while one was open for 0% of the time, Pallas kernels for 15%

profile of v6, /device:TPU:0, one launch (start us, length us, event | category | flops | bytes accessed | tf_op | source)
XLA Modules:
  0.0 24.0 jit_solution(12079183434232605905)
XLA Ops:
  0.6 0.0 copy-start.1
  0.6 0.0 copy-start
  0.7 3.1 %collective-permute-start = (bf16[4,16,2048]{2,1,0:T(8,128)(2,1)}, bf16[4,16,2048]{2,1,0:T(8,128)(2,1)S(1)}, u32[]{:S(2)}, u32[]{:S(2)}) collective-permute-start(bf16[4,16,2048]{2,1,0:T(8,128)(2,1)} %refs_0_.3), channel_id=1, source_target_pairs={{0,4},{4,0},{8,12},{12,8},{1,5},{5,1},{9,13},{13,9},{2,6},{6,2},{1... | collective-permute-start | bytes 786440 | tf_op jit(solution)/shard_map/ppermute | solution.py:384
  3.7 2.2 %attend.1.rows_ref = bf16[16,2432]{1,0:T(8,128)(2,1)S(1)} custom-call(bf16[18,2048]{1,0:T(8,128)(2,1)} %q_ref.1, bf16[2,18,128,256]{3,2,1,0:T(8,128)(2,1)} %cache_ref.1, s32[18]{0:T(128)} %lengths_ref.1, s32[18]{0:T(128)} %index_ref.1), custom_call_target="tpu_custom_call" | custom-call | flops 75497472 | bytes 2359296 | tf_op jit(solution)/shard_map/attend/pallas_call | solution.py:128
  6.0 2.7 %collective-permute-start.1 = (bf16[16,2432]{1,0:T(8,128)(2,1)S(1)}, bf16[16,2432]{1,0:T(8,128)(2,1)S(1)}, u32[]{:S(2)}, u32[]{:S(2)}) collective-permute-start(bf16[16,2432]{1,0:T(8,128)(2,1)S(1)} %attend.1.rows_ref), channel_id=1, source_target_pairs={{0,8},{4,12},{8,0},{12,4},{1,9},{5,13},{9,1},{13,5},{2,10},{6,14},... | collective-permute-start | bytes 233480 | tf_op jit(solution)/shard_map/ppermute | solution.py:379
  9.3 0.7 %attention_out.1 = (bf16[18,2048]{1,0:T(8,128)(2,1)}, f32[18,128]{1,0:T(8,128)S(1)}) custom-call(s32[1]{0:T(128)S(6)} %copy.9.live_ref, bf16[16,2432]{1,0:T(8,128)(2,1)S(1)} %attend.1.rows_ref), custom_call_target="tpu_custom_call" | custom-call | tf_op jit(solution)/shard_map/attention_out/pallas_call | solution.py:168
  10.0 0.0 copy-done
  10.0 0.4 %collective-permute-start.2 = (bf16[4,16,2048]{2,1,0:T(8,128)(2,1)S(1)}, bf16[4,16,2048]{2,1,0:T(8,128)(2,1)S(1)}, u32[]{:S(2)}, u32[]{:S(2)}) collective-permute-start(bf16[4,16,2048]{2,1,0:T(8,128)(2,1)S(1)} %copy-done), channel_id=1, source_target_pairs={{0,4},{4,0},{8,12},{12,8},{1,5},{5,1},{9,13},{13,9},{2,6},{6,2},{1... | collective-permute-start | bytes 786440 | tf_op jit(solution)/shard_map/ppermute | solution.py:384
  10.4 1.9 %collective-permute-done.1.refs_2_ = bf16[16,2432]{1,0:T(8,128)(2,1)S(1)} collective-permute-done((bf16[16,2432]{1,0:T(8,128)(2,1)S(1)}, bf16[16,2432]{1,0:T(8,128)(2,1)S(1)}, u32[]{:S(2)}, u32[]{:S(2)}) %collective-permute-start.1) | collective-permute-done | bytes 77856 | tf_op jit(solution)/shard_map/ppermute | solution.py:379
  12.3 0.0 collective-permute-done.refs_1_
  12.3 0.0 copy-done.1
  12.3 0.3 %lower.1 = (f32[16,64]{1,0:T(8,128)S(1)}, s32[2,32]{1,0:T(2,128)S(1)}) custom-call(s32[1,32]{1,0:T(1,128)S(1)} %get-tuple-element.11.own_index_ref, bf16[32,2048]{1,0:T(8,128)(2,1)S(1)} %get-tuple-element.12.own_wide_ref, bf16[4,16,2048]{2,1,0:T(8,128)(2,1)S(1)} %copy-done.1, bf16[4,16,2048]{2,1,0:T(8,128)(2,1)S(1)} %collective-permute-done.refs_1_, ...), custom_call_target="tpu_custom_call" | custom-call | flops 20000000000 | tf_op jit(solution)/shard_map/lower/pallas_call | solution.py:280
  12.6 1.6 %collective-permute-start.3 = (f32[16,64]{1,0:T(8,128)S(1)}, f32[16,64]{1,0:T(8,128)S(1)}, u32[]{:S(2)}, u32[]{:S(2)}) collective-permute-start(f32[16,64]{1,0:T(8,128)S(1)} %get-tuple-element.15.refs_2_), channel_id=1, source_target_pairs={{0,2},{1,3},{2,0},{3,1},{4,6},{5,7},{6,4},{7,5},{8,10},{9,11},{10,... | collective-permute-start | bytes 12296 | tf_op jit(solution)/shard_map/ppermute | solution.py:384
  14.2 0.0 collective-permute-start.4
  14.2 0.6 %collective-permute-start.5 = (f32[16,64]{1,0:T(8,128)S(1)}, f32[16,64]{1,0:T(8,128)S(1)}, u32[]{:S(2)}, u32[]{:S(2)}) collective-permute-start(f32[16,64]{1,0:T(8,128)S(1)} %get-tuple-element.15.refs_2_), channel_id=1, source_target_pairs={{0,1},{1,0},{2,3},{3,2},{4,5},{5,4},{6,7},{7,6},{8,9},{9,8},{10,11... | collective-permute-start | bytes 12296 | tf_op jit(solution)/shard_map/ppermute | solution.py:384
  14.9 2.7 %collective-permute-done.2.refs_1_ = bf16[4,16,2048]{2,1,0:T(8,128)(2,1)S(1)} collective-permute-done((bf16[4,16,2048]{2,1,0:T(8,128)(2,1)S(1)}, bf16[4,16,2048]{2,1,0:T(8,128)(2,1)S(1)}, u32[]{:S(2)}, u32[]{:S(2)}) %collective-permute-start.2) | collective-permute-done | bytes 262176 | tf_op jit(solution)/shard_map/ppermute | solution.py:384
  17.5 0.0 collective-permute-done.3.refs_3_
  17.5 0.0 collective-permute-done.4.refs_4_
  17.5 0.0 collective-permute-done.5.refs_5_
  17.6 0.3 %raise_rows.1 = bf16[16,2304]{1,0:T(8,128)(2,1)S(1)} custom-call(s32[2,32]{1,0:T(2,128)S(1)} %get-tuple-element.13.index_ref, bf16[4,16,2048]{2,1,0:T(8,128)(2,1)S(1)} %copy-done, bf16[4,16,2048]{2,1,0:T(8,128)(2,1)S(1)} %collective-permute-done.2.refs_1_, f32[16,64]{1,0:T(8,128)S(1)} %get-tuple-element.15.refs_2_, ...), custom_call_target="tpu_custom_call" | custom-call | tf_op jit(solution)/shard_map/raise_rows/pallas_call | solution.py:343
  17.8 3.2 %collective-permute-start.6 = (bf16[16,2304]{1,0:T(8,128)(2,1)S(1)}, bf16[16,2304]{1,0:T(8,128)(2,1)S(1)}, u32[]{:S(2)}, u32[]{:S(2)}) collective-permute-start(bf16[16,2304]{1,0:T(8,128)(2,1)S(1)} %raise_rows.1), channel_id=1, source_target_pairs={{0,8},{4,12},{8,0},{12,4},{1,9},{5,13},{9,1},{13,5},{2,10},{6,14},... | collective-permute-start | bytes 221192 | tf_op jit(solution)/shard_map/ppermute | solution.py:379
  21.0 0.3 %raise_own.1.own_ref = f32[18,2048]{1,0:T(8,128)S(1)} custom-call(s32[2,32]{1,0:T(2,128)S(1)} %get-tuple-element.13.index_ref, bf16[4,16,2048]{2,1,0:T(8,128)(2,1)S(1)} %copy-done, bf16[4,16,2048]{2,1,0:T(8,128)(2,1)S(1)} %collective-permute-done.2.refs_1_, f32[16,64]{1,0:T(8,128)S(1)} %get-tuple-element.15.refs_2_, ...), custom_call_target="tpu_custom_call" | custom-call | tf_op jit(solution)/shard_map/raise_own/pallas_call | solution.py:367
  21.3 2.0 %collective-permute-done.6.refs_0_ = bf16[16,2304]{1,0:T(8,128)(2,1)S(1)} collective-permute-done((bf16[16,2304]{1,0:T(8,128)(2,1)S(1)}, bf16[16,2304]{1,0:T(8,128)(2,1)S(1)}, u32[]{:S(2)}, u32[]{:S(2)}) %collective-permute-start.6) | collective-permute-done | bytes 73760 | tf_op jit(solution)/shard_map/ppermute | solution.py:379
  23.3 0.7 %adapted_out.1 = bf16[18,2048]{1,0:T(8,128)(2,1)} custom-call(f32[18,128]{1,0:T(8,128)S(1)} %get-tuple-element.10.alive_ref, f32[18,2048]{1,0:T(8,128)S(1)} %raise_own.1.own_ref, bf16[16,2304]{1,0:T(8,128)(2,1)S(1)} %collective-permute-done.6.refs_0_), custom_call_target="tpu_custom_call" | custom-call | tf_op jit(solution)/shard_map/adapted_out/pallas_call | solution.py:196
  (1 shorter events, 0.0 us)
Async XLA Ops:
  0.6 11.7 %copy-start.1 = (bf16[4,16,2048]{2,1,0:T(8,128)(2,1)S(1)}, bf16[4,16,2048]{2,1,0:T(8,128)(2,1)}, u32[]{:S(2)}) copy-start(bf16[4,16,2048]{2,1,0:T(8,128)(2,1)} %refs_0_.3) | copy-start | bytes 786436
  0.6 9.3 %copy-start = (bf16[4,16,2048]{2,1,0:T(8,128)(2,1)S(1)}, bf16[4,16,2048]{2,1,0:T(8,128)(2,1)}, u32[]{:S(2)}) copy-start(bf16[4,16,2048]{2,1,0:T(8,128)(2,1)} %refs_0_.5) | copy-start | bytes 786436
  0.7 11.7 %collective-permute-start = (bf16[4,16,2048]{2,1,0:T(8,128)(2,1)}, bf16[4,16,2048]{2,1,0:T(8,128)(2,1)S(1)}, u32[]{:S(2)}, u32[]{:S(2)}) collective-permute-start(bf16[4,16,2048]{2,1,0:T(8,128)(2,1)} %refs_0_.3), channel_id=1, source_target_pairs={{0,4},{4,0},{8,12},{12,8},{1,5},{5,1},{9,13},{13,9},{2,6},{6,2},{1... | collective-permute-start | bytes 786440 | tf_op jit(solution)/shard_map/ppermute | solution.py:384
  6.0 6.3 %collective-permute-start.1 = (bf16[16,2432]{1,0:T(8,128)(2,1)S(1)}, bf16[16,2432]{1,0:T(8,128)(2,1)S(1)}, u32[]{:S(2)}, u32[]{:S(2)}) collective-permute-start(bf16[16,2432]{1,0:T(8,128)(2,1)S(1)} %attend.1.rows_ref), channel_id=1, source_target_pairs={{0,8},{4,12},{8,0},{12,4},{1,9},{5,13},{9,1},{13,5},{2,10},{6,14},... | collective-permute-start | bytes 233480 | tf_op jit(solution)/shard_map/ppermute | solution.py:379
  10.0 7.6 %collective-permute-start.2 = (bf16[4,16,2048]{2,1,0:T(8,128)(2,1)S(1)}, bf16[4,16,2048]{2,1,0:T(8,128)(2,1)S(1)}, u32[]{:S(2)}, u32[]{:S(2)}) collective-permute-start(bf16[4,16,2048]{2,1,0:T(8,128)(2,1)S(1)} %copy-done), channel_id=1, source_target_pairs={{0,4},{4,0},{8,12},{12,8},{1,5},{5,1},{9,13},{13,9},{2,6},{6,2},{1... | collective-permute-start | bytes 786440 | tf_op jit(solution)/shard_map/ppermute | solution.py:384
  12.6 4.9 %collective-permute-start.3 = (f32[16,64]{1,0:T(8,128)S(1)}, f32[16,64]{1,0:T(8,128)S(1)}, u32[]{:S(2)}, u32[]{:S(2)}) collective-permute-start(f32[16,64]{1,0:T(8,128)S(1)} %get-tuple-element.15.refs_2_), channel_id=1, source_target_pairs={{0,2},{1,3},{2,0},{3,1},{4,6},{5,7},{6,4},{7,5},{8,10},{9,11},{10,... | collective-permute-start | bytes 12296 | tf_op jit(solution)/shard_map/ppermute | solution.py:384
  14.2 3.3 %collective-permute-start.4 = (f32[16,64]{1,0:T(8,128)S(1)}, f32[16,64]{1,0:T(8,128)S(1)}, u32[]{:S(2)}, u32[]{:S(2)}) collective-permute-start(f32[16,64]{1,0:T(8,128)S(1)} %get-tuple-element.15.refs_2_), channel_id=1, source_target_pairs={{0,3},{1,2},{2,1},{3,0},{4,7},{5,6},{6,5},{7,4},{8,11},{9,10},{10,... | collective-permute-start | bytes 12296 | tf_op jit(solution)/shard_map/ppermute | solution.py:384
  14.2 3.3 %collective-permute-start.5 = (f32[16,64]{1,0:T(8,128)S(1)}, f32[16,64]{1,0:T(8,128)S(1)}, u32[]{:S(2)}, u32[]{:S(2)}) collective-permute-start(f32[16,64]{1,0:T(8,128)S(1)} %get-tuple-element.15.refs_2_), channel_id=1, source_target_pairs={{0,1},{1,0},{2,3},{3,2},{4,5},{5,4},{6,7},{7,6},{8,9},{9,8},{10,11... | collective-permute-start | bytes 12296 | tf_op jit(solution)/shard_map/ppermute | solution.py:384
  17.8 5.5 %collective-permute-start.6 = (bf16[16,2304]{1,0:T(8,128)(2,1)S(1)}, bf16[16,2304]{1,0:T(8,128)(2,1)S(1)}, u32[]{:S(2)}, u32[]{:S(2)}) collective-permute-start(bf16[16,2304]{1,0:T(8,128)(2,1)S(1)} %raise_rows.1), channel_id=1, source_target_pairs={{0,8},{4,12},{8,0},{12,4},{1,9},{5,13},{9,1},{13,5},{2,10},{6,14},... | collective-permute-start | bytes 221192 | tf_op jit(solution)/shard_map/ppermute | solution.py:379

commit v7 on v5

--- a/solution.py
+++ b/solution.py
@@ -13,6 +13,7 @@
 SCALING = 2.0
 LANES = 128
 GROUP = 16
+COLUMNS = 512
 DIGIT = 7
 
 VMEM = pl.BlockSpec(memory_space=pltpu.VMEM)
@@ -318,16 +319,20 @@
     for source in range(sources):
         total = packed[:, source * pad : (source + 1) * pad]
         spread = spread_ranks(index_ref[1 + source : 2 + source, :], total, holders, local_count)
-        wide = lax.dot_general(spread, up, (((0,), (0,)), ((), ())), preferred_element_type=jnp.float32)
         out_ref = outs[source]
-        for group in range(lines.groups):
-            block = wide[group * GROUP : (group + 1) * GROUP, :]
-            out_ref[:, group * cols : (group + 1) * cols] = block.astype(jnp.bfloat16)
         if lines.left:
             small[...] = jnp.zeros(small.shape, jnp.float32)
-            for head in range(heads):
-                block = wide[lines.main : slots, head * HEAD_DIM : (head + 1) * HEAD_DIM]
-                small[pl.ds(head, lines.left, stride=heads), :] = block
+        step = min(cols, COLUMNS)
+        for first in range(0, cols, step):
+            block_up = up[:, first : first + step]
+            wide = lax.dot_general(spread, block_up, (((0,), (0,)), ((), ())), preferred_element_type=jnp.float32)
+            for group in range(lines.groups):
+                block = wide[group * GROUP : (group + 1) * GROUP, :]
+                out_ref[:, group * cols + first : group * cols + first + block.shape[1]] = block.astype(jnp.bfloat16)
+            if lines.left:
+                for lane in range(0, wide.shape[1], HEAD_DIM):
+                    block = wide[lines.main : slots, lane : lane + HEAD_DIM]
+                    small[pl.ds((first + lane) // HEAD_DIM, lines.left, stride=heads), :] = block
         for number in range(lines.tiles):
             block = small[number * GROUP : (number + 1) * GROUP, :]
             out_ref[:, lines.tile(number)] = block.astype(jnp.bfloat16)

time: 24.2 us -> 24.2 us (level)
  no operation moved by 1% of the time
where the time goes in v7:
time: 24.2 us; the launch traced here: 24 us
  starting transfers between devices  11.6 us (48%)
  waiting for transfers between devices  6.64 us (27%)
  Pallas kernels  4.45 us (18%)
  between operations  1.33 us (5%)
    ppermute x2, starting transfers between devices, shift(): lax.ppermute(block, axis, [(i, (i + offset) % size) for i in range(size)])  5.82 us
    ppermute x5, starting transfers between devices, swap(): return lax.ppermute(block, axis, [(i, i ^ bits) for i in range(size)])  5.74 us
    ppermute x2, waiting for transfers between devices, shift(): lax.ppermute(block, axis, [(i, (i + offset) % size) for i in range(size)])  3.94 us
    ppermute x5, waiting for transfers between devices, swap(): return lax.ppermute(block, axis, [(i, i ^ bits) for i in range(size)])  2.7 us
    pallas_call x1, Pallas kernels, attend(): pl.pallas_call(attend_kernel, out_shape=jax.ShapeDtypeStruct((GROUP, line...  2.24 us
    pallas_call x1, Pallas kernels, adapted_out(): pl.pallas_call(functools.partial(adapted_kernel, slots, heads), out_shape...  0.67 us
    pallas_call x1, Pallas kernels, attention_out(): pl.pallas_call(functools.partial(attention_kernel, slots, heads), out_sha...  0.66 us
  transfers between devices with their start and end apart: 7, of which 3 were waited for; matrix products, arithmetic and copies ran while one was open for 0% of the time, Pallas kernels for 15%

profile of v7, /device:TPU:0, one launch (start us, length us, event | category | flops | bytes accessed | tf_op | source)
XLA Modules:
  0.0 24.0 jit_solution(6878469079949313803)
XLA Ops:
  0.6 0.0 copy-start.1
  0.6 0.0 copy-start
  0.7 3.1 %collective-permute-start = (bf16[4,16,2048]{2,1,0:T(8,128)(2,1)}, bf16[4,16,2048]{2,1,0:T(8,128)(2,1)S(1)}, u32[]{:S(2)}, u32[]{:S(2)}) collective-permute-start(bf16[4,16,2048]{2,1,0:T(8,128)(2,1)} %refs_0_.3), channel_id=1, source_target_pairs={{0,4},{4,0},{8,12},{12,8},{1,5},{5,1},{9,13},{13,9},{2,6},{6,2},{1... | collective-permute-start | bytes 786440 | tf_op jit(solution)/shard_map/ppermute | solution.py:384
  3.7 2.2 %attend.1.rows_ref = bf16[16,2432]{1,0:T(8,128)(2,1)S(1)} custom-call(bf16[18,2048]{1,0:T(8,128)(2,1)} %q_ref.1, bf16[2,18,128,256]{3,2,1,0:T(8,128)(2,1)} %cache_ref.1, s32[18]{0:T(128)} %lengths_ref.1, s32[18]{0:T(128)} %index_ref.1), custom_call_target="tpu_custom_call" | custom-call | flops 75497472 | bytes 2359296 | tf_op jit(solution)/shard_map/attend/pallas_call | solution.py:129
  6.0 2.7 %collective-permute-start.1 = (bf16[16,2432]{1,0:T(8,128)(2,1)S(1)}, bf16[16,2432]{1,0:T(8,128)(2,1)S(1)}, u32[]{:S(2)}, u32[]{:S(2)}) collective-permute-start(bf16[16,2432]{1,0:T(8,128)(2,1)S(1)} %attend.1.rows_ref), channel_id=1, source_target_pairs={{0,8},{4,12},{8,0},{12,4},{1,9},{5,13},{9,1},{13,5},{2,10},{6,14},... | collective-permute-start | bytes 233480 | tf_op jit(solution)/shard_map/ppermute | solution.py:379
  9.3 0.7 %attention_out.1 = (bf16[18,2048]{1,0:T(8,128)(2,1)}, f32[18,128]{1,0:T(8,128)S(1)}) custom-call(s32[1]{0:T(128)S(6)} %copy.9.live_ref, bf16[16,2432]{1,0:T(8,128)(2,1)S(1)} %attend.1.rows_ref), custom_call_target="tpu_custom_call" | custom-call | tf_op jit(solution)/shard_map/attention_out/pallas_call | solution.py:169
  10.0 0.0 copy-done
  10.0 0.4 %collective-permute-start.2 = (bf16[4,16,2048]{2,1,0:T(8,128)(2,1)S(1)}, bf16[4,16,2048]{2,1,0:T(8,128)(2,1)S(1)}, u32[]{:S(2)}, u32[]{:S(2)}) collective-permute-start(bf16[4,16,2048]{2,1,0:T(8,128)(2,1)S(1)} %copy-done), channel_id=1, source_target_pairs={{0,4},{4,0},{8,12},{12,8},{1,5},{5,1},{9,13},{13,9},{2,6},{6,2},{1... | collective-permute-start | bytes 786440 | tf_op jit(solution)/shard_map/ppermute | solution.py:384
  10.4 1.9 %collective-permute-done.1.refs_2_ = bf16[16,2432]{1,0:T(8,128)(2,1)S(1)} collective-permute-done((bf16[16,2432]{1,0:T(8,128)(2,1)S(1)}, bf16[16,2432]{1,0:T(8,128)(2,1)S(1)}, u32[]{:S(2)}, u32[]{:S(2)}) %collective-permute-start.1) | collective-permute-done | bytes 77856 | tf_op jit(solution)/shard_map/ppermute | solution.py:379
  12.3 0.0 collective-permute-done.refs_1_
  12.3 0.0 copy-done.1
  12.3 0.3 %lower.1 = (f32[16,64]{1,0:T(8,128)S(1)}, s32[2,32]{1,0:T(2,128)S(1)}) custom-call(s32[1,32]{1,0:T(1,128)S(1)} %get-tuple-element.11.own_index_ref, bf16[32,2048]{1,0:T(8,128)(2,1)S(1)} %get-tuple-element.12.own_wide_ref, bf16[4,16,2048]{2,1,0:T(8,128)(2,1)S(1)} %copy-done.1, bf16[4,16,2048]{2,1,0:T(8,128)(2,1)S(1)} %collective-permute-done.refs_1_, ...), custom_call_target="tpu_custom_call" | custom-call | flops 20000000000 | tf_op jit(solution)/shard_map/lower/pallas_call | solution.py:276
  12.6 1.6 %collective-permute-start.3 = (f32[16,64]{1,0:T(8,128)S(1)}, f32[16,64]{1,0:T(8,128)S(1)}, u32[]{:S(2)}, u32[]{:S(2)}) collective-permute-start(f32[16,64]{1,0:T(8,128)S(1)} %get-tuple-element.15.refs_2_), channel_id=1, source_target_pairs={{0,2},{1,3},{2,0},{3,1},{4,6},{5,7},{6,4},{7,5},{8,10},{9,11},{10,... | collective-permute-start | bytes 12296 | tf_op jit(solution)/shard_map/ppermute | solution.py:384
  14.2 0.0 collective-permute-start.4
  14.2 0.6 %collective-permute-start.5 = (f32[16,64]{1,0:T(8,128)S(1)}, f32[16,64]{1,0:T(8,128)S(1)}, u32[]{:S(2)}, u32[]{:S(2)}) collective-permute-start(f32[16,64]{1,0:T(8,128)S(1)} %get-tuple-element.15.refs_2_), channel_id=1, source_target_pairs={{0,1},{1,0},{2,3},{3,2},{4,5},{5,4},{6,7},{7,6},{8,9},{9,8},{10,11... | collective-permute-start | bytes 12296 | tf_op jit(solution)/shard_map/ppermute | solution.py:384
  14.9 2.7 %collective-permute-done.2.refs_1_ = bf16[4,16,2048]{2,1,0:T(8,128)(2,1)S(1)} collective-permute-done((bf16[4,16,2048]{2,1,0:T(8,128)(2,1)S(1)}, bf16[4,16,2048]{2,1,0:T(8,128)(2,1)S(1)}, u32[]{:S(2)}, u32[]{:S(2)}) %collective-permute-start.2) | collective-permute-done | bytes 262176 | tf_op jit(solution)/shard_map/ppermute | solution.py:384
  17.5 0.0 collective-permute-done.3.refs_3_
  17.5 0.0 collective-permute-done.4.refs_4_
  17.5 0.0 collective-permute-done.5.refs_5_
  17.6 0.3 %raise_rows.1 = bf16[16,2304]{1,0:T(8,128)(2,1)S(1)} custom-call(s32[2,32]{1,0:T(2,128)S(1)} %get-tuple-element.13.index_ref, bf16[4,16,2048]{2,1,0:T(8,128)(2,1)S(1)} %copy-done, bf16[4,16,2048]{2,1,0:T(8,128)(2,1)S(1)} %collective-permute-done.2.refs_1_, f32[16,64]{1,0:T(8,128)S(1)} %get-tuple-element.15.refs_2_, ...), custom_call_target="tpu_custom_call" | custom-call | tf_op jit(solution)/shard_map/raise_rows/pallas_call | solution.py:343
  17.8 3.2 %collective-permute-start.6 = (bf16[16,2304]{1,0:T(8,128)(2,1)S(1)}, bf16[16,2304]{1,0:T(8,128)(2,1)S(1)}, u32[]{:S(2)}, u32[]{:S(2)}) collective-permute-start(bf16[16,2304]{1,0:T(8,128)(2,1)S(1)} %raise_rows.1), channel_id=1, source_target_pairs={{0,8},{4,12},{8,0},{12,4},{1,9},{5,13},{9,1},{13,5},{2,10},{6,14},... | collective-permute-start | bytes 221192 | tf_op jit(solution)/shard_map/ppermute | solution.py:379
  21.0 0.3 %raise_own.1.own_ref = f32[18,2048]{1,0:T(8,128)S(1)} custom-call(s32[2,32]{1,0:T(2,128)S(1)} %get-tuple-element.13.index_ref, bf16[4,16,2048]{2,1,0:T(8,128)(2,1)S(1)} %copy-done, bf16[4,16,2048]{2,1,0:T(8,128)(2,1)S(1)} %collective-permute-done.2.refs_1_, f32[16,64]{1,0:T(8,128)S(1)} %get-tuple-element.15.refs_2_, ...), custom_call_target="tpu_custom_call" | custom-call | tf_op jit(solution)/shard_map/raise_own/pallas_call | solution.py:367
  21.3 2.0 %collective-permute-done.6.refs_0_ = bf16[16,2304]{1,0:T(8,128)(2,1)S(1)} collective-permute-done((bf16[16,2304]{1,0:T(8,128)(2,1)S(1)}, bf16[16,2304]{1,0:T(8,128)(2,1)S(1)}, u32[]{:S(2)}, u32[]{:S(2)}) %collective-permute-start.6) | collective-permute-done | bytes 73760 | tf_op jit(solution)/shard_map/ppermute | solution.py:379
  23.3 0.7 %adapted_out.1 = bf16[18,2048]{1,0:T(8,128)(2,1)} custom-call(f32[18,128]{1,0:T(8,128)S(1)} %get-tuple-element.10.alive_ref, f32[18,2048]{1,0:T(8,128)S(1)} %raise_own.1.own_ref, bf16[16,2304]{1,0:T(8,128)(2,1)S(1)} %collective-permute-done.6.refs_0_), custom_call_target="tpu_custom_call" | custom-call | tf_op jit(solution)/shard_map/adapted_out/pallas_call | solution.py:197
  (1 shorter events, 0.0 us)
Async XLA Ops:
  0.6 11.7 %copy-start.1 = (bf16[4,16,2048]{2,1,0:T(8,128)(2,1)S(1)}, bf16[4,16,2048]{2,1,0:T(8,128)(2,1)}, u32[]{:S(2)}) copy-start(bf16[4,16,2048]{2,1,0:T(8,128)(2,1)} %refs_0_.3) | copy-start | bytes 786436
  0.6 9.3 %copy-start = (bf16[4,16,2048]{2,1,0:T(8,128)(2,1)S(1)}, bf16[4,16,2048]{2,1,0:T(8,128)(2,1)}, u32[]{:S(2)}) copy-start(bf16[4,16,2048]{2,1,0:T(8,128)(2,1)} %refs_0_.5) | copy-start | bytes 786436
  0.7 11.7 %collective-permute-start = (bf16[4,16,2048]{2,1,0:T(8,128)(2,1)}, bf16[4,16,2048]{2,1,0:T(8,128)(2,1)S(1)}, u32[]{:S(2)}, u32[]{:S(2)}) collective-permute-start(bf16[4,16,2048]{2,1,0:T(8,128)(2,1)} %refs_0_.3), channel_id=1, source_target_pairs={{0,4},{4,0},{8,12},{12,8},{1,5},{5,1},{9,13},{13,9},{2,6},{6,2},{1... | collective-permute-start | bytes 786440 | tf_op jit(solution)/shard_map/ppermute | solution.py:384
  6.0 6.3 %collective-permute-start.1 = (bf16[16,2432]{1,0:T(8,128)(2,1)S(1)}, bf16[16,2432]{1,0:T(8,128)(2,1)S(1)}, u32[]{:S(2)}, u32[]{:S(2)}) collective-permute-start(bf16[16,2432]{1,0:T(8,128)(2,1)S(1)} %attend.1.rows_ref), channel_id=1, source_target_pairs={{0,8},{4,12},{8,0},{12,4},{1,9},{5,13},{9,1},{13,5},{2,10},{6,14},... | collective-permute-start | bytes 233480 | tf_op jit(solution)/shard_map/ppermute | solution.py:379
  10.0 7.6 %collective-permute-start.2 = (bf16[4,16,2048]{2,1,0:T(8,128)(2,1)S(1)}, bf16[4,16,2048]{2,1,0:T(8,128)(2,1)S(1)}, u32[]{:S(2)}, u32[]{:S(2)}) collective-permute-start(bf16[4,16,2048]{2,1,0:T(8,128)(2,1)S(1)} %copy-done), channel_id=1, source_target_pairs={{0,4},{4,0},{8,12},{12,8},{1,5},{5,1},{9,13},{13,9},{2,6},{6,2},{1... | collective-permute-start | bytes 786440 | tf_op jit(solution)/shard_map/ppermute | solution.py:384
  12.6 4.9 %collective-permute-start.3 = (f32[16,64]{1,0:T(8,128)S(1)}, f32[16,64]{1,0:T(8,128)S(1)}, u32[]{:S(2)}, u32[]{:S(2)}) collective-permute-start(f32[16,64]{1,0:T(8,128)S(1)} %get-tuple-element.15.refs_2_), channel_id=1, source_target_pairs={{0,2},{1,3},{2,0},{3,1},{4,6},{5,7},{6,4},{7,5},{8,10},{9,11},{10,... | collective-permute-start | bytes 12296 | tf_op jit(solution)/shard_map/ppermute | solution.py:384
  14.2 3.3 %collective-permute-start.4 = (f32[16,64]{1,0:T(8,128)S(1)}, f32[16,64]{1,0:T(8,128)S(1)}, u32[]{:S(2)}, u32[]{:S(2)}) collective-permute-start(f32[16,64]{1,0:T(8,128)S(1)} %get-tuple-element.15.refs_2_), channel_id=1, source_target_pairs={{0,3},{1,2},{2,1},{3,0},{4,7},{5,6},{6,5},{7,4},{8,11},{9,10},{10,... | collective-permute-start | bytes 12296 | tf_op jit(solution)/shard_map/ppermute | solution.py:384
  14.2 3.3 %collective-permute-start.5 = (f32[16,64]{1,0:T(8,128)S(1)}, f32[16,64]{1,0:T(8,128)S(1)}, u32[]{:S(2)}, u32[]{:S(2)}) collective-permute-start(f32[16,64]{1,0:T(8,128)S(1)} %get-tuple-element.15.refs_2_), channel_id=1, source_target_pairs={{0,1},{1,0},{2,3},{3,2},{4,5},{5,4},{6,7},{7,6},{8,9},{9,8},{10,11... | collective-permute-start | bytes 12296 | tf_op jit(solution)/shard_map/ppermute | solution.py:384
  17.8 5.5 %collective-permute-start.6 = (bf16[16,2304]{1,0:T(8,128)(2,1)S(1)}, bf16[16,2304]{1,0:T(8,128)(2,1)S(1)}, u32[]{:S(2)}, u32[]{:S(2)}) collective-permute-start(bf16[16,2304]{1,0:T(8,128)(2,1)S(1)} %raise_rows.1), channel_id=1, source_target_pairs={{0,8},{4,12},{8,0},{12,4},{1,9},{5,13},{9,1},{13,5},{2,10},{6,14},... | collective-permute-start | bytes 221192 | tf_op jit(solution)/shard_map/ppermute | solution.py:379

commit v8 on v5

--- a/solution.py
+++ b/solution.py
@@ -301,9 +301,7 @@
 
 
 def stack_ups(up_refs):
-    local_count, rank, cols = up_refs[0].shape
-    up = [up_ref[...].reshape(local_count * rank, cols) for up_ref in up_refs]
-    return jnp.concatenate(up, axis=0)
+    return jnp.concatenate([ref[...].reshape(-1, ref.shape[2]) for ref in up_refs], axis=0)
 
 
 def raise_kernel(slots, heads, sources, holders, index_ref, *refs):
@@ -317,7 +315,7 @@
     pad = index_ref.shape[1]
     for source in range(sources):
         total = packed[:, source * pad : (source + 1) * pad]
-        spread = spread_ranks(index_ref[1 + source : 2 + source, :], total, holders, local_count)
+        spread = spread_ranks(index_ref[1 + source : 2 + source, :], total, min(holders, 2), local_count)
         wide = lax.dot_general(spread, up, (((0,), (0,)), ((), ())), preferred_element_type=jnp.float32)
         out_ref = outs[source]
         for group in range(lines.groups):
@@ -353,7 +351,7 @@
     for other in partials[1:]:
         packed += other[...]
     total = packed[:, packed.shape[1] - index_ref.shape[1] :]
-    spread = spread_ranks(index_ref[0:1, :], total, holders, local_count)
+    spread = spread_ranks(index_ref[0:1, :], total, min(holders, 2), local_count)
     wide = lax.dot_general(spread, stack_ups(up_refs), (((0,), (0,)), ((), ())), preferred_element_type=jnp.float32)
     out_ref[...] = wide[:slots, :]
 
@@ -383,7 +381,7 @@
     size = lax.axis_size(axis)
     if size & (size - 1):
         return [shift(block, axis, k) for k in range(1, size)]
-    return [swap(block, axis, k) for k in [*range(2, size), 1]]
+    return [shift(block, axis, k) for k in [*range(2, size), 1]]
 
 
 def on_device(queries, past_cache, lengths, live_counts, adapter_index, adapter_down, adapter_up):
@@ -401,7 +399,9 @@
     attention, alive = attention_out(live_counts, rows, slots, heads)
     own = own_lines(rows, slots, heads, pad)
     later_up = lax.optimization_barrier((adapter_up, alive))[0]
-    ups = [adapter_up] + [swap(later_up, "replica") for _ in range(1, holders)]
+    half = -(-adapter_up.shape[0] // 2)
+    halves = [later_up[:half], later_up[half:]] if holders > 1 else []
+    ups = [adapter_up] + [swap(part, "replica") for part in halves if part.shape[0]]
     partial, index = lower(own, downs, gathered, slots, heads, pad)
     partials = [partial] + exchange(partial, "tensor")
     widened = raise_rows(index, ups, partials, slots, heads, sources - 1)

time: 24.2 us -> 24.2 us (level)
  waiting for transfers between devices: 6.64 us -> 5.11 us
  starting transfers between devices: 11.6 us -> 13.1 us
    ppermute x2 -> x5, starting transfers between devices: 5.82 us -> 7.89 us  [shift(): lax.ppermute(block, axis, [(i, (i + offset) % size) for i in range(size)])]
    ppermute x2 -> x5, waiting for transfers between devices: 3.94 us -> 2.28 us  [shift(): lax.ppermute(block, axis, [(i, (i + offset) % size) for i in range(size)])]
    ppermute x5 -> x3, starting transfers between devices: 5.74 us -> 5.18 us  [swap(): return lax.ppermute(block, axis, [(i, i ^ bits) for i in range(size)])]
    ppermute x5 -> x3, waiting for transfers between devices: 2.7 us -> 2.83 us  [swap(): return lax.ppermute(block, axis, [(i, i ^ bits) for i in range(size)])]
  transfers between devices with their start and end apart: 7 -> 8, of which waited for: 3 -> 4; matrix products, arithmetic and copies ran while one was open for 0% -> 0% of each run, Pallas kernels for 15% -> 15%
where the time goes in v8:
time: 24.2 us; the launch traced here: 24 us
  starting transfers between devices  13.1 us (54%)
  waiting for transfers between devices  5.11 us (21%)
  Pallas kernels  4.45 us (18%)
  between operations  1.34 us (6%)
    ppermute x5, starting transfers between devices, shift(): lax.ppermute(block, axis, [(i, (i + offset) % size) for i in range(size)])  7.89 us
    ppermute x3, starting transfers between devices, swap(): return lax.ppermute(block, axis, [(i, i ^ bits) for i in range(size)])  5.18 us
    ppermute x3, waiting for transfers between devices, swap(): return lax.ppermute(block, axis, [(i, i ^ bits) for i in range(size)])  2.83 us
    ppermute x5, waiting for transfers between devices, shift(): lax.ppermute(block, axis, [(i, (i + offset) % size) for i in range(size)])  2.28 us
    pallas_call x1, Pallas kernels, attend(): pl.pallas_call(attend_kernel, out_shape=jax.ShapeDtypeStruct((GROUP, line...  2.24 us
    pallas_call x1, Pallas kernels, adapted_out(): pl.pallas_call(functools.partial(adapted_kernel, slots, heads), out_shape...  0.67 us
    pallas_call x1, Pallas kernels, attention_out(): pl.pallas_call(functools.partial(attention_kernel, slots, heads), out_sha...  0.66 us
  transfers between devices with their start and end apart: 8, of which 4 were waited for; matrix products, arithmetic and copies ran while one was open for 0% of the time, Pallas kernels for 15%

profile of v8, /device:TPU:0, one launch (start us, length us, event | category | flops | bytes accessed | tf_op | source)
XLA Modules:
  0.0 24.0 jit_solution(2818892980067856743)
XLA Ops:
  0.6 0.0 copy-start.1
  0.6 0.0 copy-start
  0.7 3.1 %collective-permute-start = (bf16[4,16,2048]{2,1,0:T(8,128)(2,1)}, bf16[4,16,2048]{2,1,0:T(8,128)(2,1)S(1)}, u32[]{:S(2)}, u32[]{:S(2)}) collective-permute-start(bf16[4,16,2048]{2,1,0:T(8,128)(2,1)} %refs_0_.3), channel_id=1, source_target_pairs={{0,4},{4,0},{8,12},{12,8},{1,5},{5,1},{9,13},{13,9},{2,6},{6,2},{1... | collective-permute-start | bytes 786440 | tf_op jit(solution)/shard_map/ppermute | solution.py:377
  3.7 2.2 %attend.1.rows_ref = bf16[16,2432]{1,0:T(8,128)(2,1)S(1)} custom-call(bf16[18,2048]{1,0:T(8,128)(2,1)} %q_ref.1, bf16[2,18,128,256]{3,2,1,0:T(8,128)(2,1)} %cache_ref.1, s32[18]{0:T(128)} %lengths_ref.1, s32[18]{0:T(128)} %index_ref.1), custom_call_target="tpu_custom_call" | custom-call | flops 75497472 | bytes 2359296 | tf_op jit(solution)/shard_map/attend/pallas_call | solution.py:128
  6.0 2.7 %collective-permute-start.1 = (bf16[16,2432]{1,0:T(8,128)(2,1)S(1)}, bf16[16,2432]{1,0:T(8,128)(2,1)S(1)}, u32[]{:S(2)}, u32[]{:S(2)}) collective-permute-start(bf16[16,2432]{1,0:T(8,128)(2,1)S(1)} %attend.1.rows_ref), channel_id=1, source_target_pairs={{0,8},{4,12},{8,0},{12,4},{1,9},{5,13},{9,1},{13,5},{2,10},{6,14},... | collective-permute-start | bytes 233480 | tf_op jit(solution)/shard_map/ppermute | solution.py:372
  9.3 0.7 %attention_out.1 = (bf16[18,2048]{1,0:T(8,128)(2,1)}, f32[18,128]{1,0:T(8,128)S(1)}) custom-call(s32[1]{0:T(128)S(6)} %copy.9.live_ref, bf16[16,2432]{1,0:T(8,128)(2,1)S(1)} %attend.1.rows_ref), custom_call_target="tpu_custom_call" | custom-call | tf_op jit(solution)/shard_map/attention_out/pallas_call | solution.py:168
  10.0 0.0 copy-done
  10.0 0.5 %collective-permute-start.2 = (bf16[2,16,2048]{2,1,0:T(8,128)(2,1)S(1)}, bf16[2,16,2048]{2,1,0:T(8,128)(2,1)S(1)}, u32[]{:S(2)}, u32[]{:S(2)}) collective-permute-start(bf16[2,16,2048]{2,1,0:T(8,128)(2,1)S(1)} %get-tuple-element.17), channel_id=1, source_target_pairs={{0,4},{4,0},{8,12},{12,8},{1,5},{5,1},{9,13},{13,9},{2,6},{6,2},{1... | collective-permute-start | bytes 393224 | tf_op jit(solution)/shard_map/ppermute | solution.py:377
  10.5 1.6 %collective-permute-start.3 = (bf16[2,16,2048]{2,1,0:T(8,128)(2,1)S(1)}, bf16[2,16,2048]{2,1,0:T(8,128)(2,1)S(1)}, u32[]{:S(2)}, u32[]{:S(2)}) collective-permute-start(bf16[2,16,2048]{2,1,0:T(8,128)(2,1)S(1)} %get-tuple-element.16), channel_id=1, source_target_pairs={{0,4},{4,0},{8,12},{12,8},{1,5},{5,1},{9,13},{13,9},{2,6},{6,2},{1... | collective-permute-start | bytes 393224 | tf_op jit(solution)/shard_map/ppermute | solution.py:377
  12.1 0.2 collective-permute-done.1.refs_2_
  12.3 0.0 collective-permute-done.refs_1_
  12.3 0.0 copy-done.1
  12.3 0.3 %lower.1 = (f32[16,64]{1,0:T(8,128)S(1)}, s32[2,32]{1,0:T(2,128)S(1)}) custom-call(s32[1,32]{1,0:T(1,128)S(1)} %get-tuple-element.11.own_index_ref, bf16[32,2048]{1,0:T(8,128)(2,1)S(1)} %get-tuple-element.12.own_wide_ref, bf16[4,16,2048]{2,1,0:T(8,128)(2,1)S(1)} %copy-done.1, bf16[4,16,2048]{2,1,0:T(8,128)(2,1)S(1)} %collective-permute-done.refs_1_, ...), custom_call_target="tpu_custom_call" | custom-call | flops 20000000000 | tf_op jit(solution)/shard_map/lower/pallas_call | solution.py:275
  12.6 1.6 %collective-permute-start.4 = (f32[16,64]{1,0:T(8,128)S(1)}, f32[16,64]{1,0:T(8,128)S(1)}, u32[]{:S(2)}, u32[]{:S(2)}) collective-permute-start(f32[16,64]{1,0:T(8,128)S(1)} %get-tuple-element.15.refs_3_), channel_id=1, source_target_pairs={{0,2},{1,3},{2,0},{3,1},{4,6},{5,7},{6,4},{7,5},{8,10},{9,11},{10,... | collective-permute-start | bytes 12296 | tf_op jit(solution)/shard_map/ppermute | solution.py:372
  14.2 0.0 collective-permute-start.5
  14.2 0.5 %collective-permute-start.6 = (f32[16,64]{1,0:T(8,128)S(1)}, f32[16,64]{1,0:T(8,128)S(1)}, u32[]{:S(2)}, u32[]{:S(2)}) collective-permute-start(f32[16,64]{1,0:T(8,128)S(1)} %get-tuple-element.15.refs_3_), channel_id=1, source_target_pairs={{0,1},{1,2},{2,3},{3,0},{4,5},{5,6},{6,7},{7,4},{8,9},{9,10},{10,1... | collective-permute-start | bytes 12296 | tf_op jit(solution)/shard_map/ppermute | solution.py:372
  14.7 1.4 %collective-permute-done.2.refs_1_ = bf16[2,16,2048]{2,1,0:T(8,128)(2,1)S(1)} collective-permute-done((bf16[2,16,2048]{2,1,0:T(8,128)(2,1)S(1)}, bf16[2,16,2048]{2,1,0:T(8,128)(2,1)S(1)}, u32[]{:S(2)}, u32[]{:S(2)}) %collective-permute-start.2) | collective-permute-done | bytes 131104 | tf_op jit(solution)/shard_map/ppermute | solution.py:377
  16.1 1.4 %collective-permute-done.3.refs_2_ = bf16[2,16,2048]{2,1,0:T(8,128)(2,1)S(1)} collective-permute-done((bf16[2,16,2048]{2,1,0:T(8,128)(2,1)S(1)}, bf16[2,16,2048]{2,1,0:T(8,128)(2,1)S(1)}, u32[]{:S(2)}, u32[]{:S(2)}) %collective-permute-start.3) | collective-permute-done | bytes 131104 | tf_op jit(solution)/shard_map/ppermute | solution.py:377
  17.5 0.0 collective-permute-done.4.refs_4_
  17.5 0.0 collective-permute-done.5.refs_5_
  17.5 0.0 collective-permute-done.6.refs_6_
  17.6 0.3 %raise_rows.1 = bf16[16,2304]{1,0:T(8,128)(2,1)S(1)} custom-call(s32[2,32]{1,0:T(2,128)S(1)} %get-tuple-element.13.index_ref, bf16[4,16,2048]{2,1,0:T(8,128)(2,1)S(1)} %copy-done, bf16[2,16,2048]{2,1,0:T(8,128)(2,1)S(1)} %collective-permute-done.2.refs_1_, bf16[2,16,2048]{2,1,0:T(8,128)(2,1)S(1)} %collective-permute-done.3.refs_2_, ...), custom_call_target="tpu_custom_call" | custom-call | tf_op jit(solution)/shard_map/raise_rows/pallas_call | solution.py:336
  17.8 3.2 %collective-permute-start.7 = (bf16[16,2304]{1,0:T(8,128)(2,1)S(1)}, bf16[16,2304]{1,0:T(8,128)(2,1)S(1)}, u32[]{:S(2)}, u32[]{:S(2)}) collective-permute-start(bf16[16,2304]{1,0:T(8,128)(2,1)S(1)} %raise_rows.1), channel_id=1, source_target_pairs={{0,8},{4,12},{8,0},{12,4},{1,9},{5,13},{9,1},{13,5},{2,10},{6,14},... | collective-permute-start | bytes 221192 | tf_op jit(solution)/shard_map/ppermute | solution.py:372
  21.0 0.3 %raise_own.1.own_ref = f32[18,2048]{1,0:T(8,128)S(1)} custom-call(s32[2,32]{1,0:T(2,128)S(1)} %get-tuple-element.13.index_ref, bf16[4,16,2048]{2,1,0:T(8,128)(2,1)S(1)} %copy-done, bf16[2,16,2048]{2,1,0:T(8,128)(2,1)S(1)} %collective-permute-done.2.refs_1_, bf16[2,16,2048]{2,1,0:T(8,128)(2,1)S(1)} %collective-permute-done.3.refs_2_, ...), custom_call_target="tpu_custom_call" | custom-call | tf_op jit(solution)/shard_map/raise_own/pallas_call | solution.py:360
  21.3 2.0 %collective-permute-done.7.refs_0_ = bf16[16,2304]{1,0:T(8,128)(2,1)S(1)} collective-permute-done((bf16[16,2304]{1,0:T(8,128)(2,1)S(1)}, bf16[16,2304]{1,0:T(8,128)(2,1)S(1)}, u32[]{:S(2)}, u32[]{:S(2)}) %collective-permute-start.7) | collective-permute-done | bytes 73760 | tf_op jit(solution)/shard_map/ppermute | solution.py:372
  23.3 0.7 %adapted_out.1 = bf16[18,2048]{1,0:T(8,128)(2,1)} custom-call(f32[18,128]{1,0:T(8,128)S(1)} %get-tuple-element.10.alive_ref, f32[18,2048]{1,0:T(8,128)S(1)} %raise_own.1.own_ref, bf16[16,2304]{1,0:T(8,128)(2,1)S(1)} %collective-permute-done.7.refs_0_), custom_call_target="tpu_custom_call" | custom-call | tf_op jit(solution)/shard_map/adapted_out/pallas_call | solution.py:196
  (2 shorter events, 0.0 us)
Async XLA Ops:
  0.6 11.7 %copy-start.1 = (bf16[4,16,2048]{2,1,0:T(8,128)(2,1)S(1)}, bf16[4,16,2048]{2,1,0:T(8,128)(2,1)}, u32[]{:S(2)}) copy-start(bf16[4,16,2048]{2,1,0:T(8,128)(2,1)} %refs_0_.3) | copy-start | bytes 786436
  0.6 9.3 %copy-start = (bf16[4,16,2048]{2,1,0:T(8,128)(2,1)S(1)}, bf16[4,16,2048]{2,1,0:T(8,128)(2,1)}, u32[]{:S(2)}) copy-start(bf16[4,16,2048]{2,1,0:T(8,128)(2,1)} %refs_0_.5) | copy-start | bytes 786436
  0.7 11.7 %collective-permute-start = (bf16[4,16,2048]{2,1,0:T(8,128)(2,1)}, bf16[4,16,2048]{2,1,0:T(8,128)(2,1)S(1)}, u32[]{:S(2)}, u32[]{:S(2)}) collective-permute-start(bf16[4,16,2048]{2,1,0:T(8,128)(2,1)} %refs_0_.3), channel_id=1, source_target_pairs={{0,4},{4,0},{8,12},{12,8},{1,5},{5,1},{9,13},{13,9},{2,6},{6,2},{1... | collective-permute-start | bytes 786440 | tf_op jit(solution)/shard_map/ppermute | solution.py:377
  6.0 6.3 %collective-permute-start.1 = (bf16[16,2432]{1,0:T(8,128)(2,1)S(1)}, bf16[16,2432]{1,0:T(8,128)(2,1)S(1)}, u32[]{:S(2)}, u32[]{:S(2)}) collective-permute-start(bf16[16,2432]{1,0:T(8,128)(2,1)S(1)} %attend.1.rows_ref), channel_id=1, source_target_pairs={{0,8},{4,12},{8,0},{12,4},{1,9},{5,13},{9,1},{13,5},{2,10},{6,14},... | collective-permute-start | bytes 233480 | tf_op jit(solution)/shard_map/ppermute | solution.py:372
  10.0 6.2 %collective-permute-start.2 = (bf16[2,16,2048]{2,1,0:T(8,128)(2,1)S(1)}, bf16[2,16,2048]{2,1,0:T(8,128)(2,1)S(1)}, u32[]{:S(2)}, u32[]{:S(2)}) collective-permute-start(bf16[2,16,2048]{2,1,0:T(8,128)(2,1)S(1)} %get-tuple-element.17), channel_id=1, source_target_pairs={{0,4},{4,0},{8,12},{12,8},{1,5},{5,1},{9,13},{13,9},{2,6},{6,2},{1... | collective-permute-start | bytes 393224 | tf_op jit(solution)/shard_map/ppermute | solution.py:377
  10.5 7.0 %collective-permute-start.3 = (bf16[2,16,2048]{2,1,0:T(8,128)(2,1)S(1)}, bf16[2,16,2048]{2,1,0:T(8,128)(2,1)S(1)}, u32[]{:S(2)}, u32[]{:S(2)}) collective-permute-start(bf16[2,16,2048]{2,1,0:T(8,128)(2,1)S(1)} %get-tuple-element.16), channel_id=1, source_target_pairs={{0,4},{4,0},{8,12},{12,8},{1,5},{5,1},{9,13},{13,9},{2,6},{6,2},{1... | collective-permute-start | bytes 393224 | tf_op jit(solution)/shard_map/ppermute | solution.py:377
  12.6 4.9 %collective-permute-start.4 = (f32[16,64]{1,0:T(8,128)S(1)}, f32[16,64]{1,0:T(8,128)S(1)}, u32[]{:S(2)}, u32[]{:S(2)}) collective-permute-start(f32[16,64]{1,0:T(8,128)S(1)} %get-tuple-element.15.refs_3_), channel_id=1, source_target_pairs={{0,2},{1,3},{2,0},{3,1},{4,6},{5,7},{6,4},{7,5},{8,10},{9,11},{10,... | collective-permute-start | bytes 12296 | tf_op jit(solution)/shard_map/ppermute | solution.py:372
  14.2 3.3 %collective-permute-start.5 = (f32[16,64]{1,0:T(8,128)S(1)}, f32[16,64]{1,0:T(8,128)S(1)}, u32[]{:S(2)}, u32[]{:S(2)}) collective-permute-start(f32[16,64]{1,0:T(8,128)S(1)} %get-tuple-element.15.refs_3_), channel_id=1, source_target_pairs={{0,3},{1,0},{2,1},{3,2},{4,7},{5,4},{6,5},{7,6},{8,11},{9,8},{10,9... | collective-permute-start | bytes 12296 | tf_op jit(solution)/shard_map/ppermute | solution.py:372
  14.2 3.3 %collective-permute-start.6 = (f32[16,64]{1,0:T(8,128)S(1)}, f32[16,64]{1,0:T(8,128)S(1)}, u32[]{:S(2)}, u32[]{:S(2)}) collective-permute-start(f32[16,64]{1,0:T(8,128)S(1)} %get-tuple-element.15.refs_3_), channel_id=1, source_target_pairs={{0,1},{1,2},{2,3},{3,0},{4,5},{5,6},{6,7},{7,4},{8,9},{9,10},{10,1... | collective-permute-start | bytes 12296 | tf_op jit(solution)/shard_map/ppermute | solution.py:372
  17.8 5.5 %collective-permute-start.7 = (bf16[16,2304]{1,0:T(8,128)(2,1)S(1)}, bf16[16,2304]{1,0:T(8,128)(2,1)S(1)}, u32[]{:S(2)}, u32[]{:S(2)}) collective-permute-start(bf16[16,2304]{1,0:T(8,128)(2,1)S(1)} %raise_rows.1), channel_id=1, source_target_pairs={{0,8},{4,12},{8,0},{12,4},{1,9},{5,13},{9,1},{13,5},{2,10},{6,14},... | collective-permute-start | bytes 221192 | tf_op jit(solution)/shard_map/ppermute | solution.py:372

commit v9 on v8

--- a/solution.py
+++ b/solution.py
@@ -255,9 +255,14 @@
     for block in range(sources + 1):
         index_ref[block : block + 1, :] = named[block - 1]
     down = jnp.concatenate([ref[...].reshape(local_count * rank, cols) for ref in down_refs], axis=0)
-    rows = own_wide_ref[...]
-    if sources:
-        rows = jnp.concatenate([wide[...], rows], axis=0)
+    lines = Lines(slots, heads)
+    blocks = []
+    for source in range(sources):
+        for group in range(lines.groups):
+            blocks.append(rows_refs[source][:, group * cols : (group + 1) * cols])
+        if pad > lines.main:
+            blocks.append(wide[source * pad + lines.main : (source + 1) * pad, :])
+    rows = jnp.concatenate(blocks + [own_wide_ref[...]], axis=0)
     every = lax.dot_general(down, rows, (((1,), (1,)), ((), ())), preferred_element_type=jnp.float32)
     named = jnp.concatenate(named, axis=1)
     total = jnp.zeros((rank, named.shape[1]), jnp.float32)

time: 24.2 us -> 24.2 us (level)
  no operation moved by 1% of the time
where the time goes in v9:
time: 24.2 us; the launch traced here: 24 us
  starting transfers between devices  13.1 us (54%)
  waiting for transfers between devices  5.11 us (21%)
  Pallas kernels  4.45 us (18%)
  between operations  1.34 us (6%)
    ppermute x5, starting transfers between devices, shift(): lax.ppermute(block, axis, [(i, (i + offset) % size) for i in range(size)])  7.89 us
    ppermute x3, starting transfers between devices, swap(): return lax.ppermute(block, axis, [(i, i ^ bits) for i in range(size)])  5.18 us
    ppermute x3, waiting for transfers between devices, swap(): return lax.ppermute(block, axis, [(i, i ^ bits) for i in range(size)])  2.83 us
    ppermute x5, waiting for transfers between devices, shift(): lax.ppermute(block, axis, [(i, (i + offset) % size) for i in range(size)])  2.28 us
    pallas_call x1, Pallas kernels, attend(): pl.pallas_call(attend_kernel, out_shape=jax.ShapeDtypeStruct((GROUP, line...  2.24 us
    pallas_call x1, Pallas kernels, adapted_out(): pl.pallas_call(functools.partial(adapted_kernel, slots, heads), out_shape...  0.67 us
    pallas_call x1, Pallas kernels, attention_out(): pl.pallas_call(functools.partial(attention_kernel, slots, heads), out_sha...  0.66 us
  transfers between devices with their start and end apart: 8, of which 4 were waited for; matrix products, arithmetic and copies ran while one was open for 0% of the time, Pallas kernels for 15%

profile of v9, /device:TPU:0, one launch (start us, length us, event | category | flops | bytes accessed | tf_op | source)
XLA Modules:
  0.0 24.0 jit_solution(234243589744266191)
XLA Ops:
  0.6 0.0 copy-start.1
  0.6 0.0 copy-start
  0.7 3.1 %collective-permute-start = (bf16[4,16,2048]{2,1,0:T(8,128)(2,1)}, bf16[4,16,2048]{2,1,0:T(8,128)(2,1)S(1)}, u32[]{:S(2)}, u32[]{:S(2)}) collective-permute-start(bf16[4,16,2048]{2,1,0:T(8,128)(2,1)} %refs_0_.3), channel_id=1, source_target_pairs={{0,4},{4,0},{8,12},{12,8},{1,5},{5,1},{9,13},{13,9},{2,6},{6,2},{1... | collective-permute-start | bytes 786440 | tf_op jit(solution)/shard_map/ppermute | solution.py:382
  3.7 2.2 %attend.1.rows_ref = bf16[16,2432]{1,0:T(8,128)(2,1)S(1)} custom-call(bf16[18,2048]{1,0:T(8,128)(2,1)} %q_ref.1, bf16[2,18,128,256]{3,2,1,0:T(8,128)(2,1)} %cache_ref.1, s32[18]{0:T(128)} %lengths_ref.1, s32[18]{0:T(128)} %index_ref.1), custom_call_target="tpu_custom_call" | custom-call | flops 75497472 | bytes 2359296 | tf_op jit(solution)/shard_map/attend/pallas_call | solution.py:128
  6.0 2.7 %collective-permute-start.1 = (bf16[16,2432]{1,0:T(8,128)(2,1)S(1)}, bf16[16,2432]{1,0:T(8,128)(2,1)S(1)}, u32[]{:S(2)}, u32[]{:S(2)}) collective-permute-start(bf16[16,2432]{1,0:T(8,128)(2,1)S(1)} %attend.1.rows_ref), channel_id=1, source_target_pairs={{0,8},{4,12},{8,0},{12,4},{1,9},{5,13},{9,1},{13,5},{2,10},{6,14},... | collective-permute-start | bytes 233480 | tf_op jit(solution)/shard_map/ppermute | solution.py:377
  9.3 0.7 %attention_out.1 = (bf16[18,2048]{1,0:T(8,128)(2,1)}, f32[18,128]{1,0:T(8,128)S(1)}) custom-call(s32[1]{0:T(128)S(6)} %copy.9.live_ref, bf16[16,2432]{1,0:T(8,128)(2,1)S(1)} %attend.1.rows_ref), custom_call_target="tpu_custom_call" | custom-call | tf_op jit(solution)/shard_map/attention_out/pallas_call | solution.py:168
  10.0 0.0 copy-done
  10.0 0.5 %collective-permute-start.2 = (bf16[2,16,2048]{2,1,0:T(8,128)(2,1)S(1)}, bf16[2,16,2048]{2,1,0:T(8,128)(2,1)S(1)}, u32[]{:S(2)}, u32[]{:S(2)}) collective-permute-start(bf16[2,16,2048]{2,1,0:T(8,128)(2,1)S(1)} %get-tuple-element.17), channel_id=1, source_target_pairs={{0,4},{4,0},{8,12},{12,8},{1,5},{5,1},{9,13},{13,9},{2,6},{6,2},{1... | collective-permute-start | bytes 393224 | tf_op jit(solution)/shard_map/ppermute | solution.py:382
  10.5 1.6 %collective-permute-start.3 = (bf16[2,16,2048]{2,1,0:T(8,128)(2,1)S(1)}, bf16[2,16,2048]{2,1,0:T(8,128)(2,1)S(1)}, u32[]{:S(2)}, u32[]{:S(2)}) collective-permute-start(bf16[2,16,2048]{2,1,0:T(8,128)(2,1)S(1)} %get-tuple-element.16), channel_id=1, source_target_pairs={{0,4},{4,0},{8,12},{12,8},{1,5},{5,1},{9,13},{13,9},{2,6},{6,2},{1... | collective-permute-start | bytes 393224 | tf_op jit(solution)/shard_map/ppermute | solution.py:382
  12.1 0.2 collective-permute-done.1.refs_2_
  12.3 0.0 collective-permute-done.refs_1_
  12.3 0.0 copy-done.1
  12.3 0.3 %lower.1 = (f32[16,64]{1,0:T(8,128)S(1)}, s32[2,32]{1,0:T(2,128)S(1)}) custom-call(s32[1,32]{1,0:T(1,128)S(1)} %get-tuple-element.11.own_index_ref, bf16[32,2048]{1,0:T(8,128)(2,1)S(1)} %get-tuple-element.12.own_wide_ref, bf16[4,16,2048]{2,1,0:T(8,128)(2,1)S(1)} %copy-done.1, bf16[4,16,2048]{2,1,0:T(8,128)(2,1)S(1)} %collective-permute-done.refs_1_, ...), custom_call_target="tpu_custom_call" | custom-call | flops 20000000000 | tf_op jit(solution)/shard_map/lower/pallas_call | solution.py:280
  12.6 1.6 %collective-permute-start.4 = (f32[16,64]{1,0:T(8,128)S(1)}, f32[16,64]{1,0:T(8,128)S(1)}, u32[]{:S(2)}, u32[]{:S(2)}) collective-permute-start(f32[16,64]{1,0:T(8,128)S(1)} %get-tuple-element.15.refs_3_), channel_id=1, source_target_pairs={{0,2},{1,3},{2,0},{3,1},{4,6},{5,7},{6,4},{7,5},{8,10},{9,11},{10,... | collective-permute-start | bytes 12296 | tf_op jit(solution)/shard_map/ppermute | solution.py:377
  14.2 0.0 collective-permute-start.5
  14.2 0.5 %collective-permute-start.6 = (f32[16,64]{1,0:T(8,128)S(1)}, f32[16,64]{1,0:T(8,128)S(1)}, u32[]{:S(2)}, u32[]{:S(2)}) collective-permute-start(f32[16,64]{1,0:T(8,128)S(1)} %get-tuple-element.15.refs_3_), channel_id=1, source_target_pairs={{0,1},{1,2},{2,3},{3,0},{4,5},{5,6},{6,7},{7,4},{8,9},{9,10},{10,1... | collective-permute-start | bytes 12296 | tf_op jit(solution)/shard_map/ppermute | solution.py:377
  14.7 1.4 %collective-permute-done.2.refs_1_ = bf16[2,16,2048]{2,1,0:T(8,128)(2,1)S(1)} collective-permute-done((bf16[2,16,2048]{2,1,0:T(8,128)(2,1)S(1)}, bf16[2,16,2048]{2,1,0:T(8,128)(2,1)S(1)}, u32[]{:S(2)}, u32[]{:S(2)}) %collective-permute-start.2) | collective-permute-done | bytes 131104 | tf_op jit(solution)/shard_map/ppermute | solution.py:382
  16.1 1.4 %collective-permute-done.3.refs_2_ = bf16[2,16,2048]{2,1,0:T(8,128)(2,1)S(1)} collective-permute-done((bf16[2,16,2048]{2,1,0:T(8,128)(2,1)S(1)}, bf16[2,16,2048]{2,1,0:T(8,128)(2,1)S(1)}, u32[]{:S(2)}, u32[]{:S(2)}) %collective-permute-start.3) | collective-permute-done | bytes 131104 | tf_op jit(solution)/shard_map/ppermute | solution.py:382
  17.5 0.0 collective-permute-done.4.refs_4_
  17.5 0.0 collective-permute-done.5.refs_5_
  17.5 0.0 collective-permute-done.6.refs_6_
  17.6 0.3 %raise_rows.1 = bf16[16,2304]{1,0:T(8,128)(2,1)S(1)} custom-call(s32[2,32]{1,0:T(2,128)S(1)} %get-tuple-element.13.index_ref, bf16[4,16,2048]{2,1,0:T(8,128)(2,1)S(1)} %copy-done, bf16[2,16,2048]{2,1,0:T(8,128)(2,1)S(1)} %collective-permute-done.2.refs_1_, bf16[2,16,2048]{2,1,0:T(8,128)(2,1)S(1)} %collective-permute-done.3.refs_2_, ...), custom_call_target="tpu_custom_call" | custom-call | tf_op jit(solution)/shard_map/raise_rows/pallas_call | solution.py:341
  17.8 3.2 %collective-permute-start.7 = (bf16[16,2304]{1,0:T(8,128)(2,1)S(1)}, bf16[16,2304]{1,0:T(8,128)(2,1)S(1)}, u32[]{:S(2)}, u32[]{:S(2)}) collective-permute-start(bf16[16,2304]{1,0:T(8,128)(2,1)S(1)} %raise_rows.1), channel_id=1, source_target_pairs={{0,8},{4,12},{8,0},{12,4},{1,9},{5,13},{9,1},{13,5},{2,10},{6,14},... | collective-permute-start | bytes 221192 | tf_op jit(solution)/shard_map/ppermute | solution.py:377
  21.0 0.3 %raise_own.1.own_ref = f32[18,2048]{1,0:T(8,128)S(1)} custom-call(s32[2,32]{1,0:T(2,128)S(1)} %get-tuple-element.13.index_ref, bf16[4,16,2048]{2,1,0:T(8,128)(2,1)S(1)} %copy-done, bf16[2,16,2048]{2,1,0:T(8,128)(2,1)S(1)} %collective-permute-done.2.refs_1_, bf16[2,16,2048]{2,1,0:T(8,128)(2,1)S(1)} %collective-permute-done.3.refs_2_, ...), custom_call_target="tpu_custom_call" | custom-call | tf_op jit(solution)/shard_map/raise_own/pallas_call | solution.py:365
  21.3 2.0 %collective-permute-done.7.refs_0_ = bf16[16,2304]{1,0:T(8,128)(2,1)S(1)} collective-permute-done((bf16[16,2304]{1,0:T(8,128)(2,1)S(1)}, bf16[16,2304]{1,0:T(8,128)(2,1)S(1)}, u32[]{:S(2)}, u32[]{:S(2)}) %collective-permute-start.7) | collective-permute-done | bytes 73760 | tf_op jit(solution)/shard_map/ppermute | solution.py:377
  23.3 0.7 %adapted_out.1 = bf16[18,2048]{1,0:T(8,128)(2,1)} custom-call(f32[18,128]{1,0:T(8,128)S(1)} %get-tuple-element.10.alive_ref, f32[18,2048]{1,0:T(8,128)S(1)} %raise_own.1.own_ref, bf16[16,2304]{1,0:T(8,128)(2,1)S(1)} %collective-permute-done.7.refs_0_), custom_call_target="tpu_custom_call" | custom-call | tf_op jit(solution)/shard_map/adapted_out/pallas_call | solution.py:196
  (2 shorter events, 0.0 us)
Async XLA Ops:
  0.6 11.7 %copy-start.1 = (bf16[4,16,2048]{2,1,0:T(8,128)(2,1)S(1)}, bf16[4,16,2048]{2,1,0:T(8,128)(2,1)}, u32[]{:S(2)}) copy-start(bf16[4,16,2048]{2,1,0:T(8,128)(2,1)} %refs_0_.3) | copy-start | bytes 786436
  0.6 9.3 %copy-start = (bf16[4,16,2048]{2,1,0:T(8,128)(2,1)S(1)}, bf16[4,16,2048]{2,1,0:T(8,128)(2,1)}, u32[]{:S(2)}) copy-start(bf16[4,16,2048]{2,1,0:T(8,128)(2,1)} %refs_0_.5) | copy-start | bytes 786436
  0.7 11.7 %collective-permute-start = (bf16[4,16,2048]{2,1,0:T(8,128)(2,1)}, bf16[4,16,2048]{2,1,0:T(8,128)(2,1)S(1)}, u32[]{:S(2)}, u32[]{:S(2)}) collective-permute-start(bf16[4,16,2048]{2,1,0:T(8,128)(2,1)} %refs_0_.3), channel_id=1, source_target_pairs={{0,4},{4,0},{8,12},{12,8},{1,5},{5,1},{9,13},{13,9},{2,6},{6,2},{1... | collective-permute-start | bytes 786440 | tf_op jit(solution)/shard_map/ppermute | solution.py:382
  6.0 6.3 %collective-permute-start.1 = (bf16[16,2432]{1,0:T(8,128)(2,1)S(1)}, bf16[16,2432]{1,0:T(8,128)(2,1)S(1)}, u32[]{:S(2)}, u32[]{:S(2)}) collective-permute-start(bf16[16,2432]{1,0:T(8,128)(2,1)S(1)} %attend.1.rows_ref), channel_id=1, source_target_pairs={{0,8},{4,12},{8,0},{12,4},{1,9},{5,13},{9,1},{13,5},{2,10},{6,14},... | collective-permute-start | bytes 233480 | tf_op jit(solution)/shard_map/ppermute | solution.py:377
  10.0 6.2 %collective-permute-start.2 = (bf16[2,16,2048]{2,1,0:T(8,128)(2,1)S(1)}, bf16[2,16,2048]{2,1,0:T(8,128)(2,1)S(1)}, u32[]{:S(2)}, u32[]{:S(2)}) collective-permute-start(bf16[2,16,2048]{2,1,0:T(8,128)(2,1)S(1)} %get-tuple-element.17), channel_id=1, source_target_pairs={{0,4},{4,0},{8,12},{12,8},{1,5},{5,1},{9,13},{13,9},{2,6},{6,2},{1... | collective-permute-start | bytes 393224 | tf_op jit(solution)/shard_map/ppermute | solution.py:382
  10.5 7.0 %collective-permute-start.3 = (bf16[2,16,2048]{2,1,0:T(8,128)(2,1)S(1)}, bf16[2,16,2048]{2,1,0:T(8,128)(2,1)S(1)}, u32[]{:S(2)}, u32[]{:S(2)}) collective-permute-start(bf16[2,16,2048]{2,1,0:T(8,128)(2,1)S(1)} %get-tuple-element.16), channel_id=1, source_target_pairs={{0,4},{4,0},{8,12},{12,8},{1,5},{5,1},{9,13},{13,9},{2,6},{6,2},{1... | collective-permute-start | bytes 393224 | tf_op jit(solution)/shard_map/ppermute | solution.py:382
  12.6 4.9 %collective-permute-start.4 = (f32[16,64]{1,0:T(8,128)S(1)}, f32[16,64]{1,0:T(8,128)S(1)}, u32[]{:S(2)}, u32[]{:S(2)}) collective-permute-start(f32[16,64]{1,0:T(8,128)S(1)} %get-tuple-element.15.refs_3_), channel_id=1, source_target_pairs={{0,2},{1,3},{2,0},{3,1},{4,6},{5,7},{6,4},{7,5},{8,10},{9,11},{10,... | collective-permute-start | bytes 12296 | tf_op jit(solution)/shard_map/ppermute | solution.py:377
  14.2 3.3 %collective-permute-start.5 = (f32[16,64]{1,0:T(8,128)S(1)}, f32[16,64]{1,0:T(8,128)S(1)}, u32[]{:S(2)}, u32[]{:S(2)}) collective-permute-start(f32[16,64]{1,0:T(8,128)S(1)} %get-tuple-element.15.refs_3_), channel_id=1, source_target_pairs={{0,3},{1,0},{2,1},{3,2},{4,7},{5,4},{6,5},{7,6},{8,11},{9,8},{10,9... | collective-permute-start | bytes 12296 | tf_op jit(solution)/shard_map/ppermute | solution.py:377
  14.2 3.3 %collective-permute-start.6 = (f32[16,64]{1,0:T(8,128)S(1)}, f32[16,64]{1,0:T(8,128)S(1)}, u32[]{:S(2)}, u32[]{:S(2)}) collective-permute-start(f32[16,64]{1,0:T(8,128)S(1)} %get-tuple-element.15.refs_3_), channel_id=1, source_target_pairs={{0,1},{1,2},{2,3},{3,0},{4,5},{5,6},{6,7},{7,4},{8,9},{9,10},{10,1... | collective-permute-start | bytes 12296 | tf_op jit(solution)/shard_map/ppermute | solution.py:377
  17.8 5.5 %collective-permute-start.7 = (bf16[16,2304]{1,0:T(8,128)(2,1)S(1)}, bf16[16,2304]{1,0:T(8,128)(2,1)S(1)}, u32[]{:S(2)}, u32[]{:S(2)}) collective-permute-start(bf16[16,2304]{1,0:T(8,128)(2,1)S(1)} %raise_rows.1), channel_id=1, source_target_pairs={{0,8},{4,12},{8,0},{12,4},{1,9},{5,13},{9,1},{13,5},{2,10},{6,14},... | collective-permute-start | bytes 221192 | tf_op jit(solution)/shard_map/ppermute | solution.py:377
